TPU v7x, 256 devices: a whole 4x4x8 slice. The times are simulated.
256 devices in a mesh: rep: 8 (over y, core), shard: 32 (over x, z).
Axes of the slice: x: 4, y: 4, z: 8, core: 2. Of those that a mesh axis runs over, the one named last changes fastest.
Arguments:
- tokens: bfloat16 [114688, 12288], P(('rep', 'shard')), may hold values from -60 to 60
- cotangent: bfloat16 [114688, 256], P(('rep', 'shard')), may hold values from -40 to 40
- master: float32 [12288, 256], P('shard'), may hold values from -4 to 4
- first_moment: float32 [12288, 256], P('shard'), may hold values from -3 to 3
- second_moment: float32 [12288, 256], P('shard'), may hold values from 0.05 to 2
Outputs:
- master_new: float32 [12288, 256], P('shard')
- first_new: float32 [12288, 256], P('shard')
- second_new: float32 [12288, 256], P('shard')
- activations: bfloat16 [114688, 256], P(('rep', 'shard'))
All inputs are finite; a program needn't handle non-finite values.
Results may differ from a plain program's by a relative error of at most 0.015.
Values may be sent and summed in bfloat16 or wider, within the bound.
No kernel may reach another device: no remote copies, remote signals or barrier semaphores. Data moves between devices by JAX's collectives and lax.ppermute only.
A program may use at most 64 MiB of HBM per device.

v0:
```python
import jax
import jax.numpy as jnp
from jax import lax
from jax.sharding import PartitionSpec as P

D = 12288
COLS = 256
STEP = 10


beta_first = 0.9
beta_second = 0.95
learn_rate = 0.02
decay_rate = 0.1
epsilon = 1e-08


def apply_update(grads, master, first, second, total):
    rms_value = jnp.sqrt(total / (D * COLS))
    factor = 1.0 / jnp.maximum(rms_value, 1.0)
    clipped = grads * factor
    first_new = beta_first * first + (1.0 - beta_first) * clipped
    second_new = beta_second * second + (1.0 - beta_second) * clipped * clipped
    first_hat = first_new / (1.0 - beta_first**STEP)
    second_hat = second_new / (1.0 - beta_second**STEP)
    master_new = master - learn_rate * (
        first_hat / (jnp.sqrt(second_hat) + epsilon) + decay_rate * master
    )
    return (master_new, first_new, second_new)


def row_terms(source, cotangent):
    return lax.dot_general(
        source, cotangent, (((0,), (0,)), ((), ())), preferred_element_type=jnp.float32
    )


def body(tokens, cotangent, master, first_moment, second_moment):
    width = tokens.shape[1]
    grads = lax.psum_scatter(
        row_terms(tokens, cotangent).astype(jnp.bfloat16), "shard", scatter_dimension=0, tiled=True
    ).astype(jnp.float32)
    grads = lax.psum(grads.astype(jnp.bfloat16), "rep").astype(jnp.float32)
    total = lax.psum(jnp.sum(grads * grads), "shard")
    master_new, first_new, second_new = apply_update(
        grads, master, first_moment, second_moment, total
    )
    weight = master_new.astype(jnp.bfloat16)
    outputs = jnp.dot(
        tokens,
        lax.all_gather(weight, "shard", axis=0, tiled=True),
        preferred_element_type=jnp.float32,
    )
    activations = (outputs * width ** (-0.5)).astype(jnp.bfloat16)
    return (master_new, first_new, second_new, activations)


def solution(mesh):
    in_specs = (
        P(("rep", "shard"), None),
        P(("rep", "shard"), None),
        P("shard", None),
        P("shard", None),
        P("shard", None),
    )
    out_specs = (P("shard", None), P("shard", None), P("shard", None), P(("rep", "shard"), None))
    return jax.shard_map(body, mesh=mesh, in_specs=in_specs, out_specs=out_specs, check_vma=False)
```

profile of v0, /device:TPU:1, one launch (start us, length us, event | category | flops | bytes accessed | tf_op | source)
XLA Modules:
  0.0 488.7 jit_solution(8905422166836374512)
XLA Ops:
  7.2 0.0 copy-start
  7.2 0.0 copy-start.3
  7.2 0.0 copy-start.2
  7.2 0.0 copy-start.1
  7.2 0.0 reduce-scatter.2.cloned.1.call-start
  7.3 0.9 copy-done
  8.1 10.3 %convolution_convert_fusion = bf16[12288,256]{1,0:T(8,128)(2,1)} fusion(bf16[448,12288]{1,0:T(8,128)(2,1)} %param.5, bf16[448,256]{1,0:T(8,128)(2,1)S(1)} %copy-done), kind=kOutput, calls=%fused_computation | convolution fusion | flops 2821718016 | bytes 17530880 | tf_op jit(solution)/shard_map/dot_general | solution.py:33
  18.4 0.0 reduce-scatter.2.cloned.1.call-update
  18.5 0.0 all-reduce.2.cloned.1.call-start
  18.5 225.1 %reduce-scatter.2.cloned.1.call-done = bf16[384,256]{1,0:T(8,128)(2,1)} async-done(((bf16[12288,256]{1,0:T(8,128)(2,1)}), bf16[384,256]{1,0:T(8,128)(2,1)}) %reduce-scatter.2.cloned.1.call-update) | async-done | bytes 196624 | tf_op jit(solution)/shard_map/reduce_scatter | solution.py:40
  243.6 0.0 all-reduce.2.cloned.1.call-update
  243.6 0.0 all-gather.2.cloned.1.call-start
  243.7 66.9 %all-reduce.2.cloned.1.call-done = bf16[384,256]{1,0:T(8,128)(2,1)} async-done(((bf16[384,256]{1,0:T(8,128)(2,1)}), bf16[384,256]{1,0:T(8,128)(2,1)}) %all-reduce.2.cloned.1.call-update) | async-done | bytes 196624 | tf_op jit(solution)/shard_map/psum | solution.py:43
  310.5 1.6 fusion.4
  312.1 61.7 %psum.15 = f32[]{:T(128)} all-reduce(f32[]{:T(128)} %fusion.4), channel_id=1, replica_groups=mesh['rep'=8,'shard'=32] {'shard'}, use_global_device_ids=true, to_apply=%region_3.0 | all-reduce | flops 1 | bytes 8 | tf_op jit(solution)/shard_map/psum | solution.py:44
  374.6 0.0 copy-done.3
  374.6 0.0 copy-done.2
  374.6 0.0 copy-done.1
  374.6 2.2 fusion.6
  376.8 0.0 all-gather.2.cloned.1.call-update
  376.8 95.7 %all-gather.2.cloned.1.call-done = bf16[12288,256]{1,0:T(8,128)(2,1)} async-done(((bf16[384,256]{1,0:T(8,128)(2,1)}), bf16[12288,256]{1,0:T(8,128)(2,1)}) %all-gather.2.cloned.1.call-update) | async-done | bytes 6291472 | tf_op jit(solution)/shard_map/all_gather | solution.py:51
  472.5 9.7 %fusion.1 = bf16[448,256]{1,0:T(8,128)(2,1)} fusion(bf16[448,12288]{1,0:T(8,128)(2,1)} %param.5, bf16[12288,256]{1,0:T(8,128)(2,1)} %all-gather.2.cloned.1.call-done), kind=kOutput, calls=%fused_computation.3 | convolution fusion | flops 2818801664 | bytes 17530880 | tf_op jit(solution)/shard_map/dot_general | solution.py:49
Async XLA Ops:
  7.2 0.9 copy-start
  7.2 367.4 %copy-start.3 = (f32[384,256]{1,0:T(8,128)S(1)}, f32[384,256]{1,0:T(8,128)}, u32[]{:S(2)}) copy-start(f32[384,256]{1,0:T(8,128)} %param.9) | copy-start | bytes 1179652
  7.2 367.4 %copy-start.2 = (f32[384,256]{1,0:T(8,128)S(1)}, f32[384,256]{1,0:T(8,128)}, u32[]{:S(2)}) copy-start(f32[384,256]{1,0:T(8,128)} %param.8) | copy-start | bytes 1179652
  7.2 367.4 %copy-start.1 = (f32[384,256]{1,0:T(8,128)S(1)}, f32[384,256]{1,0:T(8,128)}, u32[]{:S(2)}) copy-start(f32[384,256]{1,0:T(8,128)} %param.7) | copy-start | bytes 1179652
  7.2 236.4 %reduce-scatter.2.cloned.1.call-start = ((), (), s32[]{:S(2)}) async-start(), calls=%async_computation.1 | async-start | bytes 6488064 | tf_op jit(solution)/shard_map/reduce_scatter | solution.py:40
  18.5 292.0 %all-reduce.2.cloned.1.call-start = ((), (), s32[]{:S(2)}) async-start(), calls=%async_computation.2 | async-start | bytes 393216 | tf_op jit(solution)/shard_map/psum | solution.py:43
  243.6 228.9 %all-gather.2.cloned.1.call-start = ((), (), s32[]{:S(2)}) async-start(), calls=%async_computation.3 | async-start | bytes 6488064 | tf_op jit(solution)/shard_map/all_gather | solution.py:51
Sparse Core Ops, SparseCore 0:
  18.6 224.9 reduce-scatter.1
  246.0 64.4 all-reduce.1
  377.0 95.5 all-gather.1
where the time goes:
time: 489 us
  waiting for transfers between devices  388 us (79%)
  blocking collectives  61.7 us (13%)
  matrix products  20 us (4%)
  between operations  14.5 us (3%)
    reduce_scatter x1, waiting for transfers between devices, body(): lax.psum_scatter(row_terms(tokens, cotangent).astype(jnp.bfloat16), 'shar...  225 us
    all_gather x1, waiting for transfers between devices, body(): lax.all_gather(weight, 'shard', axis=0, tiled=True)  95.7 us
    psum x1, waiting for transfers between devices, body(): grads = lax.psum(grads.astype(jnp.bfloat16), 'rep').astype(jnp.float32)  66.9 us
    psum x1, blocking collectives, body(): total = lax.psum(jnp.sum(grads * grads), 'shard')  61.7 us
    dot_general x1, matrix products, row_terms(): lax.dot_general(source, cotangent, (((0,), (0,)), ((), ())), preferred_el...  10.3 us
  transfers between devices with their start and end apart: 3, of which 3 were waited for; matrix products, arithmetic and copies ran while one was open for 0% of the time, Pallas kernels for 0%

commit v1 on v0

v1 whole, which is shorter than its diff:
```python
import functools

import jax
import jax.numpy as jnp
from jax import lax
from jax.experimental import pallas as pl
from jax.experimental.pallas import tpu as pltpu
from jax.sharding import Mesh, PartitionSpec as P

STEP = 10

beta_first = 0.9
beta_second = 0.95
learn_rate = 0.02
decay_rate = 0.1
epsilon = 1e-08

NY, NC, NX, NZ = 4, 2, 4, 8
SIZE = {"y": NY, "core": NC, "x": NX, "z": NZ}
NAMES = ("y", "core", "x", "z")
f32 = jnp.float32
bf16 = jnp.bfloat16


def apply_update(grads, master, first, second, total, count):
    rms_value = jnp.sqrt(total / count)
    factor = 1.0 / jnp.maximum(rms_value, 1.0)
    clipped = grads * factor
    first_new = beta_first * first + (1.0 - beta_first) * clipped
    second_new = beta_second * second + (1.0 - beta_second) * clipped * clipped
    first_hat = first_new / (1.0 - beta_first**STEP)
    second_hat = second_new / (1.0 - beta_second**STEP)
    master_new = master - learn_rate * (
        first_hat / (jnp.sqrt(second_hat) + epsilon) + decay_rate * master
    )
    return (master_new, first_new, second_new)


def send(value, axis, step):
    n = SIZE[axis]
    return lax.ppermute(value, axis, [(i, (i + step) % n) for i in range(n)])


FAR_FIRST = (2, 1, 3)


def block_of(width):
    for size in (1024, 512, 384, 256, 128):
        if width % size == 0:
            return size
    return width


def partial_kernel(chunk_ref, cot_ref, tokens_ref, own_ref, other_ref):
    terms = jnp.dot(cot_ref[...], tokens_ref[...], preferred_element_type=f32).astype(bf16)
    half = terms.shape[0] // 2
    own_ref[...] = terms[:half]
    other_ref[...] = terms[half:]


def partial_terms(chunk, cot_rows, tokens):
    count, width = tokens.shape
    cols, chunk_width = cot_rows.shape[0], width // NX
    block = block_of(chunk_width)
    steps = chunk_width // block
    half = jax.ShapeDtypeStruct((cols // 2, chunk_width), bf16)
    out_spec = pl.BlockSpec((cols // 2, block), lambda i, c: (0, i))
    return pl.pallas_call(
        partial_kernel,
        grid_spec=pltpu.PrefetchScalarGridSpec(
            num_scalar_prefetch=1,
            grid=(steps,),
            in_specs=[
                pl.BlockSpec((cols, count), lambda i, c: (0, 0)),
                pl.BlockSpec((count, block), lambda i, c: (0, c[0] * steps + i)),
            ],
            out_specs=[out_spec, out_spec],
        ),
        out_shape=[half, half],
        cost_estimate=pl.CostEstimate(
            flops=2 * cols * count * chunk_width,
            bytes_accessed=2 * (count * chunk_width + cols * chunk_width + cols * count),
            transcendentals=0,
        ),
        name="partial_terms",
    )(chunk.reshape(1), cot_rows, tokens)


def forward_kernel(scale, chunk_ref, tokens_ref, weight_ref, out_ref, total):
    step = pl.program_id(0)

    @pl.when(step == 0)
    def _():
        total[...] = jnp.zeros_like(total)

    total[...] += lax.dot_general(
        tokens_ref[...], weight_ref[...], (((1,), (1,)), ((), ())), preferred_element_type=f32
    )

    @pl.when(step == pl.num_programs(0) - 1)
    def _():
        out_ref[...] = (total[...] * scale).astype(bf16)


def forward(x, tokens, weight):
    count, width = tokens.shape
    cols, chunk_width = weight.shape[0], width // NX
    block = block_of(chunk_width)
    steps = chunk_width // block
    return pl.pallas_call(
        functools.partial(forward_kernel, width ** (-0.5)),
        grid_spec=pltpu.PrefetchScalarGridSpec(
            num_scalar_prefetch=1,
            grid=(NX * steps,),
            in_specs=[
                pl.BlockSpec(
                    (count, block),
                    lambda i, c: (0, lax.rem(c[0] + NX - i // steps, NX) * steps + lax.rem(i, steps)),
                ),
                pl.BlockSpec((cols, block), lambda i, c: (0, i)),
            ],
            out_specs=pl.BlockSpec((count, cols), lambda i, c: (0, 0)),
            scratch_shapes=[pltpu.VMEM((count, cols), f32)],
        ),
        out_shape=jax.ShapeDtypeStruct((count, cols), bf16),
        cost_estimate=pl.CostEstimate(
            flops=2 * cols * count * width,
            bytes_accessed=2 * (count * width + cols * width + cols * count),
            transcendentals=0,
        ),
        name="forward",
    )(x.reshape(1), tokens, weight)


def rolled(value, y, back=False):
    shift = (NY - y) % NY if back else y
    wide = jnp.concatenate([value, value], -1)
    part = value.shape[-1] // NY
    return lax.dynamic_slice_in_dim(wide, shift * part, NY * part, value.ndim - 1)


def own_first(value, c, y, back=False):
    quarter = value.shape[1] // 4
    parts = [rolled(value[:, i * quarter : (i + 1) * quarter], y, back) for i in range(4)]
    lower, upper = jnp.concatenate(parts[:2], 1), jnp.concatenate(parts[2:], 1)
    return jnp.where(
        c == 0, jnp.concatenate([lower, upper], 1), jnp.concatenate([upper, lower], 1)
    )


def add(*parts):
    total = parts[0].astype(f32)
    for part in parts[1:]:
        total = total + part.astype(f32)
    return total


def body(tokens, cotangent, master, first_moment, second_moment):
    y, c, x = lax.axis_index("y"), lax.axis_index("core"), lax.axis_index("x")
    rows, cols = master.shape
    count = rows * NX * NZ * cols
    unit = cols // (NC * 2 * NY)
    quad = NY * unit
    span = rows * NZ

    cot_rows = own_first(cotangent, c, y).T
    chip = {}
    for d in (2, 1, 3, 0):
        own, other = partial_terms((x + d) % NX, cot_rows, tokens)
        chip[d] = add(own, send(other, "core", 1)).astype(bf16)
    got = [send(chip[d][:quad], "x", d) for d in FAR_FIRST]
    half_b = jnp.concatenate([chip[d][quad:] for d in range(NX)], 1)
    got_b = [send(half_b[d * unit : (d + 1) * unit], "y", d) for d in FAR_FIRST]
    half_a = add(chip[0][:quad], *got).astype(bf16)
    half_b = add(half_b[:unit], *got_b).astype(bf16)
    got = [send(half_a[d * unit : (d + 1) * unit], "y", d) for d in FAR_FIRST]
    got_b = [send(half_b[:, d * span : (d + 1) * span], "x", d) for d in FAR_FIRST]
    half_a = add(half_a[:unit], *got).astype(bf16)
    half_b = add(half_b[:, :span], *got_b).astype(bf16)
    plane = jnp.concatenate([half_a, half_b])
    planes = lax.all_to_all(plane, "z", 1, 0, tiled=True).reshape(NZ, 2 * unit, rows)
    piece = jnp.sum(planes.astype(f32), 0)

    square = jnp.sum(piece * piece).reshape(1, 1)
    squares = lax.all_to_all(
        jnp.broadcast_to(square, (NY * NC * NX * NZ, 1)), NAMES, 0, 0, tiled=True
    )
    total = jnp.sum(squares)
    piece = piece.astype(bf16)

    def state_piece(state):
        at = c * (cols // 2) + y * unit
        return jnp.concatenate(
            [lax.dynamic_slice_in_dim(state, at + h * quad, unit, 1) for h in range(2)], 1
        ).T

    states = [state_piece(state) for state in (master, first_moment, second_moment)]
    weight = apply_update(piece.astype(f32), *states, total, count)[0].astype(bf16)

    plane = lax.all_to_all(jnp.tile(weight, (NZ, 1)), "z", 0, 1, tiled=True)
    got = [plane[:unit]] + [send(plane[:unit], "y", d) for d in (1, 2, 3)]
    got_b = [plane[unit:]] + [send(plane[unit:], "x", d) for d in (1, 2, 3)]
    half_a = jnp.concatenate(got, 0)
    half_b = jnp.concatenate(got_b, 1)
    got = [half_a] + [send(half_a, "x", d) for d in (1, 2, 3)]
    got_b = [half_b] + [send(half_b, "y", d) for d in (1, 2, 3)]

    def whole(parts, parts_b):
        return [jnp.concatenate(parts, 1)] + parts_b

    other = [send(part, "core", 1) for part in got]
    other_b = [send(part, "core", 1) for part in got_b]
    weight = jnp.concatenate(whole(got, got_b) + whole(other, other_b), 0)
    out = forward(x, tokens, weight)
    pieces = [out[:, i * unit : (i + 1) * unit] for i in range(NC * 2 * NY)]
    out = jnp.concatenate(
        [pieces[q * NY + (NY - e) % NY] for q in range(NC * 2) for e in range(NY)], 1
    )
    activations = own_first(out, c, y, back=True)

    grads = lax.all_to_all(jnp.tile(piece, (NY * NC, 1)), ("core", "y"), 0, 0, tiled=True)
    grads = grads.reshape(NC, NY, 2, unit, rows).transpose(0, 2, 1, 3, 4).reshape(cols, rows)
    master_new, first_new, second_new = apply_update(
        grads.T.astype(f32), master, first_moment, second_moment, total, count
    )
    return (master_new, first_new, second_new, activations)


def solution(mesh):
    fine = Mesh(mesh.devices.reshape(NY, NC, NX, NZ), NAMES)
    by_token, by_row = P(NAMES, None), P(("x", "z"), None)
    return jax.shard_map(
        body,
        mesh=fine,
        in_specs=(by_token, by_token, by_row, by_row, by_row),
        out_specs=(by_row, by_row, by_row, by_token),
        check_vma=False,
    )
```

time: 489 us -> 210 us (0.43)
  waiting for transfers between devices: 388 us -> 49.3 us
  starting transfers between devices: 0.12 us -> 85.3 us
  blocking collectives: 61.7 us -> 12 us
  Pallas kernels: 0 us -> 29.7 us
  local copies, waits for them, and re-layouts: 0.87 us -> 23.1 us
  matrix products: 20 us -> 0 us
  between operations: 14.5 us -> 1.84 us
    reduce_scatter x1 -> x0, waiting for transfers between devices: 225 us -> none  [body(): lax.psum_scatter(row_terms(tokens, cotangent).astype(jnp.bfloat16), 'shar...]
    all_gather x1 -> x0, waiting for transfers between devices: 95.7 us -> none  [body(): lax.all_gather(weight, 'shard', axis=0, tiled=True)]
    psum x1 -> x0, waiting for transfers between devices: 66.9 us -> none  [body(): grads = lax.psum(grads.astype(jnp.bfloat16), 'rep').astype(jnp.float32)]
    psum x1 -> x0, blocking collectives: 61.7 us -> none  [body(): total = lax.psum(jnp.sum(grads * grads), 'shard')]
    ppermute x0 -> x36, starting transfers between devices: none -> 56.8 us  [send(): return lax.ppermute(value, axis, [(i, (i + step) % n) for i in range(n)])]
    pallas_call x0 -> x5, Pallas kernels: none -> 29.7 us  [the longest x4 17.2 us: partial_terms(): pl.pallas_call(partial_kernel, grid_spec=pltpu.PrefetchScalarGridSpec(num...]
    all_to_all x0 -> x3, starting transfers between devices: none -> 28.6 us  [the longest x1 13.1 us: body(): lax.all_to_all(jnp.broadcast_to(square, (NY * NC * NX * NZ, 1)), NAMES, 0...]
    ppermute x0 -> x36, waiting for transfers between devices: none -> 28.3 us  [send(): return lax.ppermute(value, axis, [(i, (i + step) % n) for i in range(n)])]
  transfers between devices with their start and end apart: 3 -> 39, of which waited for: 3 -> 14; matrix products, arithmetic and copies ran while one was open for 0% -> 8% of each run, Pallas kernels for 0% -> 6%
where the time goes in v1:
time: 210 us; the launch traced here: 209 us
  starting transfers between devices  85.3 us (41%)
  waiting for transfers between devices  49.3 us (23%)
  Pallas kernels  29.7 us (14%)
  local copies, waits for them, and re-layouts  23.1 us (11%)
  blocking collectives  12 us (6%)
  other arithmetic  7.73 us (4%)
    ppermute x36, starting transfers between devices, send(): return lax.ppermute(value, axis, [(i, (i + step) % n) for i in range(n)])  56.8 us
    ppermute x36, waiting for transfers between devices, send(): return lax.ppermute(value, axis, [(i, (i + step) % n) for i in range(n)])  28.3 us
    pallas_call x4, Pallas kernels, partial_terms(): pl.pallas_call(partial_kernel, grid_spec=pltpu.PrefetchScalarGridSpec(num...  17.2 us
    all_to_all x1, starting transfers between devices, body(): lax.all_to_all(jnp.broadcast_to(square, (NY * NC * NX * NZ, 1)), NAMES, 0...  13.1 us
    all_to_all x1, waiting for transfers between devices, body(): lax.all_to_all(jnp.broadcast_to(square, (NY * NC * NX * NZ, 1)), NAMES, 0...  13 us
    pallas_call x1, Pallas kernels, forward(): pl.pallas_call(functools.partial(forward_kernel, width ** (-0.5)), grid_s...  12.5 us
    unnamed x35, local copies, waits for them, and re-layouts  12 us
    all_to_all x1, blocking collectives, body(): plane = lax.all_to_all(jnp.tile(weight, (NZ, 1)), 'z', 0, 1, tiled=True)  12 us
  transfers between devices with their start and end apart: 39, of which 14 were waited for; matrix products, arithmetic and copies ran while one was open for 8% of the time, Pallas kernels for 6%

profile of v1, /device:TPU:1, one launch (start us, length us, event | category | flops | bytes accessed | tf_op | source)
XLA Modules:
  0.0 208.9 jit_solution(4170408247616615827)
XLA Ops:
  3.6 4.3 %partial_terms.7 = (bf16[128,3072]{1,0:T(8,128)(2,1)}, bf16[128,3072]{1,0:T(8,128)(2,1)}) custom-call(s32[1]{0:T(128)} %bitcast.4.chunk_ref, bf16[256,448]{1,0:T(8,128)(2,1)} %copy.74.cot_ref, bf16[448,12288]{1,0:T(8,128)(2,1)} %tokens_ref.9), custom_call_target="tpu_custom_call" | custom-call | flops 704643072 | bytes 4554752 | tf_op jit(solution)/shard_map/partial_terms/pallas_call | solution.py:68
  7.8 3.2 %collective-permute-start.5 = (bf16[128,3072]{1,0:T(8,128)(2,1)}, bf16[128,3072]{1,0:T(8,128)(2,1)S(1)}, u32[]{:S(2)}, u32[]{:S(2)}) collective-permute-start(bf16[128,3072]{1,0:T(8,128)(2,1)} %get-tuple-element.19), channel_id=1, source_target_pairs={{0,32},{32,0},{1,33},{33,1},{2,34},{34,2},{3,35},{35,3},{4,36},{36... | collective-permute-start | bytes 2359304 | tf_op jit(solution)/shard_map/ppermute | solution.py:41
  11.1 4.3 %partial_terms.5 = (bf16[128,3072]{1,0:T(8,128)(2,1)}, bf16[128,3072]{1,0:T(8,128)(2,1)}) custom-call(s32[1]{0:T(128)} %bitcast.2.chunk_ref, bf16[256,448]{1,0:T(8,128)(2,1)} %copy.74.cot_ref, bf16[448,12288]{1,0:T(8,128)(2,1)} %tokens_ref.9), custom_call_target="tpu_custom_call" | custom-call | flops 704643072 | bytes 4554752 | tf_op jit(solution)/shard_map/partial_terms/pallas_call | solution.py:68
  15.4 4.3 %partial_terms.6 = (bf16[128,3072]{1,0:T(8,128)(2,1)}, bf16[128,3072]{1,0:T(8,128)(2,1)}) custom-call(s32[1]{0:T(128)} %bitcast.3.chunk_ref, bf16[256,448]{1,0:T(8,128)(2,1)} %copy.74.cot_ref, bf16[448,12288]{1,0:T(8,128)(2,1)} %tokens_ref.9), custom_call_target="tpu_custom_call" | custom-call | flops 704643072 | bytes 4554752 | tf_op jit(solution)/shard_map/partial_terms/pallas_call | solution.py:68
  20.2 4.4 %partial_terms.4 = (bf16[128,3072]{1,0:T(8,128)(2,1)}, bf16[128,3072]{1,0:T(8,128)(2,1)}) custom-call(s32[1]{0:T(128)} %bitcast.chunk_ref, bf16[256,448]{1,0:T(8,128)(2,1)} %copy.74.cot_ref, bf16[448,12288]{1,0:T(8,128)(2,1)} %tokens_ref.9), custom_call_target="tpu_custom_call" | custom-call | flops 704643072 | bytes 4554752 | tf_op jit(solution)/shard_map/partial_terms/pallas_call | solution.py:68
  30.2 2.5 %collective-permute-start.6 = (bf16[64,3072]{1,0:T(8,128)(2,1)S(1)}, bf16[64,3072]{1,0:T(8,128)(2,1)S(1)}, u32[]{:S(2)}, u32[]{:S(2)}) collective-permute-start(bf16[64,3072]{1,0:T(8,128)(2,1)S(1)} %get-tuple-element.48), channel_id=1, source_target_pairs={{0,24},{8,0},{16,8},{24,16},{1,25},{9,1},{17,9},{25,17},{2,26},{10... | collective-permute-start | bytes 1179656 | tf_op jit(solution)/shard_map/ppermute | solution.py:41
  32.7 5.4 %collective-permute-done.12 = bf16[16,12288]{1,0:T(8,128)(2,1)S(1)} collective-permute-done((bf16[16,12288]{1,0:T(8,128)(2,1)S(1)}, bf16[16,12288]{1,0:T(8,128)(2,1)S(1)}, u32[]{:S(2)}, u32[]{:S(2)}) %collective-permute-start.12) | collective-permute-done | bytes 393248 | tf_op jit(solution)/shard_map/ppermute | solution.py:41
  38.1 9.8 %collective-permute-start.2 = (bf16[64,3072]{1,0:T(8,128)(2,1)S(1)}, bf16[64,3072]{1,0:T(8,128)(2,1)S(1)}, u32[]{:S(2)}, u32[]{:S(2)}) collective-permute-start(bf16[64,3072]{1,0:T(8,128)(2,1)S(1)} %get-tuple-element.44), channel_id=1, source_target_pairs={{0,16},{8,24},{16,0},{24,8},{1,17},{9,25},{17,1},{25,9},{2,18},{10... | collective-permute-start | bytes 1179656 | tf_op jit(solution)/shard_map/ppermute | solution.py:41
  48.7 2.6 %collective-permute-start.15 = (bf16[16,3072]{1,0:T(8,128)(2,1)S(1)}, bf16[16,3072]{1,0:T(8,128)(2,1)S(1)}, u32[]{:S(2)}, u32[]{:S(2)}) collective-permute-start(bf16[16,3072]{1,0:T(8,128)(2,1)S(1)} %get-tuple-element.54), channel_id=1, source_target_pairs={{0,24},{8,0},{16,8},{24,16},{1,25},{9,1},{17,9},{25,17},{2,26},{10... | collective-permute-start | bytes 294920 | tf_op jit(solution)/shard_map/ppermute | solution.py:41
  51.3 1.7 collective-permute-start.13
  53.0 3.3 %collective-permute-done.2 = bf16[64,3072]{1,0:T(8,128)(2,1)S(1)} collective-permute-done((bf16[64,3072]{1,0:T(8,128)(2,1)S(1)}, bf16[64,3072]{1,0:T(8,128)(2,1)S(1)}, u32[]{:S(2)}, u32[]{:S(2)}) %collective-permute-start.2) | collective-permute-done | bytes 393248 | tf_op jit(solution)/shard_map/ppermute | solution.py:41
  56.5 3.8 %collective-permute-start.9 = (bf16[16,3072]{1,0:T(8,128)(2,1)S(1)}, bf16[16,3072]{1,0:T(8,128)(2,1)S(1)}, u32[]{:S(2)}, u32[]{:S(2)}) collective-permute-start(bf16[16,3072]{1,0:T(8,128)(2,1)S(1)} %get-tuple-element.51), channel_id=1, source_target_pairs={{0,192},{64,0},{128,64},{192,128},{1,193},{65,1},{129,65},{193,129... | collective-permute-start | bytes 294920 | tf_op jit(solution)/shard_map/ppermute | solution.py:41
  62.0 4.1 %collective-permute-done.8 = bf16[16,3072]{1,0:T(8,128)(2,1)S(1)} collective-permute-done((bf16[16,3072]{1,0:T(8,128)(2,1)S(1)}, bf16[16,3072]{1,0:T(8,128)(2,1)S(1)}, u32[]{:S(2)}, u32[]{:S(2)}) %collective-permute-start.8) | collective-permute-done | bytes 98336 | tf_op jit(solution)/shard_map/ppermute | solution.py:41
  66.9 8.1 %all-to-all-start = ((bf16[32,8,384]{2,0,1:T(8,128)(2,1)}), bf16[32,8,384]{2,0,1:T(8,128)(2,1)S(1)}, u32[]{:S(2)}, u32[]{:S(2)}) async-start(bf16[32,8,384]{2,0,1:T(8,128)(2,1)} %bitcast.49), calls=%async_computation | async-start | bytes 393216 | tf_op jit(solution)/shard_map/all_to_all | solution.py:181
  75.5 8.1 %all-to-all-done = bf16[32,8,384]{2,0,1:T(8,128)(2,1)S(1)} async-done(((bf16[32,8,384]{2,0,1:T(8,128)(2,1)}), bf16[32,8,384]{2,0,1:T(8,128)(2,1)S(1)}, u32[]{:S(2)}, u32[]{:S(2)}) %all-to-all-start) | async-done | bytes 196640 | tf_op jit(solution)/shard_map/all_to_all | solution.py:181
  85.6 13.1 %all-to-all-start.2 = ((f32[256,1,1]{2,1,0:T(1,128)}), f32[256,1,1]{2,1,0:T(1,128)S(1)}, u32[]{:S(2)}, u32[]{:S(2)}) async-start(f32[256,1,1]{2,1,0:T(1,128)} %broadcast_in_dim.2), calls=%async_computation.2 | async-start | bytes 262144 | tf_op jit(solution)/shard_map/all_to_all | solution.py:185
  98.7 13.0 %all-to-all-done.2 = f32[256,1,1]{2,1,0:T(1,128)S(1)} async-done(((f32[256,1,1]{2,1,0:T(1,128)}), f32[256,1,1]{2,1,0:T(1,128)S(1)}, u32[]{:S(2)}, u32[]{:S(2)}) %all-to-all-start.2) | async-done | bytes 1056 | tf_op jit(solution)/shard_map/all_to_all | solution.py:185
  113.4 12.0 %all_to_all.38 = bf16[8,32,384]{2,1,0:T(8,128)(2,1)S(1)} all-to-all(bf16[8,32,384]{2,1,0:T(8,128)(2,1)S(1)} %tile.5), channel_id=1, replica_groups=mesh['y'=4,'core'=2,'x'=4,'z'=8] {'z'}, dimensions={0} | all-to-all | bytes 393216 | tf_op jit(solution)/shard_map/all_to_all | solution.py:200
  125.8 1.7 collective-permute-start.17
  128.3 2.9 %collective-permute-done.16 = bf16[16,3072]{1,0:T(8,128)(2,1)S(1)} collective-permute-done((bf16[16,3072]{1,0:T(8,128)(2,1)S(1)}, bf16[16,3072]{1,0:T(8,128)(2,1)S(1)}, u32[]{:S(2)}, u32[]{:S(2)}) %collective-permute-start.16) | collective-permute-done | bytes 98336 | tf_op jit(solution)/shard_map/ppermute | solution.py:41
  132.3 2.1 collective-permute-start.20
  135.1 7.4 %all-to-all-start.1 = ((bf16[8,32,384]{2,1,0:T(8,128)(2,1)}), bf16[8,32,384]{2,1,0:T(8,128)(2,1)S(1)}, u32[]{:S(2)}, u32[]{:S(2)}) async-start(bf16[8,32,384]{2,1,0:T(8,128)(2,1)} %tile.4), calls=%async_computation.1 | async-start | bytes 393216 | tf_op jit(solution)/shard_map/all_to_all | solution.py:221
  143.9 2.8 %collective-permute-start.23 = (bf16[16,3072]{1,0:T(8,128)(2,1)S(1)}, bf16[16,3072]{1,0:T(8,128)(2,1)S(1)}, u32[]{:S(2)}, u32[]{:S(2)}) collective-permute-start(bf16[16,3072]{1,0:T(8,128)(2,1)S(1)} %bitcast.58), channel_id=1, source_target_pairs={{0,16},{8,24},{16,0},{24,8},{1,17},{9,25},{17,1},{25,9},{2,18},{10... | collective-permute-start | bytes 294920 | tf_op jit(solution)/shard_map/ppermute | solution.py:41
  147.9 5.9 %collective-permute-done.19 = bf16[64,3072]{1,0:T(8,128)(2,1)S(1)} collective-permute-done((bf16[64,3072]{1,0:T(8,128)(2,1)S(1)}, bf16[64,3072]{1,0:T(8,128)(2,1)S(1)}, u32[]{:S(2)}, u32[]{:S(2)}) %collective-permute-start.19) | collective-permute-done | bytes 393248 | tf_op jit(solution)/shard_map/ppermute | solution.py:41
  161.2 2.5 %collective-permute-start.28 = (bf16[64,3072]{1,0:T(8,128)(2,1)S(1)}, bf16[64,3072]{1,0:T(8,128)(2,1)S(1)}, u32[]{:S(2)}, u32[]{:S(2)}) collective-permute-start(bf16[64,3072]{1,0:T(8,128)(2,1)S(1)} %constant_dynamic-update-slice_fusion), channel_id=1, source_target_pairs={{0,32},{32,0},{1,33},{33,1},{2,34},{34,2},{3,35},{35,3},{4,36},{36... | collective-permute-start | bytes 1179656 | tf_op jit(solution)/shard_map/ppermute | solution.py:41
  163.7 2.9 %collective-permute-start.26 = (bf16[16,12288]{1,0:T(8,128)(2,1)}, bf16[16,12288]{1,0:T(8,128)(2,1)S(1)}, u32[]{:S(2)}, u32[]{:S(2)}) collective-permute-start(bf16[16,12288]{1,0:T(8,128)(2,1)} %get-tuple-element.84), channel_id=1, source_target_pairs={{0,128},{64,192},{128,0},{192,64},{1,129},{65,193},{129,1},{193,65... | collective-permute-start | bytes 1179656 | tf_op jit(solution)/shard_map/ppermute | solution.py:41
  166.9 1.6 collective-permute-done.25
  168.5 11.0 %collective-permute-start.31 = (bf16[64,3072]{1,0:T(8,128)(2,1)}, bf16[64,3072]{1,0:T(8,128)(2,1)S(1)}, u32[]{:S(2)}, u32[]{:S(2)}) collective-permute-start(bf16[64,3072]{1,0:T(8,128)(2,1)} %copy-done.4), channel_id=1, source_target_pairs={{0,32},{32,0},{1,33},{33,1},{2,34},{34,2},{3,35},{35,3},{4,36},{36... | collective-permute-start | bytes 1179656 | tf_op jit(solution)/shard_map/ppermute | solution.py:41
  179.5 1.8 constant_dynamic-update-slice_fusion.14
  182.1 2.3 %collective-permute-done.27 = bf16[16,12288]{1,0:T(8,128)(2,1)S(1)} collective-permute-done((bf16[16,12288]{1,0:T(8,128)(2,1)}, bf16[16,12288]{1,0:T(8,128)(2,1)S(1)}, u32[]{:S(2)}, u32[]{:S(2)}) %collective-permute-start.27) | collective-permute-done | bytes 393248 | tf_op jit(solution)/shard_map/ppermute | solution.py:41
  191.0 12.5 %forward.1 = bf16[448,256]{1,0:T(8,128)(2,1)} custom-call(s32[1]{0:T(128)} %bitcast.10.chunk_ref, bf16[448,12288]{1,0:T(8,128)(2,1)} %tokens_ref.9, bf16[256,12288]{1,0:T(8,128)(2,1)} %constant_dynamic-update-slice_fusion.8.weight_ref), custom_call_target="tpu_custom_call" | custom-call | flops 2818572288 | bytes 17530880 | tf_op jit(solution)/shard_map/forward/pallas_call | solution.py:110
  203.5 2.6 %fusion.21 = (bf16[448,16]{1,0:T(8,128)(2,1)S(1)}, bf16[448,16]{1,0:T(8,128)(2,1)S(1)}, bf16[448,16]{1,0:T(8,128)(2,1)S(1)}, bf16[448,16]{1,0:T(8,128)(2,1)S(1)}...) fusion(bf16[448,256]{1,0:T(8,128)(2,1)} %forward.1), kind=kLoop, calls=%fused_computation.80 | loop fusion | bytes 458752 | tf_op jit(solution)/shard_map/slice | solution.py:215
  (139 shorter events, 39.2 us)
Async XLA Ops:
  7.8 16.7 %collective-permute-start.5 = (bf16[128,3072]{1,0:T(8,128)(2,1)}, bf16[128,3072]{1,0:T(8,128)(2,1)S(1)}, u32[]{:S(2)}, u32[]{:S(2)}) collective-permute-start(bf16[128,3072]{1,0:T(8,128)(2,1)} %get-tuple-element.19), channel_id=1, source_target_pairs={{0,32},{32,0},{1,33},{33,1},{2,34},{34,2},{3,35},{35,3},{4,36},{36... | collective-permute-start | bytes 2359304 | tf_op jit(solution)/shard_map/ppermute | solution.py:41
  15.4 9.5 %collective-permute-start.1 = (bf16[128,3072]{1,0:T(8,128)(2,1)}, bf16[128,3072]{1,0:T(8,128)(2,1)S(1)}, u32[]{:S(2)}, u32[]{:S(2)}) collective-permute-start(bf16[128,3072]{1,0:T(8,128)(2,1)} %get-tuple-element.15), channel_id=1, source_target_pairs={{0,32},{32,0},{1,33},{33,1},{2,34},{34,2},{3,35},{35,3},{4,36},{36... | collective-permute-start | bytes 2359304 | tf_op jit(solution)/shard_map/ppermute | solution.py:41
  19.7 6.2 %collective-permute-start.3 = (bf16[128,3072]{1,0:T(8,128)(2,1)}, bf16[128,3072]{1,0:T(8,128)(2,1)S(1)}, u32[]{:S(2)}, u32[]{:S(2)}) collective-permute-start(bf16[128,3072]{1,0:T(8,128)(2,1)} %get-tuple-element.17), channel_id=1, source_target_pairs={{0,32},{32,0},{1,33},{33,1},{2,34},{34,2},{3,35},{35,3},{4,36},{36... | collective-permute-start | bytes 2359304 | tf_op jit(solution)/shard_map/ppermute | solution.py:41
  27.5 10.7 %collective-permute-start.12 = (bf16[16,12288]{1,0:T(8,128)(2,1)S(1)}, bf16[16,12288]{1,0:T(8,128)(2,1)S(1)}, u32[]{:S(2)}, u32[]{:S(2)}) collective-permute-start(bf16[16,12288]{1,0:T(8,128)(2,1)S(1)} %get-tuple-element.42), channel_id=1, source_target_pairs={{0,192},{64,0},{128,64},{192,128},{1,193},{65,1},{129,65},{193,129... | collective-permute-start | bytes 1179656 | tf_op jit(solution)/shard_map/ppermute | solution.py:41
  28.5 19.9 %collective-permute-start.11 = (bf16[16,12288]{1,0:T(8,128)(2,1)S(1)}, bf16[16,12288]{1,0:T(8,128)(2,1)S(1)}, u32[]{:S(2)}, u32[]{:S(2)}) collective-permute-start(bf16[16,12288]{1,0:T(8,128)(2,1)S(1)} %get-tuple-element.43), channel_id=1, source_target_pairs={{0,64},{64,128},{128,192},{192,0},{1,65},{65,129},{129,193},{193,1... | collective-permute-start | bytes 1179656 | tf_op jit(solution)/shard_map/ppermute | solution.py:41
  29.0 19.4 %collective-permute-start.10 = (bf16[16,12288]{1,0:T(8,128)(2,1)S(1)}, bf16[16,12288]{1,0:T(8,128)(2,1)S(1)}, u32[]{:S(2)}, u32[]{:S(2)}) collective-permute-start(bf16[16,12288]{1,0:T(8,128)(2,1)S(1)} %get-tuple-element.41), channel_id=1, source_target_pairs={{0,128},{64,192},{128,0},{192,64},{1,129},{65,193},{129,1},{193,65... | collective-permute-start | bytes 1179656 | tf_op jit(solution)/shard_map/ppermute | solution.py:41
  30.2 21.1 %collective-permute-start.6 = (bf16[64,3072]{1,0:T(8,128)(2,1)S(1)}, bf16[64,3072]{1,0:T(8,128)(2,1)S(1)}, u32[]{:S(2)}, u32[]{:S(2)}) collective-permute-start(bf16[64,3072]{1,0:T(8,128)(2,1)S(1)} %get-tuple-element.48), channel_id=1, source_target_pairs={{0,24},{8,0},{16,8},{24,16},{1,25},{9,1},{17,9},{25,17},{2,26},{10... | collective-permute-start | bytes 1179656 | tf_op jit(solution)/shard_map/ppermute | solution.py:41
  32.7 20.3 %collective-permute-start.4 = (bf16[64,3072]{1,0:T(8,128)(2,1)S(1)}, bf16[64,3072]{1,0:T(8,128)(2,1)S(1)}, u32[]{:S(2)}, u32[]{:S(2)}) collective-permute-start(bf16[64,3072]{1,0:T(8,128)(2,1)S(1)} %get-tuple-element.46), channel_id=1, source_target_pairs={{0,8},{8,16},{16,24},{24,0},{1,9},{9,17},{17,25},{25,1},{2,10},{10... | collective-permute-start | bytes 1179656 | tf_op jit(solution)/shard_map/ppermute | solution.py:41
  38.1 18.2 %collective-permute-start.2 = (bf16[64,3072]{1,0:T(8,128)(2,1)S(1)}, bf16[64,3072]{1,0:T(8,128)(2,1)S(1)}, u32[]{:S(2)}, u32[]{:S(2)}) collective-permute-start(bf16[64,3072]{1,0:T(8,128)(2,1)S(1)} %get-tuple-element.44), channel_id=1, source_target_pairs={{0,16},{8,24},{16,0},{24,8},{1,17},{9,25},{17,1},{25,9},{2,18},{10... | collective-permute-start | bytes 1179656 | tf_op jit(solution)/shard_map/ppermute | solution.py:41
  48.7 11.7 %collective-permute-start.15 = (bf16[16,3072]{1,0:T(8,128)(2,1)S(1)}, bf16[16,3072]{1,0:T(8,128)(2,1)S(1)}, u32[]{:S(2)}, u32[]{:S(2)}) collective-permute-start(bf16[16,3072]{1,0:T(8,128)(2,1)S(1)} %get-tuple-element.54), channel_id=1, source_target_pairs={{0,24},{8,0},{16,8},{24,16},{1,25},{9,1},{17,9},{25,17},{2,26},{10... | collective-permute-start | bytes 294920 | tf_op jit(solution)/shard_map/ppermute | solution.py:41
  51.3 10.4 %collective-permute-start.14 = (bf16[16,3072]{1,0:T(8,128)(2,1)S(1)}, bf16[16,3072]{1,0:T(8,128)(2,1)S(1)}, u32[]{:S(2)}, u32[]{:S(2)}) collective-permute-start(bf16[16,3072]{1,0:T(8,128)(2,1)S(1)} %get-tuple-element.55), channel_id=1, source_target_pairs={{0,8},{8,16},{16,24},{24,0},{1,9},{9,17},{17,25},{25,1},{2,10},{10... | collective-permute-start | bytes 294920 | tf_op jit(solution)/shard_map/ppermute | solution.py:41
  51.3 10.4 %collective-permute-start.13 = (bf16[16,3072]{1,0:T(8,128)(2,1)S(1)}, bf16[16,3072]{1,0:T(8,128)(2,1)S(1)}, u32[]{:S(2)}, u32[]{:S(2)}) collective-permute-start(bf16[16,3072]{1,0:T(8,128)(2,1)S(1)} %get-tuple-element.53), channel_id=1, source_target_pairs={{0,16},{8,24},{16,0},{24,8},{1,17},{9,25},{17,1},{25,9},{2,18},{10... | collective-permute-start | bytes 294920 | tf_op jit(solution)/shard_map/ppermute | solution.py:41
  56.5 5.5 %collective-permute-start.9 = (bf16[16,3072]{1,0:T(8,128)(2,1)S(1)}, bf16[16,3072]{1,0:T(8,128)(2,1)S(1)}, u32[]{:S(2)}, u32[]{:S(2)}) collective-permute-start(bf16[16,3072]{1,0:T(8,128)(2,1)S(1)} %get-tuple-element.51), channel_id=1, source_target_pairs={{0,192},{64,0},{128,64},{192,128},{1,193},{65,1},{129,65},{193,129... | collective-permute-start | bytes 294920 | tf_op jit(solution)/shard_map/ppermute | solution.py:41
  60.4 5.7 %collective-permute-start.8 = (bf16[16,3072]{1,0:T(8,128)(2,1)S(1)}, bf16[16,3072]{1,0:T(8,128)(2,1)S(1)}, u32[]{:S(2)}, u32[]{:S(2)}) collective-permute-start(bf16[16,3072]{1,0:T(8,128)(2,1)S(1)} %get-tuple-element.52), channel_id=1, source_target_pairs={{0,64},{64,128},{128,192},{192,0},{1,65},{65,129},{129,193},{193,1... | collective-permute-start | bytes 294920 | tf_op jit(solution)/shard_map/ppermute | solution.py:41
  60.4 5.7 %collective-permute-start.7 = (bf16[16,3072]{1,0:T(8,128)(2,1)S(1)}, bf16[16,3072]{1,0:T(8,128)(2,1)S(1)}, u32[]{:S(2)}, u32[]{:S(2)}) collective-permute-start(bf16[16,3072]{1,0:T(8,128)(2,1)S(1)} %get-tuple-element.50), channel_id=1, source_target_pairs={{0,128},{64,192},{128,0},{192,64},{1,129},{65,193},{129,1},{193,65... | collective-permute-start | bytes 294920 | tf_op jit(solution)/shard_map/ppermute | solution.py:41
  66.9 16.7 %all-to-all-start = ((bf16[32,8,384]{2,0,1:T(8,128)(2,1)}), bf16[32,8,384]{2,0,1:T(8,128)(2,1)S(1)}, u32[]{:S(2)}, u32[]{:S(2)}) async-start(bf16[32,8,384]{2,0,1:T(8,128)(2,1)} %bitcast.49), calls=%async_computation | async-start | bytes 393216 | tf_op jit(solution)/shard_map/all_to_all | solution.py:181
  85.6 26.0 %all-to-all-start.2 = ((f32[256,1,1]{2,1,0:T(1,128)}), f32[256,1,1]{2,1,0:T(1,128)S(1)}, u32[]{:S(2)}, u32[]{:S(2)}) async-start(f32[256,1,1]{2,1,0:T(1,128)} %broadcast_in_dim.2), calls=%async_computation.2 | async-start | bytes 262144 | tf_op jit(solution)/shard_map/all_to_all | solution.py:185
  125.4 5.8 %collective-permute-start.16 = (bf16[16,3072]{1,0:T(8,128)(2,1)S(1)}, bf16[16,3072]{1,0:T(8,128)(2,1)S(1)}, u32[]{:S(2)}, u32[]{:S(2)}) collective-permute-start(bf16[16,3072]{1,0:T(8,128)(2,1)S(1)} %bitcast.53), channel_id=1, source_target_pairs={{0,64},{64,128},{128,192},{192,0},{1,65},{65,129},{129,193},{193,1... | collective-permute-start | bytes 294920 | tf_op jit(solution)/shard_map/ppermute | solution.py:41
  125.8 5.4 %collective-permute-start.17 = (bf16[16,3072]{1,0:T(8,128)(2,1)S(1)}, bf16[16,3072]{1,0:T(8,128)(2,1)S(1)}, u32[]{:S(2)}, u32[]{:S(2)}) collective-permute-start(bf16[16,3072]{1,0:T(8,128)(2,1)S(1)} %bitcast.55), channel_id=1, source_target_pairs={{0,128},{64,192},{128,0},{192,64},{1,129},{65,193},{129,1},{193,65... | collective-permute-start | bytes 294920 | tf_op jit(solution)/shard_map/ppermute | solution.py:41
  132.2 14.5 %collective-permute-start.21 = (bf16[64,3072]{1,0:T(8,128)(2,1)S(1)}, bf16[64,3072]{1,0:T(8,128)(2,1)S(1)}, u32[]{:S(2)}, u32[]{:S(2)}) collective-permute-start(bf16[64,3072]{1,0:T(8,128)(2,1)S(1)} %constant_dynamic-update-slice_fusion), channel_id=1, source_target_pairs={{0,24},{8,0},{16,8},{24,16},{1,25},{9,1},{17,9},{25,17},{2,26},{10... | collective-permute-start | bytes 1179656 | tf_op jit(solution)/shard_map/ppermute | solution.py:41
  132.3 15.6 %collective-permute-start.20 = (bf16[64,3072]{1,0:T(8,128)(2,1)S(1)}, bf16[64,3072]{1,0:T(8,128)(2,1)S(1)}, u32[]{:S(2)}, u32[]{:S(2)}) collective-permute-start(bf16[64,3072]{1,0:T(8,128)(2,1)S(1)} %constant_dynamic-update-slice_fusion), channel_id=1, source_target_pairs={{0,16},{8,24},{16,0},{24,8},{1,17},{9,25},{17,1},{25,9},{2,18},{10... | collective-permute-start | bytes 1179656 | tf_op jit(solution)/shard_map/ppermute | solution.py:41
  134.4 19.4 %collective-permute-start.19 = (bf16[64,3072]{1,0:T(8,128)(2,1)S(1)}, bf16[64,3072]{1,0:T(8,128)(2,1)S(1)}, u32[]{:S(2)}, u32[]{:S(2)}) collective-permute-start(bf16[64,3072]{1,0:T(8,128)(2,1)S(1)} %constant_dynamic-update-slice_fusion), channel_id=1, source_target_pairs={{0,8},{8,16},{16,24},{24,0},{1,9},{9,17},{17,25},{25,1},{2,10},{10... | collective-permute-start | bytes 1179656 | tf_op jit(solution)/shard_map/ppermute | solution.py:41
  135.1 22.9 %all-to-all-start.1 = ((bf16[8,32,384]{2,1,0:T(8,128)(2,1)}), bf16[8,32,384]{2,1,0:T(8,128)(2,1)S(1)}, u32[]{:S(2)}, u32[]{:S(2)}) async-start(bf16[8,32,384]{2,1,0:T(8,128)(2,1)} %tile.4), calls=%async_computation.1 | async-start | bytes 393216 | tf_op jit(solution)/shard_map/all_to_all | solution.py:221
  142.5 13.4 %collective-permute-start.22 = (bf16[16,3072]{1,0:T(8,128)(2,1)S(1)}, bf16[16,3072]{1,0:T(8,128)(2,1)S(1)}, u32[]{:S(2)}, u32[]{:S(2)}) collective-permute-start(bf16[16,3072]{1,0:T(8,128)(2,1)S(1)} %bitcast.57), channel_id=1, source_target_pairs={{0,8},{8,16},{16,24},{24,0},{1,9},{9,17},{17,25},{25,1},{2,10},{10... | collective-permute-start | bytes 294920 | tf_op jit(solution)/shard_map/ppermute | solution.py:41
  143.9 12.7 %collective-permute-start.23 = (bf16[16,3072]{1,0:T(8,128)(2,1)S(1)}, bf16[16,3072]{1,0:T(8,128)(2,1)S(1)}, u32[]{:S(2)}, u32[]{:S(2)}) collective-permute-start(bf16[16,3072]{1,0:T(8,128)(2,1)S(1)} %bitcast.58), channel_id=1, source_target_pairs={{0,16},{8,24},{16,0},{24,8},{1,17},{9,25},{17,1},{25,9},{2,18},{10... | collective-permute-start | bytes 294920 | tf_op jit(solution)/shard_map/ppermute | solution.py:41
  146.7 10.6 %collective-permute-start.24 = (bf16[16,3072]{1,0:T(8,128)(2,1)S(1)}, bf16[16,3072]{1,0:T(8,128)(2,1)S(1)}, u32[]{:S(2)}, u32[]{:S(2)}) collective-permute-start(bf16[16,3072]{1,0:T(8,128)(2,1)S(1)} %bitcast.59), channel_id=1, source_target_pairs={{0,24},{8,0},{16,8},{24,16},{1,25},{9,1},{17,9},{25,17},{2,26},{10... | collective-permute-start | bytes 294920 | tf_op jit(solution)/shard_map/ppermute | solution.py:41
  158.0 10.5 %collective-permute-start.25 = (bf16[16,12288]{1,0:T(8,128)(2,1)}, bf16[16,12288]{1,0:T(8,128)(2,1)}, u32[]{:S(2)}, u32[]{:S(2)}) collective-permute-start(bf16[16,12288]{1,0:T(8,128)(2,1)} %get-tuple-element.84), channel_id=1, source_target_pairs={{0,64},{64,128},{128,192},{192,0},{1,65},{65,129},{129,193},{193,1... | collective-permute-start | bytes 1179656 | tf_op jit(solution)/shard_map/ppermute | solution.py:41
  161.2 24.8 %collective-permute-start.28 = (bf16[64,3072]{1,0:T(8,128)(2,1)S(1)}, bf16[64,3072]{1,0:T(8,128)(2,1)S(1)}, u32[]{:S(2)}, u32[]{:S(2)}) collective-permute-start(bf16[64,3072]{1,0:T(8,128)(2,1)S(1)} %constant_dynamic-update-slice_fusion), channel_id=1, source_target_pairs={{0,32},{32,0},{1,33},{33,1},{2,34},{34,2},{3,35},{35,3},{4,36},{36... | collective-permute-start | bytes 1179656 | tf_op jit(solution)/shard_map/ppermute | solution.py:41
  163.7 17.6 %collective-permute-start.26 = (bf16[16,12288]{1,0:T(8,128)(2,1)}, bf16[16,12288]{1,0:T(8,128)(2,1)S(1)}, u32[]{:S(2)}, u32[]{:S(2)}) collective-permute-start(bf16[16,12288]{1,0:T(8,128)(2,1)} %get-tuple-element.84), channel_id=1, source_target_pairs={{0,128},{64,192},{128,0},{192,64},{1,129},{65,193},{129,1},{193,65... | collective-permute-start | bytes 1179656 | tf_op jit(solution)/shard_map/ppermute | solution.py:41
  166.6 17.9 %collective-permute-start.27 = (bf16[16,12288]{1,0:T(8,128)(2,1)}, bf16[16,12288]{1,0:T(8,128)(2,1)S(1)}, u32[]{:S(2)}, u32[]{:S(2)}) collective-permute-start(bf16[16,12288]{1,0:T(8,128)(2,1)} %get-tuple-element.84), channel_id=1, source_target_pairs={{0,192},{64,0},{128,64},{192,128},{1,193},{65,1},{129,65},{193,129... | collective-permute-start | bytes 1179656 | tf_op jit(solution)/shard_map/ppermute | solution.py:41
  166.6 21.3 %collective-permute-start.32 = (bf16[16,12288]{1,0:T(8,128)(2,1)}, bf16[16,12288]{1,0:T(8,128)(2,1)S(1)}, u32[]{:S(2)}, u32[]{:S(2)}) collective-permute-start(bf16[16,12288]{1,0:T(8,128)(2,1)} %get-tuple-element.84), channel_id=1, source_target_pairs={{0,32},{32,0},{1,33},{33,1},{2,34},{34,2},{3,35},{35,3},{4,36},{36... | collective-permute-start | bytes 1179656 | tf_op jit(solution)/shard_map/ppermute | solution.py:41
  168.5 17.5 %collective-permute-start.31 = (bf16[64,3072]{1,0:T(8,128)(2,1)}, bf16[64,3072]{1,0:T(8,128)(2,1)S(1)}, u32[]{:S(2)}, u32[]{:S(2)}) collective-permute-start(bf16[64,3072]{1,0:T(8,128)(2,1)} %copy-done.4), channel_id=1, source_target_pairs={{0,32},{32,0},{1,33},{33,1},{2,34},{34,2},{3,35},{35,3},{4,36},{36... | collective-permute-start | bytes 1179656 | tf_op jit(solution)/shard_map/ppermute | solution.py:41
  (15 other events, 120.7 us)

commit v2 on v0

v2 whole, which is shorter than its diff:
```python
import functools

import jax
import jax.numpy as jnp
from jax import lax
from jax.experimental import pallas as pl
from jax.experimental.pallas import tpu as pltpu
from jax.sharding import Mesh, PartitionSpec as P

STEP = 10

beta_first = 0.9
beta_second = 0.95
learn_rate = 0.02
decay_rate = 0.1
epsilon = 1e-08

NY, NC, NX, NZ = 4, 2, 4, 8
SIZE = {"y": NY, "core": NC, "x": NX, "z": NZ}
NAMES = ("y", "core", "x", "z")
f32 = jnp.float32
bf16 = jnp.bfloat16


def apply_update(grads, master, first, second, total, count):
    rms_value = jnp.sqrt(total / count)
    factor = 1.0 / jnp.maximum(rms_value, 1.0)
    clipped = grads * factor
    first_new = beta_first * first + (1.0 - beta_first) * clipped
    second_new = beta_second * second + (1.0 - beta_second) * clipped * clipped
    first_hat = first_new / (1.0 - beta_first**STEP)
    second_hat = second_new / (1.0 - beta_second**STEP)
    master_new = master - learn_rate * (
        first_hat / (jnp.sqrt(second_hat) + epsilon) + decay_rate * master
    )
    return (master_new, first_new, second_new)


def send(value, axis, step):
    n = SIZE[axis]
    return lax.ppermute(value, axis, [(i, (i + step) % n) for i in range(n)])


FAR_FIRST = (2, 1, 3)


def routed(value, step, first):
    pairs = []
    for y in range(NY):
        for c in range(NC):
            for x in range(NX):
                along_x = (c == 0) == first
                to_y, to_x = (y, (x + step) % NX) if along_x else ((y + step) % NY, x)
                pairs.append(((y * NC + c) * NX + x, (to_y * NC + c) * NX + to_x))
    return lax.ppermute(value, ("y", "core", "x"), pairs)


def block_of(width):
    for size in (1024, 512, 384, 256, 128):
        if width % size == 0:
            return size
    return width


def start_tokens(tokens_ref, held, sems, block, chunk_of):
    width = tokens_ref.shape[1]
    chunk = width // NX
    for i in range(width // block):
        d, at = i * block // chunk, i * block % chunk
        source = pl.multiple_of(chunk_of(d) * chunk + at, block)
        pltpu.make_async_copy(
            tokens_ref.at[:, pl.ds(source, block)],
            held.at[:, pl.ds(i * block, block)],
            sems.at[i],
        ).start()


def wait_tokens(tokens_ref, held, sems, block, i):
    at = pl.multiple_of(i * block, block)
    pltpu.make_async_copy(
        tokens_ref.at[:, pl.ds(0, block)], held.at[:, pl.ds(at, block)], sems.at[i]
    ).wait()
    return held[:, pl.ds(at, block)]


def partial_kernel(place_ref, cot_ref, tokens_ref, *refs):
    own, other = refs[:NX], refs[NX : 2 * NX]
    held, rows_t, rows, sems = refs[2 * NX :]
    y, c, x = place_ref[0], place_ref[1], place_ref[2]
    chunk = tokens_ref.shape[1] // NX
    half = rows.shape[0] // 2
    unit = half // NY
    block = block_of(chunk)
    start_tokens(tokens_ref, held, sems, block, lambda d: lax.rem(x + d, NX))
    rows_t[...] = cot_ref[...].astype(f32).T.astype(bf16)
    for k, core in enumerate((c, 1 - c)):
        for e in range(NY):
            at = pl.multiple_of(core * half + lax.rem(y + e, NY) * unit, unit)
            rows[pl.ds(k * half + e * unit, unit), :] = rows_t[pl.ds(at, unit), :]

    def run(by_x, by_y):
        steps = chunk // block
        first_x = by_x is own
        for d in range(NX):

            @pl.loop(0, steps)
            def _(j):
                part = wait_tokens(tokens_ref, held, sems, block, d * steps + j)
                lanes = pl.ds(pl.multiple_of(j * block, block), block)
                terms = jnp.dot(rows[...], part, preferred_element_type=f32).astype(bf16)
                mine, theirs = terms[:half], terms[half:]
                for_x, for_y = (mine, theirs) if first_x else (theirs, mine)
                by_x[d][:, lanes] = for_x
                for e in range(NY):
                    by_y[e][d * unit : (d + 1) * unit, lanes] = for_y[e * unit : (e + 1) * unit]

    @pl.when(c == 0)
    def _():
        run(own, other)

    @pl.when(c == 1)
    def _():
        run(other, own)


VMEM_LIMIT = 48 * 2**20


def partial_terms(place, cotangent, tokens):
    count, width = tokens.shape
    cols = cotangent.shape[1]
    block = block_of(width // NX)
    return pl.pallas_call(
        partial_kernel,
        in_specs=[
            pl.BlockSpec(memory_space=pltpu.SMEM),
            pl.BlockSpec(memory_space=pltpu.VMEM),
            pl.BlockSpec(memory_space=pl.ANY),
        ],
        out_specs=[pl.BlockSpec(memory_space=pltpu.VMEM)] * (2 * NX),
        out_shape=[jax.ShapeDtypeStruct((cols // 2, width // NX), bf16)] * (2 * NX),
        scratch_shapes=[
            pltpu.VMEM((count, width), bf16),
            pltpu.VMEM((cols, count), bf16),
            pltpu.VMEM((cols, count), bf16),
            pltpu.SemaphoreType.DMA((width // block,)),
        ],
        compiler_params=pltpu.CompilerParams(vmem_limit_bytes=VMEM_LIMIT),
        cost_estimate=pl.CostEstimate(
            flops=2 * cols * count * width,
            bytes_accessed=2 * (count * width + cols * width + cols * count),
            transcendentals=0,
        ),
        name="partial_terms",
    )(place, cotangent, tokens)


def forward_kernel(place_ref, tokens_ref, *refs):
    own, other = refs[:NX], refs[NX : 2 * NX]
    out_ref, held, weight, total, sems = refs[2 * NX :]
    y, c, x = place_ref[0], place_ref[1], place_ref[2]
    width = tokens_ref.shape[1]
    chunk = width // NX
    half = weight.shape[0] // 2
    unit = half // NY
    block = block_of(chunk)
    steps = chunk // block
    start_tokens(tokens_ref, held, sems, block, lambda d: lax.rem(x + NX - d, NX))

    def whole(by_x, by_y, d):
        for e in range(NY):
            at = pl.multiple_of(lax.rem(y + NY - e, NY) * unit, unit)
            weight[pl.ds(at, unit), :] = by_x[d][e * unit : (e + 1) * unit, :]
            weight[pl.ds(half + at, unit), :] = by_y[e][d * unit : (d + 1) * unit, :]

    for d in range(NX):

        @pl.when(c == 0)
        def _():
            whole(own, other, d)

        @pl.when(c == 1)
        def _():
            whole(other, own, d)

        @pl.loop(0, steps)
        def _(j):
            part = wait_tokens(tokens_ref, held, sems, block, d * steps + j)
            lanes = pl.ds(pl.multiple_of(j * block, block), block)
            terms = lax.dot_general(
                part, weight[:, lanes], (((1,), (1,)), ((), ())), preferred_element_type=f32
            )
            if d == 0:
                total[...] = jnp.where(j == 0, terms, total[...] + terms)
            else:
                total[...] += terms

    out_ref[...] = (total[...] * width ** (-0.5)).astype(bf16)


def forward(place, tokens, own, other):
    count, width = tokens.shape
    cols = 2 * own[0].shape[0]
    block = block_of(width // NX)
    return pl.pallas_call(
        forward_kernel,
        in_specs=[pl.BlockSpec(memory_space=pltpu.SMEM), pl.BlockSpec(memory_space=pl.ANY)]
        + [pl.BlockSpec(memory_space=pltpu.VMEM)] * (2 * NX),
        out_specs=pl.BlockSpec(memory_space=pltpu.VMEM),
        out_shape=jax.ShapeDtypeStruct((count, cols), bf16),
        scratch_shapes=[
            pltpu.VMEM((count, width), bf16),
            pltpu.VMEM((cols, width // NX), bf16),
            pltpu.VMEM((count, cols), f32),
            pltpu.SemaphoreType.DMA((width // block,)),
        ],
        compiler_params=pltpu.CompilerParams(vmem_limit_bytes=VMEM_LIMIT),
        cost_estimate=pl.CostEstimate(
            flops=2 * cols * count * width,
            bytes_accessed=2 * (count * width + cols * width + cols * count),
            transcendentals=0,
        ),
        name="forward",
    )(place, tokens, *own, *other)


def add(*parts):
    total = parts[0].astype(f32)
    for part in parts[1:]:
        total = total + part.astype(f32)
    return total


def body(tokens, cotangent, master, first_moment, second_moment):
    y, c, x = lax.axis_index("y"), lax.axis_index("core"), lax.axis_index("x")
    place = jnp.stack([y, c, x]).astype(jnp.int32)
    rows, cols = master.shape
    count = rows * NX * NZ * cols
    unit = cols // (NC * NY)

    terms = partial_terms(place, cotangent, tokens)
    own, other = terms[:NX], terms[NX:]
    chip = {}
    for d in (2, 1, 3, 0):
        chip[d] = add(own[d], send(other[d], "core", 1)).astype(bf16)
    got = [routed(chip[d], d, True) for d in FAR_FIRST]
    line = add(chip[0], *got).astype(bf16)
    got = [routed(line[d * unit : (d + 1) * unit], d, False) for d in FAR_FIRST]
    plane = add(line[:unit], *got).astype(bf16)
    planes = lax.all_to_all(plane, "z", 1, 0, tiled=True).reshape(NZ, unit, rows)
    piece = jnp.sum(planes.astype(f32), 0).astype(bf16)

    grads = lax.all_to_all(jnp.tile(piece, (NC * NY, 1)), ("core", "y"), 0, 0, tiled=True)
    grads = grads.astype(f32)
    square = jnp.sum(grads * grads).reshape(1, 1)
    squares = lax.all_to_all(
        jnp.broadcast_to(square, (NX * NZ, 1)), ("x", "z"), 0, 0, tiled=True
    )
    total = jnp.sum(squares)
    master_new, first_new, second_new = apply_update(
        grads.T, master, first_moment, second_moment, total, count
    )

    at = c * (cols // 2) + y * unit
    weight = lax.dynamic_slice_in_dim(master_new, at, unit, 1).T.astype(bf16)
    plane = lax.all_to_all(jnp.tile(weight, (NZ, 1)), "z", 0, 1, tiled=True)
    line = jnp.concatenate([plane] + [routed(plane, d, False) for d in (1, 2, 3)], 0)
    own = [line] + [routed(line, d, True) for d in (1, 2, 3)]
    other = [send(part, "core", 1) for part in own]
    activations = forward(place, tokens, own, other)
    return (master_new, first_new, second_new, activations)


def solution(mesh):
    fine = Mesh(mesh.devices.reshape(NY, NC, NX, NZ), NAMES)
    by_token, by_row = P(NAMES, None), P(("x", "z"), None)
    return jax.shard_map(
        body,
        mesh=fine,
        in_specs=(by_token, by_token, by_row, by_row, by_row),
        out_specs=(by_row, by_row, by_row, by_token),
        check_vma=False,
    )
```

time: 489 us -> 158 us (0.32)
  waiting for transfers between devices: 388 us -> 59.2 us
  starting transfers between devices: 0.12 us -> 39.4 us
  blocking collectives: 61.7 us -> 27.8 us
  matrix products: 20 us -> 0 us
  Pallas kernels: 0 us -> 17.6 us
  between operations: 14.5 us -> 1.74 us
  local copies, waits for them, and re-layouts: 0.87 us -> 8.29 us
    reduce_scatter x1 -> x0, waiting for transfers between devices: 225 us -> none  [body(): lax.psum_scatter(row_terms(tokens, cotangent).astype(jnp.bfloat16), 'shar...]
    all_gather x1 -> x0, waiting for transfers between devices: 95.7 us -> none  [body(): lax.all_gather(weight, 'shard', axis=0, tiled=True)]
    psum x1 -> x0, waiting for transfers between devices: 66.9 us -> none  [body(): grads = lax.psum(grads.astype(jnp.bfloat16), 'rep').astype(jnp.float32)]
    psum x1 -> x0, blocking collectives: 61.7 us -> none  [body(): total = lax.psum(jnp.sum(grads * grads), 'shard')]
    ppermute x0 -> x20, waiting for transfers between devices: none -> 45.3 us  [the longest x12 43.6 us: routed(): return lax.ppermute(value, ('y', 'core', 'x'), pairs)]
    ppermute x0 -> x20, starting transfers between devices: none -> 27.9 us  [the longest x8 14.7 us: send(): return lax.ppermute(value, axis, [(i, (i + step) % n) for i in range(n)])]
    all_to_all x0 -> x2, blocking collectives: none -> 27.8 us  [the longest x1 16.8 us: body(): lax.all_to_all(plane, 'z', 1, 0, tiled=True).reshape(NZ, unit, rows)]
    dot_general x2 -> x0, matrix products: 20 us -> none  [the longest x1 10.3 us: row_terms(): lax.dot_general(source, cotangent, (((0,), (0,)), ((), ())), preferred_el...]
  transfers between devices with their start and end apart: 3 -> 22, of which waited for: 3 -> 10; matrix products, arithmetic and copies ran while one was open for 0% -> 4% of each run, Pallas kernels for 0% -> 0%
where the time goes in v2:
time: 158 us
  waiting for transfers between devices  59.2 us (37%)
  starting transfers between devices  39.4 us (25%)
  blocking collectives  27.8 us (18%)
  Pallas kernels  17.6 us (11%)
  local copies, waits for them, and re-layouts  8.29 us (5%)
  other arithmetic  3.94 us (2%)
  between operations  1.74 us (1%)
    ppermute x12, waiting for transfers between devices, routed(): return lax.ppermute(value, ('y', 'core', 'x'), pairs)  43.6 us
    all_to_all x1, blocking collectives, body(): lax.all_to_all(plane, 'z', 1, 0, tiled=True).reshape(NZ, unit, rows)  16.8 us
    ppermute x8, starting transfers between devices, send(): return lax.ppermute(value, axis, [(i, (i + step) % n) for i in range(n)])  14.7 us
    ppermute x12, starting transfers between devices, routed(): return lax.ppermute(value, ('y', 'core', 'x'), pairs)  13.2 us
    all_to_all x1, blocking collectives, body(): plane = lax.all_to_all(jnp.tile(weight, (NZ, 1)), 'z', 0, 1, tiled=True)  11 us
    pallas_call x1, Pallas kernels, forward(): pl.pallas_call(forward_kernel, in_specs=[pl.BlockSpec(memory_space=pltpu....  9.56 us
    all_to_all x1, waiting for transfers between devices, body(): lax.all_to_all(jnp.broadcast_to(square, (NX * NZ, 1)), ('x', 'z'), 0, 0,...  8.56 us
    pallas_call x1, Pallas kernels, partial_terms(): pl.pallas_call(partial_kernel, in_specs=[pl.BlockSpec(memory_space=pltpu....  8.05 us
  transfers between devices with their start and end apart: 22, of which 10 were waited for; matrix products, arithmetic and copies ran while one was open for 4% of the time, Pallas kernels for 0%

profile of v2, /device:TPU:1, one launch (start us, length us, event | category | flops | bytes accessed | tf_op | source)
XLA Modules:
  0.0 158.0 jit_solution(14053820827599747806)
XLA Ops:
  0.7 0.9 copy-done
  1.7 8.1 %partial_terms.1 = (bf16[128,3072]{1,0:T(8,128)(2,1)S(1)}, bf16[128,3072]{1,0:T(8,128)(2,1)S(1)}, bf16[128,3072]{1,0:T(8,128)(2,1)S(1)}, bf16[128,3072]{1,0:T(8,...) custom-call(s32[3]{0:T(128)S(1)} %pad_add_fusion.place_ref, ...), custom_call_target="tpu_custom_call" | custom-call | flops 2818572288 | bytes 17530880 | tf_op jit(solution)/shard_map/partial_terms/pallas_call | solution.py:133
  9.7 3.3 %collective-permute-start.5 = (bf16[128,3072]{1,0:T(8,128)(2,1)}, bf16[128,3072]{1,0:T(8,128)(2,1)S(1)}, u32[]{:S(2)}, u32[]{:S(2)}) collective-permute-start(bf16[128,3072]{1,0:T(8,128)(2,1)} %get-tuple-element.19), channel_id=1, source_target_pairs={{0,32},{32,0},{1,33},{33,1},{2,34},{34,2},{3,35},{35,3},{4,36},{36... | collective-permute-start | bytes 2359304 | tf_op jit(solution)/shard_map/ppermute | solution.py:41
  13.7 1.6 %collective-permute-done.5 = bf16[128,3072]{1,0:T(8,128)(2,1)S(1)} collective-permute-done((bf16[128,3072]{1,0:T(8,128)(2,1)}, bf16[128,3072]{1,0:T(8,128)(2,1)S(1)}, u32[]{:S(2)}, u32[]{:S(2)}) %collective-permute-start.5) | collective-permute-done | bytes 786464 | tf_op jit(solution)/shard_map/ppermute | solution.py:41
  15.5 1.1 collective-permute-start.6
  17.5 1.3 collective-permute-start.2
  18.8 7.9 %collective-permute-done.6 = bf16[128,3072]{1,0:T(8,128)(2,1)S(1)} collective-permute-done((bf16[128,3072]{1,0:T(8,128)(2,1)S(1)}, bf16[128,3072]{1,0:T(8,128)(2,1)S(1)}, u32[]{:S(2)}, u32[]{:S(2)}) %collective-permute-start.6) | collective-permute-done | bytes 786464 | tf_op jit(solution)/shard_map/ppermute | solution.py:55
  26.7 10.9 %collective-permute-done.4 = bf16[128,3072]{1,0:T(8,128)(2,1)S(1)} collective-permute-done((bf16[128,3072]{1,0:T(8,128)(2,1)S(1)}, bf16[128,3072]{1,0:T(8,128)(2,1)S(1)}, u32[]{:S(2)}, u32[]{:S(2)}) %collective-permute-start.4) | collective-permute-done | bytes 786464 | tf_op jit(solution)/shard_map/ppermute | solution.py:55
  38.3 2.3 %collective-permute-start.9 = (bf16[32,3072]{1,0:T(8,128)(2,1)S(1)}, bf16[32,3072]{1,0:T(8,128)(2,1)S(1)}, u32[]{:S(2)}, u32[]{:S(2)}) collective-permute-start(bf16[32,3072]{1,0:T(8,128)(2,1)S(1)} %get-tuple-element.40), channel_id=1, source_target_pairs={{0,192},{8,200},{16,208},{24,216},{32,56},{40,32},{48,40},{56,48},... | collective-permute-start | bytes 589832 | tf_op jit(solution)/shard_map/ppermute | solution.py:55
  40.6 1.7 %collective-permute-start.7 = (bf16[32,3072]{1,0:T(8,128)(2,1)S(1)}, bf16[32,3072]{1,0:T(8,128)(2,1)S(1)}, u32[]{:S(2)}, u32[]{:S(2)}) collective-permute-start(bf16[32,3072]{1,0:T(8,128)(2,1)S(1)} %get-tuple-element.39), channel_id=1, source_target_pairs={{0,128},{8,136},{16,144},{24,152},{32,48},{40,56},{48,32},{56,40},... | collective-permute-start | bytes 589832 | tf_op jit(solution)/shard_map/ppermute | solution.py:55
  42.3 0.9 collective-permute-done.9
  43.2 5.5 %collective-permute-done.8 = bf16[32,3072]{1,0:T(8,128)(2,1)S(1)} collective-permute-done((bf16[32,3072]{1,0:T(8,128)(2,1)S(1)}, bf16[32,3072]{1,0:T(8,128)(2,1)S(1)}, u32[]{:S(2)}, u32[]{:S(2)}) %collective-permute-start.8) | collective-permute-done | bytes 196640 | tf_op jit(solution)/shard_map/ppermute | solution.py:55
  48.9 16.8 %all_to_all.41 = bf16[32,8,384]{2,0,1:T(8,128)(2,1)S(1)} all-to-all(bf16[32,8,384]{2,0,1:T(8,128)(2,1)S(1)} %bitcast.25), channel_id=1, replica_groups=mesh['y'=4,'core'=2,'x'=4,'z'=8] {'z'}, dimensions={1} | all-to-all | bytes 393216 | tf_op jit(solution)/shard_map/all_to_all | solution.py:250
  66.4 7.7 %all-to-all-start.1 = ((bf16[8,32,384]{2,1,0:T(8,128)(2,1)}), bf16[8,32,384]{2,1,0:T(8,128)(2,1)S(1)}, u32[]{:S(2)}, u32[]{:S(2)}) async-start(bf16[8,32,384]{2,1,0:T(8,128)(2,1)} %tile.4), calls=%async_computation.1 | async-start | bytes 393216 | tf_op jit(solution)/shard_map/all_to_all | solution.py:253
  74.6 5.3 %all-to-all-done.1 = bf16[8,32,384]{2,1,0:T(8,128)(2,1)S(1)} async-done(((bf16[8,32,384]{2,1,0:T(8,128)(2,1)}), bf16[8,32,384]{2,1,0:T(8,128)(2,1)S(1)}, u32[]{:S(2)}, u32[]{:S(2)}) %all-to-all-start.1) | async-done | bytes 196640 | tf_op jit(solution)/shard_map/all_to_all | solution.py:253
  80.6 1.3 broadcast_in_dim.2
  81.9 3.8 %all-to-all-start.2 = ((f32[32,1,1]{2,1,0:T(1,128)}), f32[32,1,1]{2,1,0:T(1,128)S(1)}, u32[]{:S(2)}, u32[]{:S(2)}) async-start(f32[32,1,1]{2,1,0:T(1,128)} %broadcast_in_dim.2), calls=%async_computation.2 | async-start | bytes 32768 | tf_op jit(solution)/shard_map/all_to_all | solution.py:256
  85.7 8.6 %all-to-all-done.2 = f32[32,1,1]{2,1,0:T(1,128)S(1)} async-done(((f32[32,1,1]{2,1,0:T(1,128)}), f32[32,1,1]{2,1,0:T(1,128)S(1)}, u32[]{:S(2)}, u32[]{:S(2)}) %all-to-all-start.2) | async-done | bytes 160 | tf_op jit(solution)/shard_map/all_to_all | solution.py:256
  95.7 1.2 multiply_subtract_fusion
  96.9 11.0 %all_to_all.42 = bf16[8,32,384]{2,1,0:T(8,128)(2,1)S(1)} all-to-all(bf16[8,32,384]{2,1,0:T(8,128)(2,1)S(1)} %tile.5), channel_id=1, replica_groups=mesh['y'=4,'core'=2,'x'=4,'z'=8] {'z'}, dimensions={0} | all-to-all | bytes 393216 | tf_op jit(solution)/shard_map/all_to_all | solution.py:266
  108.4 1.7 %collective-permute-start.11 = (bf16[32,3072]{1,0:T(8,128)(2,1)S(1)}, bf16[32,3072]{1,0:T(8,128)(2,1)S(1)}, u32[]{:S(2)}, u32[]{:S(2)}) collective-permute-start(bf16[32,3072]{1,0:T(8,128)(2,1)S(1)} %bitcast.22), channel_id=1, source_target_pairs={{0,128},{8,136},{16,144},{24,152},{32,48},{40,56},{48,32},{56,40},... | collective-permute-start | bytes 589832 | tf_op jit(solution)/shard_map/ppermute | solution.py:55
  110.0 1.0 collective-permute-start.12
  111.1 5.1 %collective-permute-done.10 = bf16[32,3072]{1,0:T(8,128)(2,1)S(1)} collective-permute-done((bf16[32,3072]{1,0:T(8,128)(2,1)S(1)}, bf16[32,3072]{1,0:T(8,128)(2,1)S(1)}, u32[]{:S(2)}, u32[]{:S(2)}) %collective-permute-start.10) | collective-permute-done | bytes 196640 | tf_op jit(solution)/shard_map/ppermute | solution.py:55
  117.4 1.4 collective-permute-start.14
  118.9 1.1 collective-permute-start.15
  119.9 4.9 %collective-permute-start.16 = (bf16[128,3072]{1,0:T(8,128)(2,1)S(1)}, bf16[128,3072]{1,0:T(8,128)(2,1)}, u32[]{:S(2)}, u32[]{:S(2)}) collective-permute-start(bf16[128,3072]{1,0:T(8,128)(2,1)S(1)} %constant_dynamic-update-slice_fusion.refs_0_), channel_id=1, source_target_pairs={{0,32},{32,0},{1,33},{33,1},{2,34},{34,2},{3,35},{35,3},{4,36},{36... | collective-permute-start | bytes 2359304 | tf_op jit(solution)/shard_map/ppermute | solution.py:41
  124.9 12.8 %collective-permute-done.13.refs_1_ = bf16[128,3072]{1,0:T(8,128)(2,1)S(1)} collective-permute-done((bf16[128,3072]{1,0:T(8,128)(2,1)S(1)}, bf16[128,3072]{1,0:T(8,128)(2,1)S(1)}, u32[]{:S(2)}, u32[]{:S(2)}) %collective-permute-start.13) | collective-permute-done | bytes 786464 | tf_op jit(solution)/shard_map/ppermute | solution.py:55
  137.6 5.0 %collective-permute-start.17 = (bf16[128,3072]{1,0:T(8,128)(2,1)S(1)}, bf16[128,3072]{1,0:T(8,128)(2,1)}, u32[]{:S(2)}, u32[]{:S(2)}) collective-permute-start(bf16[128,3072]{1,0:T(8,128)(2,1)S(1)} %collective-permute-done.13.refs_1_), channel_id=1, source_target_pairs={{0,32},{32,0},{1,33},{33,1},{2,34},{34,2},{3,35},{35,3},{4,36},{36... | collective-permute-start | bytes 2359304 | tf_op jit(solution)/shard_map/ppermute | solution.py:41
  143.5 0.9 copy.42
  144.4 1.9 %copy.43 = f32[384,256]{1,0:T(8,128)} copy(f32[384,256]{0,1:T(8,128)} %get-tuple-element.37) | data formatting | bytes 786432
  146.3 1.9 %copy.44 = f32[384,256]{1,0:T(8,128)} copy(f32[384,256]{0,1:T(8,128)} %get-tuple-element.38) | data formatting | bytes 786432
  148.3 9.6 %forward.1 = bf16[448,256]{1,0:T(8,128)(2,1)} custom-call(s32[3]{0:T(128)S(1)} %pad_add_fusion.place_ref, bf16[448,12288]{1,0:T(8,128)(2,1)} %tokens_ref.3, bf16[128,3072]{1,0:T(8,128)(2,1)S(1)} %constant_dynamic-update-slice_fusion.refs_0_, bf16[128,3072]{1,0:T(8,128)(2,1)S(1)} %collective-permute-done.13.refs_1_, ...), custom_call_target="tpu_custom_call" | custom-call | flops 2818572288 | bytes 17530880 | tf_op jit(solution)/shard_map/forward/pallas_call | solution.py:205
  (52 shorter events, 7.9 us)
Async XLA Ops:
  0.7 0.9 copy-start
  9.7 5.6 %collective-permute-start.5 = (bf16[128,3072]{1,0:T(8,128)(2,1)}, bf16[128,3072]{1,0:T(8,128)(2,1)S(1)}, u32[]{:S(2)}, u32[]{:S(2)}) collective-permute-start(bf16[128,3072]{1,0:T(8,128)(2,1)} %get-tuple-element.19), channel_id=1, source_target_pairs={{0,32},{32,0},{1,33},{33,1},{2,34},{34,2},{3,35},{35,3},{4,36},{36... | collective-permute-start | bytes 2359304 | tf_op jit(solution)/shard_map/ppermute | solution.py:41
  13.0 3.5 %collective-permute-start.3 = (bf16[128,3072]{1,0:T(8,128)(2,1)S(1)}, bf16[128,3072]{1,0:T(8,128)(2,1)S(1)}, u32[]{:S(2)}, u32[]{:S(2)}) collective-permute-start(bf16[128,3072]{1,0:T(8,128)(2,1)S(1)} %get-tuple-element.17), channel_id=1, source_target_pairs={{0,32},{32,0},{1,33},{33,1},{2,34},{34,2},{3,35},{35,3},{4,36},{36... | collective-permute-start | bytes 2359304 | tf_op jit(solution)/shard_map/ppermute | solution.py:41
  13.1 4.2 %collective-permute-start.1 = (bf16[128,3072]{1,0:T(8,128)(2,1)S(1)}, bf16[128,3072]{1,0:T(8,128)(2,1)S(1)}, u32[]{:S(2)}, u32[]{:S(2)}) collective-permute-start(bf16[128,3072]{1,0:T(8,128)(2,1)S(1)} %get-tuple-element.15), channel_id=1, source_target_pairs={{0,32},{32,0},{1,33},{33,1},{2,34},{34,2},{3,35},{35,3},{4,36},{36... | collective-permute-start | bytes 2359304 | tf_op jit(solution)/shard_map/ppermute | solution.py:41
  13.6 5.3 %collective-permute-start = (bf16[128,3072]{1,0:T(8,128)(2,1)S(1)}, bf16[128,3072]{1,0:T(8,128)(2,1)S(1)}, u32[]{:S(2)}, u32[]{:S(2)}) collective-permute-start(bf16[128,3072]{1,0:T(8,128)(2,1)S(1)} %get-tuple-element.13), channel_id=1, source_target_pairs={{0,32},{32,0},{1,33},{33,1},{2,34},{34,2},{3,35},{35,3},{4,36},{36... | collective-permute-start | bytes 2359304 | tf_op jit(solution)/shard_map/ppermute | solution.py:41
  15.5 11.2 %collective-permute-start.6 = (bf16[128,3072]{1,0:T(8,128)(2,1)S(1)}, bf16[128,3072]{1,0:T(8,128)(2,1)S(1)}, u32[]{:S(2)}, u32[]{:S(2)}) collective-permute-start(bf16[128,3072]{1,0:T(8,128)(2,1)S(1)} %add_convert_fusion.1), channel_id=1, source_target_pairs={{0,24},{8,0},{16,8},{24,16},{32,224},{40,232},{48,240},{56,248},{6... | collective-permute-start | bytes 2359304 | tf_op jit(solution)/shard_map/ppermute | solution.py:55
  16.8 20.8 %collective-permute-start.4 = (bf16[128,3072]{1,0:T(8,128)(2,1)S(1)}, bf16[128,3072]{1,0:T(8,128)(2,1)S(1)}, u32[]{:S(2)}, u32[]{:S(2)}) collective-permute-start(bf16[128,3072]{1,0:T(8,128)(2,1)S(1)} %add_convert_fusion.2), channel_id=1, source_target_pairs={{0,8},{8,16},{16,24},{24,0},{32,96},{40,104},{48,112},{56,120},{64... | collective-permute-start | bytes 2359304 | tf_op jit(solution)/shard_map/ppermute | solution.py:55
  17.5 20.1 %collective-permute-start.2 = (bf16[128,3072]{1,0:T(8,128)(2,1)S(1)}, bf16[128,3072]{1,0:T(8,128)(2,1)S(1)}, u32[]{:S(2)}, u32[]{:S(2)}) collective-permute-start(bf16[128,3072]{1,0:T(8,128)(2,1)S(1)} %add_convert_fusion.3), channel_id=1, source_target_pairs={{0,16},{8,24},{16,0},{24,8},{32,160},{40,168},{48,176},{56,184},{6... | collective-permute-start | bytes 2359304 | tf_op jit(solution)/shard_map/ppermute | solution.py:55
  38.3 35.7 %copy-start.1 = (f32[384,256]{1,0:T(8,128)S(1)}, f32[384,256]{1,0:T(8,128)}, u32[]{:S(2)}) copy-start(f32[384,256]{1,0:T(8,128)} %param.7) | copy-start | bytes 1179652
  38.3 4.9 %collective-permute-start.9 = (bf16[32,3072]{1,0:T(8,128)(2,1)S(1)}, bf16[32,3072]{1,0:T(8,128)(2,1)S(1)}, u32[]{:S(2)}, u32[]{:S(2)}) collective-permute-start(bf16[32,3072]{1,0:T(8,128)(2,1)S(1)} %get-tuple-element.40), channel_id=1, source_target_pairs={{0,192},{8,200},{16,208},{24,216},{32,56},{40,32},{48,40},{56,48},... | collective-permute-start | bytes 589832 | tf_op jit(solution)/shard_map/ppermute | solution.py:55
  40.6 8.1 %collective-permute-start.8 = (bf16[32,3072]{1,0:T(8,128)(2,1)S(1)}, bf16[32,3072]{1,0:T(8,128)(2,1)S(1)}, u32[]{:S(2)}, u32[]{:S(2)}) collective-permute-start(bf16[32,3072]{1,0:T(8,128)(2,1)S(1)} %get-tuple-element.41), channel_id=1, source_target_pairs={{0,64},{8,72},{16,80},{24,88},{32,40},{40,48},{48,56},{56,32},{64,... | collective-permute-start | bytes 589832 | tf_op jit(solution)/shard_map/ppermute | solution.py:55
  40.6 33.6 %copy-start.2 = (f32[384,256]{1,0:T(8,128)S(1)}, f32[384,256]{1,0:T(8,128)}, u32[]{:S(2)}) copy-start(f32[384,256]{1,0:T(8,128)} %param.8) | copy-start | bytes 1179652
  40.6 8.1 %collective-permute-start.7 = (bf16[32,3072]{1,0:T(8,128)(2,1)S(1)}, bf16[32,3072]{1,0:T(8,128)(2,1)S(1)}, u32[]{:S(2)}, u32[]{:S(2)}) collective-permute-start(bf16[32,3072]{1,0:T(8,128)(2,1)S(1)} %get-tuple-element.39), channel_id=1, source_target_pairs={{0,128},{8,136},{16,144},{24,152},{32,48},{40,56},{48,32},{56,40},... | collective-permute-start | bytes 589832 | tf_op jit(solution)/shard_map/ppermute | solution.py:55
  48.8 25.5 %copy-start.3 = (f32[384,256]{1,0:T(8,128)S(1)}, f32[384,256]{1,0:T(8,128)}, u32[]{:S(2)}) copy-start(f32[384,256]{1,0:T(8,128)} %param.9) | copy-start | bytes 1179652
  66.4 13.6 %all-to-all-start.1 = ((bf16[8,32,384]{2,1,0:T(8,128)(2,1)}), bf16[8,32,384]{2,1,0:T(8,128)(2,1)S(1)}, u32[]{:S(2)}, u32[]{:S(2)}) async-start(bf16[8,32,384]{2,1,0:T(8,128)(2,1)} %tile.4), calls=%async_computation.1 | async-start | bytes 393216 | tf_op jit(solution)/shard_map/all_to_all | solution.py:253
  81.9 12.4 %all-to-all-start.2 = ((f32[32,1,1]{2,1,0:T(1,128)}), f32[32,1,1]{2,1,0:T(1,128)S(1)}, u32[]{:S(2)}, u32[]{:S(2)}) async-start(f32[32,1,1]{2,1,0:T(1,128)} %broadcast_in_dim.2), calls=%async_computation.2 | async-start | bytes 32768 | tf_op jit(solution)/shard_map/all_to_all | solution.py:256
  107.9 8.2 %collective-permute-start.10 = (bf16[32,3072]{1,0:T(8,128)(2,1)S(1)}, bf16[32,3072]{1,0:T(8,128)(2,1)S(1)}, u32[]{:S(2)}, u32[]{:S(2)}) collective-permute-start(bf16[32,3072]{1,0:T(8,128)(2,1)S(1)} %bitcast.21), channel_id=1, source_target_pairs={{0,64},{8,72},{16,80},{24,88},{32,40},{40,48},{48,56},{56,32},{64,... | collective-permute-start | bytes 589832 | tf_op jit(solution)/shard_map/ppermute | solution.py:55
  108.4 7.8 %collective-permute-start.11 = (bf16[32,3072]{1,0:T(8,128)(2,1)S(1)}, bf16[32,3072]{1,0:T(8,128)(2,1)S(1)}, u32[]{:S(2)}, u32[]{:S(2)}) collective-permute-start(bf16[32,3072]{1,0:T(8,128)(2,1)S(1)} %bitcast.22), channel_id=1, source_target_pairs={{0,128},{8,136},{16,144},{24,152},{32,48},{40,56},{48,32},{56,40},... | collective-permute-start | bytes 589832 | tf_op jit(solution)/shard_map/ppermute | solution.py:55
  110.0 6.7 %collective-permute-start.12 = (bf16[32,3072]{1,0:T(8,128)(2,1)S(1)}, bf16[32,3072]{1,0:T(8,128)(2,1)S(1)}, u32[]{:S(2)}, u32[]{:S(2)}) collective-permute-start(bf16[32,3072]{1,0:T(8,128)(2,1)S(1)} %bitcast.23), channel_id=1, source_target_pairs={{0,192},{8,200},{16,208},{24,216},{32,56},{40,32},{48,40},{56,48},... | collective-permute-start | bytes 589832 | tf_op jit(solution)/shard_map/ppermute | solution.py:55
  116.8 20.8 %collective-permute-start.13 = (bf16[128,3072]{1,0:T(8,128)(2,1)S(1)}, bf16[128,3072]{1,0:T(8,128)(2,1)S(1)}, u32[]{:S(2)}, u32[]{:S(2)}) collective-permute-start(bf16[128,3072]{1,0:T(8,128)(2,1)S(1)} %constant_dynamic-update-slice_fusion.refs_0_), channel_id=1, source_target_pairs={{0,8},{8,16},{16,24},{24,0},{32,96},{40,104},{48,112},{56,120},{64... | collective-permute-start | bytes 2359304 | tf_op jit(solution)/shard_map/ppermute | solution.py:55
  117.4 25.2 %collective-permute-start.14 = (bf16[128,3072]{1,0:T(8,128)(2,1)S(1)}, bf16[128,3072]{1,0:T(8,128)(2,1)S(1)}, u32[]{:S(2)}, u32[]{:S(2)}) collective-permute-start(bf16[128,3072]{1,0:T(8,128)(2,1)S(1)} %constant_dynamic-update-slice_fusion.refs_0_), channel_id=1, source_target_pairs={{0,16},{8,24},{16,0},{24,8},{32,160},{40,168},{48,176},{56,184},{6... | collective-permute-start | bytes 2359304 | tf_op jit(solution)/shard_map/ppermute | solution.py:55
  118.9 23.8 %collective-permute-start.15 = (bf16[128,3072]{1,0:T(8,128)(2,1)S(1)}, bf16[128,3072]{1,0:T(8,128)(2,1)S(1)}, u32[]{:S(2)}, u32[]{:S(2)}) collective-permute-start(bf16[128,3072]{1,0:T(8,128)(2,1)S(1)} %constant_dynamic-update-slice_fusion.refs_0_), channel_id=1, source_target_pairs={{0,24},{8,0},{16,8},{24,16},{32,224},{40,232},{48,240},{56,248},{6... | collective-permute-start | bytes 2359304 | tf_op jit(solution)/shard_map/ppermute | solution.py:55
  119.9 28.3 %collective-permute-start.16 = (bf16[128,3072]{1,0:T(8,128)(2,1)S(1)}, bf16[128,3072]{1,0:T(8,128)(2,1)}, u32[]{:S(2)}, u32[]{:S(2)}) collective-permute-start(bf16[128,3072]{1,0:T(8,128)(2,1)S(1)} %constant_dynamic-update-slice_fusion.refs_0_), channel_id=1, source_target_pairs={{0,32},{32,0},{1,33},{33,1},{2,34},{34,2},{3,35},{35,3},{4,36},{36... | collective-permute-start | bytes 2359304 | tf_op jit(solution)/shard_map/ppermute | solution.py:41
  137.6 10.6 %collective-permute-start.17 = (bf16[128,3072]{1,0:T(8,128)(2,1)S(1)}, bf16[128,3072]{1,0:T(8,128)(2,1)}, u32[]{:S(2)}, u32[]{:S(2)}) collective-permute-start(bf16[128,3072]{1,0:T(8,128)(2,1)S(1)} %collective-permute-done.13.refs_1_), channel_id=1, source_target_pairs={{0,32},{32,0},{1,33},{33,1},{2,34},{34,2},{3,35},{35,3},{4,36},{36... | collective-permute-start | bytes 2359304 | tf_op jit(solution)/shard_map/ppermute | solution.py:41
  142.6 5.6 %collective-permute-start.18 = (bf16[128,3072]{1,0:T(8,128)(2,1)S(1)}, bf16[128,3072]{1,0:T(8,128)(2,1)}, u32[]{:S(2)}, u32[]{:S(2)}) collective-permute-start(bf16[128,3072]{1,0:T(8,128)(2,1)S(1)} %collective-permute-done.14.refs_2_), channel_id=1, source_target_pairs={{0,32},{32,0},{1,33},{33,1},{2,34},{34,2},{3,35},{35,3},{4,36},{36... | collective-permute-start | bytes 2359304 | tf_op jit(solution)/shard_map/ppermute | solution.py:41
  142.6 5.6 %collective-permute-start.19 = (bf16[128,3072]{1,0:T(8,128)(2,1)S(1)}, bf16[128,3072]{1,0:T(8,128)(2,1)}, u32[]{:S(2)}, u32[]{:S(2)}) collective-permute-start(bf16[128,3072]{1,0:T(8,128)(2,1)S(1)} %collective-permute-done.15.refs_3_), channel_id=1, source_target_pairs={{0,32},{32,0},{1,33},{33,1},{2,34},{34,2},{3,35},{35,3},{4,36},{36... | collective-permute-start | bytes 2359304 | tf_op jit(solution)/shard_map/ppermute | solution.py:41

commit v3 on v0

v3 whole, which is shorter than its diff:
```python
import functools

import jax
import jax.numpy as jnp
from jax import lax
from jax.experimental import pallas as pl
from jax.experimental.pallas import tpu as pltpu
from jax.sharding import Mesh, PartitionSpec as P

STEP = 10

beta_first = 0.9
beta_second = 0.95
learn_rate = 0.02
decay_rate = 0.1
epsilon = 1e-08

NY, NC, NX, NZ = 4, 2, 4, 8
SIZE = {"y": NY, "core": NC, "x": NX, "z": NZ}
NAMES = ("y", "core", "x", "z")
f32 = jnp.float32
bf16 = jnp.bfloat16


def apply_update(grads, master, first, second, total, count):
    rms_value = jnp.sqrt(total / count)
    factor = 1.0 / jnp.maximum(rms_value, 1.0)
    clipped = grads * factor
    first_new = beta_first * first + (1.0 - beta_first) * clipped
    second_new = beta_second * second + (1.0 - beta_second) * clipped * clipped
    first_hat = first_new / (1.0 - beta_first**STEP)
    second_hat = second_new / (1.0 - beta_second**STEP)
    master_new = master - learn_rate * (
        first_hat / (jnp.sqrt(second_hat) + epsilon) + decay_rate * master
    )
    return (master_new, first_new, second_new)


def send(value, axis, step):
    n = SIZE[axis]
    return lax.ppermute(value, axis, [(i, (i + step) % n) for i in range(n)])


FAR_FIRST = (2, 1, 3)


def routed(value, step, first):
    pairs = []
    for y in range(NY):
        for c in range(NC):
            for x in range(NX):
                along_x = (c == 0) == first
                to_y, to_x = (y, (x + step) % NX) if along_x else ((y + step) % NY, x)
                pairs.append(((y * NC + c) * NX + x, (to_y * NC + c) * NX + to_x))
    return lax.ppermute(value, ("y", "core", "x"), pairs)


VMEM_LIMIT = 24 * 2**20


def in_hbm(value):
    return pltpu.with_memory_space_constraint(value, pltpu.HBM)


def in_vmem(count):
    return [pl.BlockSpec(memory_space=pltpu.VMEM)] * count


def kernel_call(body, name, in_specs, out_shape, scratch=(), flops=0, moved=0):
    return pl.pallas_call(
        body,
        in_specs=in_specs,
        out_specs=in_vmem(len(out_shape)),
        out_shape=out_shape,
        scratch_shapes=list(scratch),
        compiler_params=pltpu.CompilerParams(vmem_limit_bytes=VMEM_LIMIT),
        cost_estimate=pl.CostEstimate(flops=flops, bytes_accessed=moved, transcendentals=0),
        name=name,
    )


def partial_kernel(place_ref, cot_ref, tokens_ref, *refs):
    own, other = refs[:NX], refs[NX : 2 * NX]
    held, cot, rows_t, rows, sems = refs[2 * NX :]
    y, c, x = place_ref[0], place_ref[1], place_ref[2]
    chunk = tokens_ref.shape[1] // NX
    half = rows.shape[0] // 2
    unit = half // NY
    cot_copy = pltpu.make_async_copy(cot_ref, cot, sems.at[NX])
    cot_copy.start()
    copies = []
    for d in range(NX):
        source = pl.multiple_of(lax.rem(x + d, NX) * chunk, chunk)
        copies.append(
            pltpu.make_async_copy(
                tokens_ref.at[:, pl.ds(source, chunk)],
                held.at[:, pl.ds(d * chunk, chunk)],
                sems.at[d],
            )
        )
        copies[-1].start()
    cot_copy.wait()
    rows_t[...] = cot[...].astype(f32).T.astype(bf16)
    for k, core in enumerate((c, 1 - c)):
        for e in range(NY):
            at = pl.multiple_of(core * half + lax.rem(y + e, NY) * unit, unit)
            rows[pl.ds(k * half + e * unit, unit), :] = rows_t[pl.ds(at, unit), :]

    for d in range(NX):
        copies[d].wait()

        def run(by_x, by_y):
            terms = jnp.dot(
                rows[...], held[:, d * chunk : (d + 1) * chunk], preferred_element_type=f32
            ).astype(bf16)
            mine, theirs = terms[:half], terms[half:]
            for_x, for_y = (mine, theirs) if by_x is own else (theirs, mine)
            by_x[d][...] = for_x
            for e in range(NY):
                by_y[e][d * unit : (d + 1) * unit, :] = for_y[e * unit : (e + 1) * unit]

        @pl.when(c == 0)
        def _():
            run(own, other)

        @pl.when(c == 1)
        def _():
            run(other, own)


def partial_terms(place, cotangent, tokens):
    count, width = tokens.shape
    cols = cotangent.shape[1]
    part = jax.ShapeDtypeStruct((cols // 2, width // NX), bf16)
    out = kernel_call(
        partial_kernel,
        "partial_terms",
        [
            pl.BlockSpec(memory_space=pltpu.SMEM),
            pl.BlockSpec(memory_space=pltpu.HBM),
            pl.BlockSpec(memory_space=pltpu.HBM),
        ],
        [part] * (2 * NX) + [jax.ShapeDtypeStruct((count, width), bf16)],
        [
            pltpu.VMEM((count, cols), bf16),
            pltpu.VMEM((cols, count), bf16),
            pltpu.VMEM((cols, count), bf16),
            pltpu.SemaphoreType.DMA((NX + 1,)),
        ],
        2 * cols * count * width,
        2 * (count * width + cols * width + cols * count),
    )(place, in_hbm(cotangent), in_hbm(tokens))
    return out[:NX], out[NX : 2 * NX], out[2 * NX]


def forward_kernel(place_ref, held, *refs):
    own, other = refs[:NX], refs[NX : 2 * NX]
    out_ref, weight, total = refs[2 * NX :]
    y, c = place_ref[0], place_ref[1]
    width = held.shape[1]
    chunk = width // NX
    half = weight.shape[1] // 2
    unit = half // NY

    def run(by_x, by_y):
        for d in range(NX):
            for e in range(NY):
                at = pl.multiple_of(lax.rem(y + NY - e, NY) * unit, unit)
                weight[d, pl.ds(at, unit), :] = by_x[d][e * unit : (e + 1) * unit, :]
                weight[d, pl.ds(half + at, unit), :] = by_y[e][d * unit : (d + 1) * unit, :]
            back = (NX - d) % NX
            terms = lax.dot_general(
                held[:, back * chunk : (back + 1) * chunk],
                weight[d],
                (((1,), (1,)), ((), ())),
                preferred_element_type=f32,
            )
            if d == 0:
                total[...] = terms
            else:
                total[...] += terms

    @pl.when(c == 0)
    def _():
        run(own, other)

    @pl.when(c == 1)
    def _():
        run(other, own)

    out_ref[...] = (total[...] * width ** (-0.5)).astype(bf16)


def forward(place, held, own, other):
    count, width = held.shape
    cols = 2 * own[0].shape[0]
    return kernel_call(
        forward_kernel,
        "forward",
        [pl.BlockSpec(memory_space=pltpu.SMEM)] + in_vmem(1 + 2 * NX),
        [jax.ShapeDtypeStruct((count, cols), bf16)],
        [pltpu.VMEM((NX, cols, width // NX), bf16), pltpu.VMEM((count, cols), f32)],
        2 * cols * count * width,
        2 * (count * width + cols * width + cols * count),
    )(place, held, *own, *other)[0]


def plane_kernel(planes_ref, piece_ref, squares_ref):
    unit = piece_ref.shape[0]
    total = planes_ref[:unit].astype(f32)
    for z in range(1, NZ):
        total += planes_ref[z * unit : (z + 1) * unit].astype(f32)
    piece_ref[...] = total.astype(bf16)
    squares_ref[...] = jnp.broadcast_to(jnp.sum(total * total), squares_ref.shape)


def plane_sum(planes):
    unit, rows = planes.shape[0] // NZ, planes.shape[1]
    everyone = NY * NC * NX * NZ
    return kernel_call(
        plane_kernel,
        "plane_sum",
        in_vmem(1),
        [jax.ShapeDtypeStruct((unit, rows), bf16), jax.ShapeDtypeStruct((everyone, 128), f32)],
    )(planes)


def weight_kernel(count, place_ref, piece_ref, squares_ref, *refs):
    states, (out_ref, wide, turned) = refs[:3], refs[3:]
    y, c = place_ref[0], place_ref[1]
    unit, rows = piece_ref.shape
    half = wide.shape[1]
    at = pl.multiple_of(y * unit, unit)
    lanes = pl.ds(pl.multiple_of(c * half, half), half)
    total = jnp.sum(squares_ref[:, :1])
    turned[...] = jnp.zeros_like(turned)
    turned[pl.ds(at, unit), :] = piece_ref[...].astype(f32)
    wide[...] = turned[...].T
    new = apply_update(wide[...], *[state[:, lanes] for state in states], total, count)[0]
    turned[...] = new.T
    mine = turned[pl.ds(at, unit), :].astype(bf16)
    for z in range(NZ):
        out_ref[z * unit : (z + 1) * unit, :] = mine


def weight_piece(place, piece, squares, states, count):
    unit, rows = piece.shape
    half = states[0].shape[1] // 2
    return kernel_call(
        functools.partial(weight_kernel, count),
        "weight_piece",
        [pl.BlockSpec(memory_space=pltpu.SMEM)] + in_vmem(2 + len(states)),
        [jax.ShapeDtypeStruct((NZ * unit, rows), bf16)],
        [pltpu.VMEM((rows, half), f32), pltpu.VMEM((half, rows), f32)],
    )(place, piece, squares, *states)[0]


def spread_kernel(piece_ref, after_ref, out_ref):
    del after_ref
    unit = piece_ref.shape[0]
    for i in range(out_ref.shape[0] // unit):
        out_ref[i * unit : (i + 1) * unit, :] = piece_ref[...]


def spread(piece, copies, after):
    unit, rows = piece.shape
    return kernel_call(
        spread_kernel,
        "spread",
        in_vmem(1) + [pl.BlockSpec(memory_space=pl.ANY)],
        [jax.ShapeDtypeStruct((copies * unit, rows), bf16)],
    )(piece, after)[0]


def update_kernel(count, grads_ref, squares_ref, *refs):
    total = jnp.sum(squares_ref[:, :1])
    new = apply_update(grads_ref[...].astype(f32).T, *[ref[...] for ref in refs[:3]], total, count)
    for ref, value in zip(refs[3:], new):
        ref[...] = value


def update(grads, squares, states, count):
    return kernel_call(
        functools.partial(update_kernel, count),
        "update",
        in_vmem(2 + len(states)),
        [jax.ShapeDtypeStruct(states[0].shape, f32)] * 3,
    )(grads, squares, *states)


def add(*parts):
    total = parts[0].astype(f32)
    for part in parts[1:]:
        total = total + part.astype(f32)
    return total


def body(tokens, cotangent, master, first_moment, second_moment):
    y, c, x = lax.axis_index("y"), lax.axis_index("core"), lax.axis_index("x")
    place = jnp.stack([y, c, x]).astype(jnp.int32)
    states = (master, first_moment, second_moment)
    rows, cols = master.shape
    count = rows * NX * NZ * cols
    unit = cols // (NC * NY)

    own, other, held = partial_terms(place, cotangent, tokens)
    chip = {}
    for d in (2, 1, 3, 0):
        chip[d] = add(own[d], send(other[d], "core", 1)).astype(bf16)
    got = [routed(chip[d], d, True) for d in FAR_FIRST]
    line = add(chip[0], *got).astype(bf16)
    got = [routed(line[d * unit : (d + 1) * unit], d, False) for d in FAR_FIRST]
    plane = add(line[:unit], *got).astype(bf16)
    planes = lax.all_to_all(plane, "z", 1, 0, tiled=True)
    piece, squares = plane_sum(planes)
    squares = lax.all_to_all(squares, NAMES, 0, 0, tiled=True)

    weight = weight_piece(place, piece, squares, states, count)
    plane = lax.all_to_all(weight, "z", 0, 1, tiled=True)
    line = jnp.concatenate([plane] + [routed(plane, d, False) for d in (1, 2, 3)], 0)
    own = [line] + [routed(line, d, True) for d in (1, 2, 3)]
    other = [send(part, "core", 1) for part in own]

    grads = lax.all_to_all(spread(piece, NC * NY, other[0]), ("core", "y"), 0, 0, tiled=True)
    master_new, first_new, second_new = update(grads, squares, states, count)
    activations = forward(place, held, own, other)
    return (master_new, first_new, second_new, activations)


def solution(mesh):
    fine = Mesh(mesh.devices.reshape(NY, NC, NX, NZ), NAMES)
    by_token, by_row = P(NAMES, None), P(("x", "z"), None)
    return jax.shard_map(
        body,
        mesh=fine,
        in_specs=(by_token, by_token, by_row, by_row, by_row),
        out_specs=(by_row, by_row, by_row, by_token),
        check_vma=False,
    )
```

time: 489 us -> 146 us (0.30)
  waiting for transfers between devices: 388 us -> 39.6 us
  starting transfers between devices: 0.12 us -> 29.9 us
  matrix products: 20 us -> 0 us
  Pallas kernels: 0 us -> 14.7 us
  between operations: 14.5 us -> 0.81 us
    reduce_scatter x1 -> x0, waiting for transfers between devices: 225 us -> none  [body(): lax.psum_scatter(row_terms(tokens, cotangent).astype(jnp.bfloat16), 'shar...]
    all_gather x1 -> x0, waiting for transfers between devices: 95.7 us -> none  [body(): lax.all_gather(weight, 'shard', axis=0, tiled=True)]
    psum x1 -> x0, waiting for transfers between devices: 66.9 us -> none  [body(): grads = lax.psum(grads.astype(jnp.bfloat16), 'rep').astype(jnp.float32)]
    psum x1 -> x0, blocking collectives: 61.7 us -> none  [body(): total = lax.psum(jnp.sum(grads * grads), 'shard')]
    all_to_all x0 -> x4, blocking collectives: none -> 59.2 us  [the longest x1 21.9 us: body(): squares = lax.all_to_all(squares, NAMES, 0, 0, tiled=True)]
    ppermute x0 -> x20, waiting for transfers between devices: none -> 39.6 us  [the longest x12 37.1 us: routed(): return lax.ppermute(value, ('y', 'core', 'x'), pairs)]
    ppermute x0 -> x20, starting transfers between devices: none -> 29.9 us  [the longest x8 19.8 us: send(): return lax.ppermute(value, axis, [(i, (i + step) % n) for i in range(n)])]
    dot_general x2 -> x0, matrix products: 20 us -> none  [the longest x1 10.3 us: row_terms(): lax.dot_general(source, cotangent, (((0,), (0,)), ((), ())), preferred_el...]
  transfers between devices with their start and end apart: 3 -> 20, of which waited for: 3 -> 10; matrix products, arithmetic and copies ran while one was open for 0% -> 0% of each run, Pallas kernels for 0% -> 1%
where the time goes in v3:
time: 146 us
  blocking collectives  59.2 us (41%)
  waiting for transfers between devices  39.6 us (27%)
  starting transfers between devices  29.9 us (20%)
  Pallas kernels  14.7 us (10%)
    ppermute x12, waiting for transfers between devices, routed(): return lax.ppermute(value, ('y', 'core', 'x'), pairs)  37.1 us
    all_to_all x1, blocking collectives, body(): squares = lax.all_to_all(squares, NAMES, 0, 0, tiled=True)  21.9 us
    ppermute x8, starting transfers between devices, send(): return lax.ppermute(value, axis, [(i, (i + step) % n) for i in range(n)])  19.8 us
    all_to_all x1, blocking collectives, body(): planes = lax.all_to_all(plane, 'z', 1, 0, tiled=True)  16.6 us
    all_to_all x1, blocking collectives, body(): plane = lax.all_to_all(weight, 'z', 0, 1, tiled=True)  12 us
    ppermute x12, starting transfers between devices, routed(): return lax.ppermute(value, ('y', 'core', 'x'), pairs)  10 us
    all_to_all x1, blocking collectives, body(): lax.all_to_all(spread(piece, NC * NY, other[0]), ('core', 'y'), 0, 0, til...  8.67 us
    pallas_call x1, Pallas kernels, partial_terms(): kernel_call(partial_kernel, 'partial_terms', [pl.BlockSpec(memory_space=p...  6.55 us
  transfers between devices with their start and end apart: 20, of which 10 were waited for; matrix products, arithmetic and copies ran while one was open for 0% of the time, Pallas kernels for 1%

profile of v3, /device:TPU:1, one launch (start us, length us, event | category | flops | bytes accessed | tf_op | source)
XLA Modules:
  0.0 145.8 jit_solution(9362552147012561886)
XLA Ops:
  0.7 6.6 %partial_terms.1 = (bf16[128,3072]{1,0:T(8,128)(2,1)S(1)}, bf16[128,3072]{1,0:T(8,128)(2,1)S(1)}, bf16[128,3072]{1,0:T(8,128)(2,1)S(1)}, bf16[128,3072]{1,0:T(8,...) custom-call(s32[3]{0:T(128)S(1)} %pad_add_fusion.place_ref, ...), custom_call_target="tpu_custom_call" | custom-call | flops 2818572288 | bytes 17530880 | tf_op jit(solution)/shard_map/partial_terms/pallas_call | solution.py:135
  7.3 3.3 %collective-permute-start.1 = (bf16[128,3072]{1,0:T(8,128)(2,1)S(1)}, bf16[128,3072]{1,0:T(8,128)(2,1)S(1)}, u32[]{:S(2)}, u32[]{:S(2)}) collective-permute-start(bf16[128,3072]{1,0:T(8,128)(2,1)S(1)} %get-tuple-element.21), channel_id=1, source_target_pairs={{0,32},{32,0},{1,33},{33,1},{2,34},{34,2},{3,35},{35,3},{4,36},{36... | collective-permute-start | bytes 2359304 | tf_op jit(solution)/shard_map/ppermute | solution.py:41
  11.2 1.3 collective-permute-done.1
  12.7 1.3 collective-permute-start.2
  14.7 1.2 collective-permute-done.5
  16.1 1.1 collective-permute-start.6
  17.2 8.3 %collective-permute-done.2 = bf16[128,3072]{1,0:T(8,128)(2,1)S(1)} collective-permute-done((bf16[128,3072]{1,0:T(8,128)(2,1)S(1)}, bf16[128,3072]{1,0:T(8,128)(2,1)S(1)}, u32[]{:S(2)}, u32[]{:S(2)}) %collective-permute-start.2) | collective-permute-done | bytes 786464 | tf_op jit(solution)/shard_map/ppermute | solution.py:55
  25.5 8.4 %collective-permute-done.4 = bf16[128,3072]{1,0:T(8,128)(2,1)S(1)} collective-permute-done((bf16[128,3072]{1,0:T(8,128)(2,1)S(1)}, bf16[128,3072]{1,0:T(8,128)(2,1)S(1)}, u32[]{:S(2)}, u32[]{:S(2)}) %collective-permute-start.4) | collective-permute-done | bytes 786464 | tf_op jit(solution)/shard_map/ppermute | solution.py:55
  33.9 0.6 add_convert_fusion
  34.6 1.5 %collective-permute-start.7 = (bf16[32,3072]{1,0:T(8,128)(2,1)S(1)}, bf16[32,3072]{1,0:T(8,128)(2,1)S(1)}, u32[]{:S(2)}, u32[]{:S(2)}) collective-permute-start(bf16[32,3072]{1,0:T(8,128)(2,1)S(1)} %get-tuple-element.32), channel_id=1, source_target_pairs={{0,128},{8,136},{16,144},{24,152},{32,48},{40,56},{48,32},{56,40},... | collective-permute-start | bytes 589832 | tf_op jit(solution)/shard_map/ppermute | solution.py:55
  36.1 0.9 collective-permute-start.9
  36.9 0.6 collective-permute-start.8
  37.5 3.5 %collective-permute-done.7 = bf16[32,3072]{1,0:T(8,128)(2,1)S(1)} collective-permute-done((bf16[32,3072]{1,0:T(8,128)(2,1)S(1)}, bf16[32,3072]{1,0:T(8,128)(2,1)S(1)}, u32[]{:S(2)}, u32[]{:S(2)}) %collective-permute-start.7) | collective-permute-done | bytes 196640 | tf_op jit(solution)/shard_map/ppermute | solution.py:55
  41.0 0.8 collective-permute-done.9
  41.8 1.3 collective-permute-done.8
  43.3 16.6 %all_to_all.60 = bf16[32,8,384]{2,0,1:T(8,128)(2,1)S(1)} all-to-all(bf16[32,8,384]{2,0,1:T(8,128)(2,1)S(1)} %bitcast.31), channel_id=1, replica_groups=mesh['y'=4,'core'=2,'x'=4,'z'=8] {'z'}, dimensions={1} | all-to-all | bytes 393216 | tf_op jit(solution)/shard_map/all_to_all | solution.py:314
  60.0 21.9 %all_to_all.61 = f32[256,1,128]{2,1,0:T(1,128)S(1)} all-to-all(f32[256,1,128]{2,1,0:T(1,128)S(1)} %bitcast.26), channel_id=1, replica_groups=mesh['y'=4,'core'=2,'x'=4,'z'=8] {'y','core','x','z'}, dimensions={0} | all-to-all | bytes 262144 | tf_op jit(solution)/shard_map/all_to_all | solution.py:316
  81.9 1.1 weight_piece.1
  83.0 12.0 %all_to_all.62 = bf16[8,32,384]{2,1,0:T(8,128)(2,1)S(1)} all-to-all(bf16[8,32,384]{2,1,0:T(8,128)(2,1)S(1)} %bitcast.25), channel_id=1, replica_groups=mesh['y'=4,'core'=2,'x'=4,'z'=8] {'z'}, dimensions={0} | all-to-all | bytes 393216 | tf_op jit(solution)/shard_map/all_to_all | solution.py:319
  95.1 2.1 %collective-permute-start.11 = (bf16[32,3072]{1,0:T(8,128)(2,1)S(1)}, bf16[32,3072]{1,0:T(8,128)(2,1)S(1)}, u32[]{:S(2)}, u32[]{:S(2)}) collective-permute-start(bf16[32,3072]{1,0:T(8,128)(2,1)S(1)} %bitcast.28), channel_id=1, source_target_pairs={{0,128},{8,136},{16,144},{24,152},{32,48},{40,56},{48,32},{56,40},... | collective-permute-start | bytes 589832 | tf_op jit(solution)/shard_map/ppermute | solution.py:55
  97.2 6.4 %collective-permute-done.10 = bf16[32,3072]{1,0:T(8,128)(2,1)S(1)} collective-permute-done((bf16[32,3072]{1,0:T(8,128)(2,1)S(1)}, bf16[32,3072]{1,0:T(8,128)(2,1)S(1)}, u32[]{:S(2)}, u32[]{:S(2)}) %collective-permute-start.10) | collective-permute-done | bytes 196640 | tf_op jit(solution)/shard_map/ppermute | solution.py:55
  103.7 0.7 collective-permute-start.16
  104.4 1.4 collective-permute-start.15
  105.8 4.3 %collective-permute-start.13 = (bf16[128,3072]{1,0:T(8,128)(2,1)S(1)}, bf16[128,3072]{1,0:T(8,128)(2,1)S(1)}, u32[]{:S(2)}, u32[]{:S(2)}) collective-permute-start(bf16[128,3072]{1,0:T(8,128)(2,1)S(1)} %constant_dynamic-update-slice_fusion.refs_0_), channel_id=1, source_target_pairs={{0,32},{32,0},{1,33},{33,1},{2,34},{34,2},{3,35},{35,3},{4,36},{36... | collective-permute-start | bytes 2359304 | tf_op jit(solution)/shard_map/ppermute | solution.py:41
  110.1 4.8 %collective-permute-done.16.refs_3_ = bf16[128,3072]{1,0:T(8,128)(2,1)S(1)} collective-permute-done((bf16[128,3072]{1,0:T(8,128)(2,1)S(1)}, bf16[128,3072]{1,0:T(8,128)(2,1)S(1)}, u32[]{:S(2)}, u32[]{:S(2)}) %collective-permute-start.16) | collective-permute-done | bytes 786464 | tf_op jit(solution)/shard_map/ppermute | solution.py:55
  115.0 4.5 %collective-permute-start.19 = (bf16[128,3072]{1,0:T(8,128)(2,1)S(1)}, bf16[128,3072]{1,0:T(8,128)(2,1)S(1)}, u32[]{:S(2)}, u32[]{:S(2)}) collective-permute-start(bf16[128,3072]{1,0:T(8,128)(2,1)S(1)} %collective-permute-done.16.refs_3_), channel_id=1, source_target_pairs={{0,32},{32,0},{1,33},{33,1},{2,34},{34,2},{3,35},{35,3},{4,36},{36... | collective-permute-start | bytes 2359304 | tf_op jit(solution)/shard_map/ppermute | solution.py:41
  119.5 2.4 %collective-permute-start.18 = (bf16[128,3072]{1,0:T(8,128)(2,1)S(1)}, bf16[128,3072]{1,0:T(8,128)(2,1)S(1)}, u32[]{:S(2)}, u32[]{:S(2)}) collective-permute-start(bf16[128,3072]{1,0:T(8,128)(2,1)S(1)} %collective-permute-done.15.refs_2_), channel_id=1, source_target_pairs={{0,32},{32,0},{1,33},{33,1},{2,34},{34,2},{3,35},{35,3},{4,36},{36... | collective-permute-start | bytes 2359304 | tf_op jit(solution)/shard_map/ppermute | solution.py:41
  121.8 3.6 %collective-permute-done.14.refs_1_ = bf16[128,3072]{1,0:T(8,128)(2,1)S(1)} collective-permute-done((bf16[128,3072]{1,0:T(8,128)(2,1)S(1)}, bf16[128,3072]{1,0:T(8,128)(2,1)S(1)}, u32[]{:S(2)}, u32[]{:S(2)}) %collective-permute-start.14) | collective-permute-done | bytes 786464 | tf_op jit(solution)/shard_map/ppermute | solution.py:55
  125.5 4.7 %collective-permute-start.17 = (bf16[128,3072]{1,0:T(8,128)(2,1)S(1)}, bf16[128,3072]{1,0:T(8,128)(2,1)S(1)}, u32[]{:S(2)}, u32[]{:S(2)}) collective-permute-start(bf16[128,3072]{1,0:T(8,128)(2,1)S(1)} %collective-permute-done.14.refs_1_), channel_id=1, source_target_pairs={{0,32},{32,0},{1,33},{33,1},{2,34},{34,2},{3,35},{35,3},{4,36},{36... | collective-permute-start | bytes 2359304 | tf_op jit(solution)/shard_map/ppermute | solution.py:41
  130.2 8.7 %all_to_all.63 = bf16[8,32,384]{2,1,0:T(8,128)(2,1)S(1)} all-to-all(bf16[8,32,384]{2,1,0:T(8,128)(2,1)S(1)} %bitcast.24), channel_id=1, replica_groups=mesh['y'=4,'core'=2,'x'=4,'z'=8] {'core','y'}, dimensions={0} | all-to-all | bytes 393216 | tf_op jit(solution)/shard_map/all_to_all | solution.py:324
  138.9 1.5 %update.1 = (f32[384,256]{1,0:T(8,128)}, f32[384,256]{1,0:T(8,128)}, f32[384,256]{1,0:T(8,128)}) custom-call(bf16[256,384]{1,0:T(8,128)(2,1)S(1)} %bitcast.23, f32[256,128]{1,0:T(8,128)S(1)} %bitcast.21, f32[384,256]{1,0:T(8,128)S(1)} %copy-done, f32[384,256]{1,0:T(8,128)S(1)} %copy-done.1, f32[384,256]{1,0:T(8,128)S(1)} %copy-done.2), custom_call_target="tpu_custom_call" | custom-call | tf_op jit(solution)/shard_map/update/pallas_call | solution.py:283
  140.4 5.3 %forward.1 = bf16[448,256]{1,0:T(8,128)(2,1)} custom-call(s32[3]{0:T(128)S(1)} %pad_add_fusion.place_ref, bf16[448,12288]{1,0:T(8,128)(2,1)S(1)} %get-tuple-element.31.held, bf16[128,3072]{1,0:T(8,128)(2,1)S(1)} %constant_dynamic-update-slice_fusion.refs_0_, bf16[128,3072]{1,0:T(8,128)(2,1)S(1)} %collective-permute-done.14.refs_1_, ...), custom_call_target="tpu_custom_call" | custom-call | flops 2818572288 | bytes 17530880 | tf_op jit(solution)/shard_map/forward/pallas_call | solution.py:197
  (37 shorter events, 2.3 us)
Async XLA Ops:
  7.3 5.2 %collective-permute-start.1 = (bf16[128,3072]{1,0:T(8,128)(2,1)S(1)}, bf16[128,3072]{1,0:T(8,128)(2,1)S(1)}, u32[]{:S(2)}, u32[]{:S(2)}) collective-permute-start(bf16[128,3072]{1,0:T(8,128)(2,1)S(1)} %get-tuple-element.21), channel_id=1, source_target_pairs={{0,32},{32,0},{1,33},{33,1},{2,34},{34,2},{3,35},{35,3},{4,36},{36... | collective-permute-start | bytes 2359304 | tf_op jit(solution)/shard_map/ppermute | solution.py:41
  10.6 3.4 %collective-permute-start.3 = (bf16[128,3072]{1,0:T(8,128)(2,1)S(1)}, bf16[128,3072]{1,0:T(8,128)(2,1)S(1)}, u32[]{:S(2)}, u32[]{:S(2)}) collective-permute-start(bf16[128,3072]{1,0:T(8,128)(2,1)S(1)} %get-tuple-element.23), channel_id=1, source_target_pairs={{0,32},{32,0},{1,33},{33,1},{2,34},{34,2},{3,35},{35,3},{4,36},{36... | collective-permute-start | bytes 2359304 | tf_op jit(solution)/shard_map/ppermute | solution.py:41
  10.7 6.5 %collective-permute-start = (bf16[128,3072]{1,0:T(8,128)(2,1)S(1)}, bf16[128,3072]{1,0:T(8,128)(2,1)S(1)}, u32[]{:S(2)}, u32[]{:S(2)}) collective-permute-start(bf16[128,3072]{1,0:T(8,128)(2,1)S(1)} %get-tuple-element.19), channel_id=1, source_target_pairs={{0,32},{32,0},{1,33},{33,1},{2,34},{34,2},{3,35},{35,3},{4,36},{36... | collective-permute-start | bytes 2359304 | tf_op jit(solution)/shard_map/ppermute | solution.py:41
  11.1 4.8 %collective-permute-start.5 = (bf16[128,3072]{1,0:T(8,128)(2,1)S(1)}, bf16[128,3072]{1,0:T(8,128)(2,1)S(1)}, u32[]{:S(2)}, u32[]{:S(2)}) collective-permute-start(bf16[128,3072]{1,0:T(8,128)(2,1)S(1)} %get-tuple-element.25), channel_id=1, source_target_pairs={{0,32},{32,0},{1,33},{33,1},{2,34},{34,2},{3,35},{35,3},{4,36},{36... | collective-permute-start | bytes 2359304 | tf_op jit(solution)/shard_map/ppermute | solution.py:41
  12.7 12.8 %collective-permute-start.2 = (bf16[128,3072]{1,0:T(8,128)(2,1)S(1)}, bf16[128,3072]{1,0:T(8,128)(2,1)S(1)}, u32[]{:S(2)}, u32[]{:S(2)}) collective-permute-start(bf16[128,3072]{1,0:T(8,128)(2,1)S(1)} %add_convert_fusion.3), channel_id=1, source_target_pairs={{0,16},{8,24},{16,0},{24,8},{32,160},{40,168},{48,176},{56,184},{6... | collective-permute-start | bytes 2359304 | tf_op jit(solution)/shard_map/ppermute | solution.py:55
  14.2 19.7 %collective-permute-start.4 = (bf16[128,3072]{1,0:T(8,128)(2,1)S(1)}, bf16[128,3072]{1,0:T(8,128)(2,1)S(1)}, u32[]{:S(2)}, u32[]{:S(2)}) collective-permute-start(bf16[128,3072]{1,0:T(8,128)(2,1)S(1)} %add_convert_fusion.2), channel_id=1, source_target_pairs={{0,8},{8,16},{16,24},{24,0},{32,96},{40,104},{48,112},{56,120},{64... | collective-permute-start | bytes 2359304 | tf_op jit(solution)/shard_map/ppermute | solution.py:55
  16.1 17.8 %collective-permute-start.6 = (bf16[128,3072]{1,0:T(8,128)(2,1)S(1)}, bf16[128,3072]{1,0:T(8,128)(2,1)S(1)}, u32[]{:S(2)}, u32[]{:S(2)}) collective-permute-start(bf16[128,3072]{1,0:T(8,128)(2,1)S(1)} %add_convert_fusion.1), channel_id=1, source_target_pairs={{0,24},{8,0},{16,8},{24,16},{32,224},{40,232},{48,240},{56,248},{6... | collective-permute-start | bytes 2359304 | tf_op jit(solution)/shard_map/ppermute | solution.py:55
  34.5 47.4 %copy-start = (f32[384,256]{1,0:T(8,128)S(1)}, f32[384,256]{1,0:T(8,128)}, u32[]{:S(2)}) copy-start(f32[384,256]{1,0:T(8,128)} %refs_0_.3) | copy-start | bytes 1179652
  34.5 47.4 %copy-start.1 = (f32[384,256]{1,0:T(8,128)S(1)}, f32[384,256]{1,0:T(8,128)}, u32[]{:S(2)}) copy-start(f32[384,256]{1,0:T(8,128)} %refs_1_.3) | copy-start | bytes 1179652
  34.5 47.4 %copy-start.2 = (f32[384,256]{1,0:T(8,128)S(1)}, f32[384,256]{1,0:T(8,128)}, u32[]{:S(2)}) copy-start(f32[384,256]{1,0:T(8,128)} %refs_2_.3) | copy-start | bytes 1179652
  34.6 6.4 %collective-permute-start.7 = (bf16[32,3072]{1,0:T(8,128)(2,1)S(1)}, bf16[32,3072]{1,0:T(8,128)(2,1)S(1)}, u32[]{:S(2)}, u32[]{:S(2)}) collective-permute-start(bf16[32,3072]{1,0:T(8,128)(2,1)S(1)} %get-tuple-element.32), channel_id=1, source_target_pairs={{0,128},{8,136},{16,144},{24,152},{32,48},{40,56},{48,32},{56,40},... | collective-permute-start | bytes 589832 | tf_op jit(solution)/shard_map/ppermute | solution.py:55
  36.1 5.8 %collective-permute-start.9 = (bf16[32,3072]{1,0:T(8,128)(2,1)S(1)}, bf16[32,3072]{1,0:T(8,128)(2,1)S(1)}, u32[]{:S(2)}, u32[]{:S(2)}) collective-permute-start(bf16[32,3072]{1,0:T(8,128)(2,1)S(1)} %get-tuple-element.33), channel_id=1, source_target_pairs={{0,192},{8,200},{16,208},{24,216},{32,56},{40,32},{48,40},{56,48},... | collective-permute-start | bytes 589832 | tf_op jit(solution)/shard_map/ppermute | solution.py:55
  36.9 6.2 %collective-permute-start.8 = (bf16[32,3072]{1,0:T(8,128)(2,1)S(1)}, bf16[32,3072]{1,0:T(8,128)(2,1)S(1)}, u32[]{:S(2)}, u32[]{:S(2)}) collective-permute-start(bf16[32,3072]{1,0:T(8,128)(2,1)S(1)} %get-tuple-element.34), channel_id=1, source_target_pairs={{0,64},{8,72},{16,80},{24,88},{32,40},{40,48},{48,56},{56,32},{64,... | collective-permute-start | bytes 589832 | tf_op jit(solution)/shard_map/ppermute | solution.py:55
  95.1 8.7 %collective-permute-start.12 = (bf16[32,3072]{1,0:T(8,128)(2,1)S(1)}, bf16[32,3072]{1,0:T(8,128)(2,1)S(1)}, u32[]{:S(2)}, u32[]{:S(2)}) collective-permute-start(bf16[32,3072]{1,0:T(8,128)(2,1)S(1)} %bitcast.27), channel_id=1, source_target_pairs={{0,192},{8,200},{16,208},{24,216},{32,56},{40,32},{48,40},{56,48},... | collective-permute-start | bytes 589832 | tf_op jit(solution)/shard_map/ppermute | solution.py:55
  95.1 8.5 %collective-permute-start.11 = (bf16[32,3072]{1,0:T(8,128)(2,1)S(1)}, bf16[32,3072]{1,0:T(8,128)(2,1)S(1)}, u32[]{:S(2)}, u32[]{:S(2)}) collective-permute-start(bf16[32,3072]{1,0:T(8,128)(2,1)S(1)} %bitcast.28), channel_id=1, source_target_pairs={{0,128},{8,136},{16,144},{24,152},{32,48},{40,56},{48,32},{56,40},... | collective-permute-start | bytes 589832 | tf_op jit(solution)/shard_map/ppermute | solution.py:55
  97.2 6.4 %collective-permute-start.10 = (bf16[32,3072]{1,0:T(8,128)(2,1)S(1)}, bf16[32,3072]{1,0:T(8,128)(2,1)S(1)}, u32[]{:S(2)}, u32[]{:S(2)}) collective-permute-start(bf16[32,3072]{1,0:T(8,128)(2,1)S(1)} %bitcast.29), channel_id=1, source_target_pairs={{0,64},{8,72},{16,80},{24,88},{32,40},{40,48},{48,56},{56,32},{64,... | collective-permute-start | bytes 589832 | tf_op jit(solution)/shard_map/ppermute | solution.py:55
  103.7 11.2 %collective-permute-start.16 = (bf16[128,3072]{1,0:T(8,128)(2,1)S(1)}, bf16[128,3072]{1,0:T(8,128)(2,1)S(1)}, u32[]{:S(2)}, u32[]{:S(2)}) collective-permute-start(bf16[128,3072]{1,0:T(8,128)(2,1)S(1)} %constant_dynamic-update-slice_fusion.refs_0_), channel_id=1, source_target_pairs={{0,24},{8,0},{16,8},{24,16},{32,224},{40,232},{48,240},{56,248},{6... | collective-permute-start | bytes 2359304 | tf_op jit(solution)/shard_map/ppermute | solution.py:55
  104.4 15.1 %collective-permute-start.15 = (bf16[128,3072]{1,0:T(8,128)(2,1)S(1)}, bf16[128,3072]{1,0:T(8,128)(2,1)S(1)}, u32[]{:S(2)}, u32[]{:S(2)}) collective-permute-start(bf16[128,3072]{1,0:T(8,128)(2,1)S(1)} %constant_dynamic-update-slice_fusion.refs_0_), channel_id=1, source_target_pairs={{0,16},{8,24},{16,0},{24,8},{32,160},{40,168},{48,176},{56,184},{6... | collective-permute-start | bytes 2359304 | tf_op jit(solution)/shard_map/ppermute | solution.py:55
  105.8 19.7 %collective-permute-start.14 = (bf16[128,3072]{1,0:T(8,128)(2,1)S(1)}, bf16[128,3072]{1,0:T(8,128)(2,1)S(1)}, u32[]{:S(2)}, u32[]{:S(2)}) collective-permute-start(bf16[128,3072]{1,0:T(8,128)(2,1)S(1)} %constant_dynamic-update-slice_fusion.refs_0_), channel_id=1, source_target_pairs={{0,8},{8,16},{16,24},{24,0},{32,96},{40,104},{48,112},{56,120},{64... | collective-permute-start | bytes 2359304 | tf_op jit(solution)/shard_map/ppermute | solution.py:55
  105.8 24.4 %collective-permute-start.13 = (bf16[128,3072]{1,0:T(8,128)(2,1)S(1)}, bf16[128,3072]{1,0:T(8,128)(2,1)S(1)}, u32[]{:S(2)}, u32[]{:S(2)}) collective-permute-start(bf16[128,3072]{1,0:T(8,128)(2,1)S(1)} %constant_dynamic-update-slice_fusion.refs_0_), channel_id=1, source_target_pairs={{0,32},{32,0},{1,33},{33,1},{2,34},{34,2},{3,35},{35,3},{4,36},{36... | collective-permute-start | bytes 2359304 | tf_op jit(solution)/shard_map/ppermute | solution.py:41
  115.0 25.4 %collective-permute-start.19 = (bf16[128,3072]{1,0:T(8,128)(2,1)S(1)}, bf16[128,3072]{1,0:T(8,128)(2,1)S(1)}, u32[]{:S(2)}, u32[]{:S(2)}) collective-permute-start(bf16[128,3072]{1,0:T(8,128)(2,1)S(1)} %collective-permute-done.16.refs_3_), channel_id=1, source_target_pairs={{0,32},{32,0},{1,33},{33,1},{2,34},{34,2},{3,35},{35,3},{4,36},{36... | collective-permute-start | bytes 2359304 | tf_op jit(solution)/shard_map/ppermute | solution.py:41
  119.5 20.9 %collective-permute-start.18 = (bf16[128,3072]{1,0:T(8,128)(2,1)S(1)}, bf16[128,3072]{1,0:T(8,128)(2,1)S(1)}, u32[]{:S(2)}, u32[]{:S(2)}) collective-permute-start(bf16[128,3072]{1,0:T(8,128)(2,1)S(1)} %collective-permute-done.15.refs_2_), channel_id=1, source_target_pairs={{0,32},{32,0},{1,33},{33,1},{2,34},{34,2},{3,35},{35,3},{4,36},{36... | collective-permute-start | bytes 2359304 | tf_op jit(solution)/shard_map/ppermute | solution.py:41
  125.5 14.9 %collective-permute-start.17 = (bf16[128,3072]{1,0:T(8,128)(2,1)S(1)}, bf16[128,3072]{1,0:T(8,128)(2,1)S(1)}, u32[]{:S(2)}, u32[]{:S(2)}) collective-permute-start(bf16[128,3072]{1,0:T(8,128)(2,1)S(1)} %collective-permute-done.14.refs_1_), channel_id=1, source_target_pairs={{0,32},{32,0},{1,33},{33,1},{2,34},{34,2},{3,35},{35,3},{4,36},{36... | collective-permute-start | bytes 2359304 | tf_op jit(solution)/shard_map/ppermute | solution.py:41

commit v4 on v3

--- a/solution.py
+++ b/solution.py
@@ -272,6 +272,21 @@
     )(piece, after)[0]
 
 
+def tie_kernel(value_ref, after_ref, out_ref):
+    pass
+
+
+def tie(value, after):
+    return pl.pallas_call(
+        tie_kernel,
+        in_specs=[pl.BlockSpec(memory_space=pl.ANY)] * 2,
+        out_specs=pl.BlockSpec(memory_space=pl.ANY),
+        out_shape=jax.ShapeDtypeStruct(value.shape, value.dtype),
+        input_output_aliases={0: 0},
+        name="tie",
+    )(value, after)
+
+
 def update_kernel(count, grads_ref, squares_ref, *refs):
     total = jnp.sum(squares_ref[:, :1])
     new = apply_update(grads_ref[...].astype(f32).T, *[ref[...] for ref in refs[:3]], total, count)
@@ -319,10 +334,10 @@
     plane = lax.all_to_all(weight, "z", 0, 1, tiled=True)
     line = jnp.concatenate([plane] + [routed(plane, d, False) for d in (1, 2, 3)], 0)
     own = [line] + [routed(line, d, True) for d in (1, 2, 3)]
+    grads = lax.all_to_all(spread(piece, NC * NY, own[3]), ("core", "y"), 0, 0, tiled=True)
+    master_new, first_new, second_new = update(grads, squares, states, count)
+    own[1] = tie(own[1], master_new)
     other = [send(part, "core", 1) for part in own]
-
-    grads = lax.all_to_all(spread(piece, NC * NY, other[0]), ("core", "y"), 0, 0, tiled=True)
-    master_new, first_new, second_new = update(grads, squares, states, count)
     activations = forward(place, held, own, other)
     return (master_new, first_new, second_new, activations)
 

time: 146 us -> 160 us (1.096)
  the two profiles are of different devices: /device:TPU:1 before, /device:TPU:3 now
where the time goes in v4:
time: 160 us; the launch traced here: 159 us
  blocking collectives  50.9 us (32%)
  waiting for transfers between devices  44.6 us (28%)
  starting transfers between devices  32.9 us (21%)
  Pallas kernels  16.7 us (10%)
  local copies, waits for them, and re-layouts  12.1 us (8%)
    ppermute x12, waiting for transfers between devices, routed(): return lax.ppermute(value, ('y', 'core', 'x'), pairs)  35.8 us
    all_to_all x1, blocking collectives, body(): squares = lax.all_to_all(squares, NAMES, 0, 0, tiled=True)  22.2 us
    all_to_all x1, blocking collectives, body(): planes = lax.all_to_all(plane, 'z', 1, 0, tiled=True)  16.7 us
    all_to_all x1, starting transfers between devices, body(): lax.all_to_all(spread(piece, NC * NY, own[3]), ('core', 'y'), 0, 0, tiled...  16.6 us
    ppermute x12, starting transfers between devices, routed(): return lax.ppermute(value, ('y', 'core', 'x'), pairs)  14 us
    all_to_all x1, blocking collectives, body(): plane = lax.all_to_all(weight, 'z', 0, 1, tiled=True)  12 us
    unnamed x23, local copies, waits for them, and re-layouts  12 us
    pallas_call x1, Pallas kernels, forward(): kernel_call(forward_kernel, 'forward', [pl.BlockSpec(memory_space=pltpu.S...  6.6 us
  transfers between devices with their start and end apart: 21, of which 10 were waited for; matrix products, arithmetic and copies ran while one was open for 0% of the time, Pallas kernels for 2%

profile of v4, /device:TPU:3, one launch (start us, length us, event | category | flops | bytes accessed | tf_op | source)
XLA Modules:
  0.0 159.4 jit_solution(12935796062985631328)
XLA Ops:
  0.7 6.4 %partial_terms.1 = (bf16[128,3072]{1,0:T(8,128)(2,1)S(1)}, bf16[128,3072]{1,0:T(8,128)(2,1)S(1)}, bf16[128,3072]{1,0:T(8,128)(2,1)S(1)}, bf16[128,3072]{1,0:T(8,...) custom-call(s32[3]{0:T(128)S(1)} %pad_add_fusion.place_ref, ...), custom_call_target="tpu_custom_call" | custom-call | flops 2818572288 | bytes 17530880 | tf_op jit(solution)/shard_map/partial_terms/pallas_call | solution.py:135
  7.2 4.2 %copy-done = bf16[448,12288]{1,0:T(8,128)(2,1)} copy-done((bf16[448,12288]{1,0:T(8,128)(2,1)}, bf16[448,12288]{1,0:T(8,128)(2,1)S(1)}, u32[]{:S(2)}) %copy-start) | copy-done | bytes 11010072
  11.3 0.7 collective-permute-start.1
  12.5 1.4 collective-permute-done.1
  14.1 3.0 %collective-permute-start.2 = (bf16[128,3072]{1,0:T(8,128)(2,1)S(1)}, bf16[128,3072]{1,0:T(8,128)(2,1)S(1)}, u32[]{:S(2)}, u32[]{:S(2)}) collective-permute-start(bf16[128,3072]{1,0:T(8,128)(2,1)S(1)} %add_convert_fusion.3), channel_id=1, source_target_pairs={{0,16},{8,24},{16,0},{24,8},{32,160},{40,168},{48,176},{56,184},{6... | collective-permute-start | bytes 2359304 | tf_op jit(solution)/shard_map/ppermute | solution.py:55
  18.0 2.4 %collective-permute-start.6 = (bf16[128,3072]{1,0:T(8,128)(2,1)S(1)}, bf16[128,3072]{1,0:T(8,128)(2,1)S(1)}, u32[]{:S(2)}, u32[]{:S(2)}) collective-permute-start(bf16[128,3072]{1,0:T(8,128)(2,1)S(1)} %add_convert_fusion.1), channel_id=1, source_target_pairs={{0,24},{8,0},{16,8},{24,16},{32,224},{40,232},{48,240},{56,248},{6... | collective-permute-start | bytes 2359304 | tf_op jit(solution)/shard_map/ppermute | solution.py:55
  20.3 6.3 %collective-permute-done.2 = bf16[128,3072]{1,0:T(8,128)(2,1)S(1)} collective-permute-done((bf16[128,3072]{1,0:T(8,128)(2,1)S(1)}, bf16[128,3072]{1,0:T(8,128)(2,1)S(1)}, u32[]{:S(2)}, u32[]{:S(2)}) %collective-permute-start.2) | collective-permute-done | bytes 786464 | tf_op jit(solution)/shard_map/ppermute | solution.py:55
  26.7 8.3 %collective-permute-done.4 = bf16[128,3072]{1,0:T(8,128)(2,1)S(1)} collective-permute-done((bf16[128,3072]{1,0:T(8,128)(2,1)S(1)}, bf16[128,3072]{1,0:T(8,128)(2,1)S(1)}, u32[]{:S(2)}, u32[]{:S(2)}) %collective-permute-start.4) | collective-permute-done | bytes 786464 | tf_op jit(solution)/shard_map/ppermute | solution.py:55
  35.0 0.7 collective-permute-done.6
  36.4 1.9 %collective-permute-start.7 = (bf16[32,3072]{1,0:T(8,128)(2,1)S(1)}, bf16[32,3072]{1,0:T(8,128)(2,1)S(1)}, u32[]{:S(2)}, u32[]{:S(2)}) collective-permute-start(bf16[32,3072]{1,0:T(8,128)(2,1)S(1)} %get-tuple-element.32), channel_id=1, source_target_pairs={{0,128},{8,136},{16,144},{24,152},{32,48},{40,56},{48,32},{56,40},... | collective-permute-start | bytes 589832 | tf_op jit(solution)/shard_map/ppermute | solution.py:55
  38.3 1.2 collective-permute-start.9
  39.8 3.0 %collective-permute-done.7 = bf16[32,3072]{1,0:T(8,128)(2,1)S(1)} collective-permute-done((bf16[32,3072]{1,0:T(8,128)(2,1)S(1)}, bf16[32,3072]{1,0:T(8,128)(2,1)S(1)}, u32[]{:S(2)}, u32[]{:S(2)}) %collective-permute-start.7) | collective-permute-done | bytes 196640 | tf_op jit(solution)/shard_map/ppermute | solution.py:55
  42.8 2.1 %collective-permute-done.9 = bf16[32,3072]{1,0:T(8,128)(2,1)S(1)} collective-permute-done((bf16[32,3072]{1,0:T(8,128)(2,1)S(1)}, bf16[32,3072]{1,0:T(8,128)(2,1)S(1)}, u32[]{:S(2)}, u32[]{:S(2)}) %collective-permute-start.9) | collective-permute-done | bytes 196640 | tf_op jit(solution)/shard_map/ppermute | solution.py:55
  45.1 16.7 %all_to_all.60 = bf16[32,8,384]{2,0,1:T(8,128)(2,1)S(1)} all-to-all(bf16[32,8,384]{2,0,1:T(8,128)(2,1)S(1)} %bitcast.30), channel_id=1, replica_groups=mesh['y'=4,'core'=2,'x'=4,'z'=8] {'z'}, dimensions={1} | all-to-all | bytes 393216 | tf_op jit(solution)/shard_map/all_to_all | solution.py:329
  61.9 22.2 %all_to_all.61 = f32[256,1,128]{2,1,0:T(1,128)S(1)} all-to-all(f32[256,1,128]{2,1,0:T(1,128)S(1)} %bitcast.25), channel_id=1, replica_groups=mesh['y'=4,'core'=2,'x'=4,'z'=8] {'y','core','x','z'}, dimensions={0} | all-to-all | bytes 262144 | tf_op jit(solution)/shard_map/all_to_all | solution.py:331
  84.2 1.1 weight_piece.1
  85.2 12.0 %all_to_all.62 = bf16[8,32,384]{2,1,0:T(8,128)(2,1)S(1)} all-to-all(bf16[8,32,384]{2,1,0:T(8,128)(2,1)S(1)} %bitcast.24), channel_id=1, replica_groups=mesh['y'=4,'core'=2,'x'=4,'z'=8] {'z'}, dimensions={0} | all-to-all | bytes 393216 | tf_op jit(solution)/shard_map/all_to_all | solution.py:334
  97.3 1.2 collective-permute-start.12
  98.5 1.3 collective-permute-start.10
  99.8 6.3 %collective-permute-done.10 = bf16[32,3072]{1,0:T(8,128)(2,1)S(1)} collective-permute-done((bf16[32,3072]{1,0:T(8,128)(2,1)S(1)}, bf16[32,3072]{1,0:T(8,128)(2,1)S(1)}, u32[]{:S(2)}, u32[]{:S(2)}) %collective-permute-start.10) | collective-permute-done | bytes 196640 | tf_op jit(solution)/shard_map/ppermute | solution.py:55
  106.2 0.9 collective-permute-start.13
  107.1 1.3 collective-permute-start.15
  108.4 9.0 %collective-permute-done.13.after_ref.refs_3_ = bf16[128,3072]{1,0:T(8,128)(2,1)S(1)} collective-permute-done((bf16[128,3072]{1,0:T(8,128)(2,1)S(1)}, bf16[128,3072]{1,0:T(8,128)(2,1)S(1)}, u32[]{:S(2)}, u32[]{:S(2)}) %collective-permute-start.13) | collective-permute-done | bytes 786464 | tf_op jit(solution)/shard_map/ppermute | solution.py:55
  118.1 16.6 %all-to-all-start.3 = ((bf16[8,32,384]{2,1,0:T(8,128)(2,1)}), bf16[8,32,384]{2,1,0:T(8,128)(2,1)}, u32[]{:S(2)}, u32[]{:S(2)}) async-start(bf16[8,32,384]{2,1,0:T(8,128)(2,1)} %bitcast.23), calls=%async_computation.3 | async-start | bytes 393216 | tf_op jit(solution)/shard_map/all_to_all | solution.py:337
  135.5 5.3 %all-to-all-done.3 = bf16[8,32,384]{2,1,0:T(8,128)(2,1)} async-done(((bf16[8,32,384]{2,1,0:T(8,128)(2,1)}), bf16[8,32,384]{2,1,0:T(8,128)(2,1)}, u32[]{:S(2)}, u32[]{:S(2)}) %all-to-all-start.3) | async-done | bytes 196640 | tf_op jit(solution)/shard_map/all_to_all | solution.py:337
  140.8 0.9 copy-done.8
  141.7 2.4 %update.1 = (f32[384,256]{1,0:T(8,128)}, f32[384,256]{1,0:T(8,128)}, f32[384,256]{1,0:T(8,128)}) custom-call(bf16[256,384]{1,0:T(8,128)(2,1)} %bitcast.11.grads_ref, f32[256,128]{1,0:T(8,128)S(1)} %bitcast.21, f32[384,256]{1,0:T(8,128)S(1)} %copy-done.4, f32[384,256]{1,0:T(8,128)S(1)} %copy-done.5, f32[384,256]{1,0:T(8,128)S(1)} %copy-done.6), custom_call_target="tpu_custom_call" | custom-call | tf_op jit(solution)/shard_map/update/pallas_call | solution.py:298
  144.1 0.9 copy-done.2
  145.4 2.1 %collective-permute-done.17.refs_5_ = bf16[128,3072]{1,0:T(8,128)(2,1)S(1)} collective-permute-done((bf16[128,3072]{1,0:T(8,128)(2,1)}, bf16[128,3072]{1,0:T(8,128)(2,1)S(1)}, u32[]{:S(2)}, u32[]{:S(2)}) %collective-permute-start.17) | collective-permute-done | bytes 786464 | tf_op jit(solution)/shard_map/ppermute | solution.py:41
  147.5 4.1 %copy-done.1 = bf16[448,12288]{1,0:T(8,128)(2,1)S(1)} copy-done((bf16[448,12288]{1,0:T(8,128)(2,1)S(1)}, bf16[448,12288]{1,0:T(8,128)(2,1)}, u32[]{:S(2)}) %copy-start.1) | copy-done | bytes 11010072
  151.6 1.1 copy-done.3
  152.8 6.6 %forward.1 = bf16[448,256]{1,0:T(8,128)(2,1)} custom-call(s32[3]{0:T(128)S(1)} %pad_add_fusion.place_ref, bf16[448,12288]{1,0:T(8,128)(2,1)S(1)} %copy-done.1, bf16[128,3072]{1,0:T(8,128)(2,1)S(1)} %constant_dynamic-update-slice_fusion.refs_0_, bf16[128,3072]{1,0:T(8,128)(2,1)S(1)} %copy-done.3, bf16[128,3072]{1,0:T(8,128)(2,1)} %collective-permute-done.15.refs_2_, ...), custom_call_target="tpu_custom_call" | custom-call | flops 2818572288 | bytes 17530880 | tf_op jit(solution)/shard_map/forward/pallas_call | solution.py:197
  (53 shorter events, 4.9 us)
Async XLA Ops:
  7.2 4.2 %copy-start = (bf16[448,12288]{1,0:T(8,128)(2,1)}, bf16[448,12288]{1,0:T(8,128)(2,1)S(1)}, u32[]{:S(2)}) copy-start(bf16[448,12288]{1,0:T(8,128)(2,1)S(1)} %get-tuple-element.31.held) | copy-start | bytes 33030148
  11.3 2.6 %collective-permute-start.1 = (bf16[128,3072]{1,0:T(8,128)(2,1)S(1)}, bf16[128,3072]{1,0:T(8,128)(2,1)S(1)}, u32[]{:S(2)}, u32[]{:S(2)}) collective-permute-start(bf16[128,3072]{1,0:T(8,128)(2,1)S(1)} %get-tuple-element.21), channel_id=1, source_target_pairs={{0,32},{32,0},{1,33},{33,1},{2,34},{34,2},{3,35},{35,3},{4,36},{36... | collective-permute-start | bytes 2359304 | tf_op jit(solution)/shard_map/ppermute | solution.py:41
  12.0 5.1 %collective-permute-start.3 = (bf16[128,3072]{1,0:T(8,128)(2,1)S(1)}, bf16[128,3072]{1,0:T(8,128)(2,1)S(1)}, u32[]{:S(2)}, u32[]{:S(2)}) collective-permute-start(bf16[128,3072]{1,0:T(8,128)(2,1)S(1)} %get-tuple-element.23), channel_id=1, source_target_pairs={{0,32},{32,0},{1,33},{33,1},{2,34},{34,2},{3,35},{35,3},{4,36},{36... | collective-permute-start | bytes 2359304 | tf_op jit(solution)/shard_map/ppermute | solution.py:41
  12.0 8.3 %collective-permute-start = (bf16[128,3072]{1,0:T(8,128)(2,1)S(1)}, bf16[128,3072]{1,0:T(8,128)(2,1)S(1)}, u32[]{:S(2)}, u32[]{:S(2)}) collective-permute-start(bf16[128,3072]{1,0:T(8,128)(2,1)S(1)} %get-tuple-element.19), channel_id=1, source_target_pairs={{0,32},{32,0},{1,33},{33,1},{2,34},{34,2},{3,35},{35,3},{4,36},{36... | collective-permute-start | bytes 2359304 | tf_op jit(solution)/shard_map/ppermute | solution.py:41
  12.5 5.3 %collective-permute-start.5 = (bf16[128,3072]{1,0:T(8,128)(2,1)S(1)}, bf16[128,3072]{1,0:T(8,128)(2,1)S(1)}, u32[]{:S(2)}, u32[]{:S(2)}) collective-permute-start(bf16[128,3072]{1,0:T(8,128)(2,1)S(1)} %get-tuple-element.25), channel_id=1, source_target_pairs={{0,32},{32,0},{1,33},{33,1},{2,34},{34,2},{3,35},{35,3},{4,36},{36... | collective-permute-start | bytes 2359304 | tf_op jit(solution)/shard_map/ppermute | solution.py:41
  14.1 12.5 %collective-permute-start.2 = (bf16[128,3072]{1,0:T(8,128)(2,1)S(1)}, bf16[128,3072]{1,0:T(8,128)(2,1)S(1)}, u32[]{:S(2)}, u32[]{:S(2)}) collective-permute-start(bf16[128,3072]{1,0:T(8,128)(2,1)S(1)} %add_convert_fusion.3), channel_id=1, source_target_pairs={{0,16},{8,24},{16,0},{24,8},{32,160},{40,168},{48,176},{56,184},{6... | collective-permute-start | bytes 2359304 | tf_op jit(solution)/shard_map/ppermute | solution.py:55
  17.3 17.7 %collective-permute-start.4 = (bf16[128,3072]{1,0:T(8,128)(2,1)S(1)}, bf16[128,3072]{1,0:T(8,128)(2,1)S(1)}, u32[]{:S(2)}, u32[]{:S(2)}) collective-permute-start(bf16[128,3072]{1,0:T(8,128)(2,1)S(1)} %add_convert_fusion.2), channel_id=1, source_target_pairs={{0,8},{8,16},{16,24},{24,0},{32,96},{40,104},{48,112},{56,120},{64... | collective-permute-start | bytes 2359304 | tf_op jit(solution)/shard_map/ppermute | solution.py:55
  18.0 17.7 %collective-permute-start.6 = (bf16[128,3072]{1,0:T(8,128)(2,1)S(1)}, bf16[128,3072]{1,0:T(8,128)(2,1)S(1)}, u32[]{:S(2)}, u32[]{:S(2)}) collective-permute-start(bf16[128,3072]{1,0:T(8,128)(2,1)S(1)} %add_convert_fusion.1), channel_id=1, source_target_pairs={{0,24},{8,0},{16,8},{24,16},{32,224},{40,232},{48,240},{56,248},{6... | collective-permute-start | bytes 2359304 | tf_op jit(solution)/shard_map/ppermute | solution.py:55
  36.3 47.9 %copy-start.4 = (f32[384,256]{1,0:T(8,128)S(1)}, f32[384,256]{1,0:T(8,128)}, u32[]{:S(2)}) copy-start(f32[384,256]{1,0:T(8,128)} %refs_0_.3) | copy-start | bytes 1179652
  36.3 47.9 %copy-start.5 = (f32[384,256]{1,0:T(8,128)S(1)}, f32[384,256]{1,0:T(8,128)}, u32[]{:S(2)}) copy-start(f32[384,256]{1,0:T(8,128)} %refs_1_.3) | copy-start | bytes 1179652
  36.3 47.8 %copy-start.6 = (f32[384,256]{1,0:T(8,128)S(1)}, f32[384,256]{1,0:T(8,128)}, u32[]{:S(2)}) copy-start(f32[384,256]{1,0:T(8,128)} %refs_2_.3) | copy-start | bytes 1179652
  36.4 6.4 %collective-permute-start.7 = (bf16[32,3072]{1,0:T(8,128)(2,1)S(1)}, bf16[32,3072]{1,0:T(8,128)(2,1)S(1)}, u32[]{:S(2)}, u32[]{:S(2)}) collective-permute-start(bf16[32,3072]{1,0:T(8,128)(2,1)S(1)} %get-tuple-element.32), channel_id=1, source_target_pairs={{0,128},{8,136},{16,144},{24,152},{32,48},{40,56},{48,32},{56,40},... | collective-permute-start | bytes 589832 | tf_op jit(solution)/shard_map/ppermute | solution.py:55
  38.3 6.6 %collective-permute-start.9 = (bf16[32,3072]{1,0:T(8,128)(2,1)S(1)}, bf16[32,3072]{1,0:T(8,128)(2,1)S(1)}, u32[]{:S(2)}, u32[]{:S(2)}) collective-permute-start(bf16[32,3072]{1,0:T(8,128)(2,1)S(1)} %get-tuple-element.33), channel_id=1, source_target_pairs={{0,192},{8,200},{16,208},{24,216},{32,56},{40,32},{48,40},{56,48},... | collective-permute-start | bytes 589832 | tf_op jit(solution)/shard_map/ppermute | solution.py:55
  39.5 5.5 %collective-permute-start.8 = (bf16[32,3072]{1,0:T(8,128)(2,1)S(1)}, bf16[32,3072]{1,0:T(8,128)(2,1)S(1)}, u32[]{:S(2)}, u32[]{:S(2)}) collective-permute-start(bf16[32,3072]{1,0:T(8,128)(2,1)S(1)} %get-tuple-element.34), channel_id=1, source_target_pairs={{0,64},{8,72},{16,80},{24,88},{32,40},{40,48},{48,56},{56,32},{64,... | collective-permute-start | bytes 589832 | tf_op jit(solution)/shard_map/ppermute | solution.py:55
  84.2 22.0 %copy-start.7 = (f32[256,1,128]{2,1,0:T(1,128)}, f32[256,1,128]{2,1,0:T(1,128)S(1)}, u32[]{:S(2)}) copy-start(f32[256,1,128]{2,1,0:T(1,128)S(1)} %all_to_all.61) | copy-start | bytes 393220
  97.3 8.9 %collective-permute-start.12 = (bf16[32,3072]{1,0:T(8,128)(2,1)S(1)}, bf16[32,3072]{1,0:T(8,128)(2,1)S(1)}, u32[]{:S(2)}, u32[]{:S(2)}) collective-permute-start(bf16[32,3072]{1,0:T(8,128)(2,1)S(1)} %bitcast.26), channel_id=1, source_target_pairs={{0,192},{8,200},{16,208},{24,216},{32,56},{40,32},{48,40},{56,48},... | collective-permute-start | bytes 589832 | tf_op jit(solution)/shard_map/ppermute | solution.py:55
  98.5 7.6 %collective-permute-start.11 = (bf16[32,3072]{1,0:T(8,128)(2,1)S(1)}, bf16[32,3072]{1,0:T(8,128)(2,1)S(1)}, u32[]{:S(2)}, u32[]{:S(2)}) collective-permute-start(bf16[32,3072]{1,0:T(8,128)(2,1)S(1)} %bitcast.27), channel_id=1, source_target_pairs={{0,128},{8,136},{16,144},{24,152},{32,48},{40,56},{48,32},{56,40},... | collective-permute-start | bytes 589832 | tf_op jit(solution)/shard_map/ppermute | solution.py:55
  98.5 7.6 %collective-permute-start.10 = (bf16[32,3072]{1,0:T(8,128)(2,1)S(1)}, bf16[32,3072]{1,0:T(8,128)(2,1)S(1)}, u32[]{:S(2)}, u32[]{:S(2)}) collective-permute-start(bf16[32,3072]{1,0:T(8,128)(2,1)S(1)} %bitcast.28), channel_id=1, source_target_pairs={{0,64},{8,72},{16,80},{24,88},{32,40},{40,48},{48,56},{56,32},{64,... | collective-permute-start | bytes 589832 | tf_op jit(solution)/shard_map/ppermute | solution.py:55
  106.2 11.2 %collective-permute-start.13 = (bf16[128,3072]{1,0:T(8,128)(2,1)S(1)}, bf16[128,3072]{1,0:T(8,128)(2,1)S(1)}, u32[]{:S(2)}, u32[]{:S(2)}) collective-permute-start(bf16[128,3072]{1,0:T(8,128)(2,1)S(1)} %constant_dynamic-update-slice_fusion.refs_0_), channel_id=1, source_target_pairs={{0,24},{8,0},{16,8},{24,16},{32,224},{40,232},{48,240},{56,248},{6... | collective-permute-start | bytes 2359304 | tf_op jit(solution)/shard_map/ppermute | solution.py:55
  107.1 28.2 %collective-permute-start.15 = (bf16[128,3072]{1,0:T(8,128)(2,1)S(1)}, bf16[128,3072]{1,0:T(8,128)(2,1)}, u32[]{:S(2)}, u32[]{:S(2)}) collective-permute-start(bf16[128,3072]{1,0:T(8,128)(2,1)S(1)} %constant_dynamic-update-slice_fusion.refs_0_), channel_id=1, source_target_pairs={{0,16},{8,24},{16,0},{24,8},{32,160},{40,168},{48,176},{56,184},{6... | collective-permute-start | bytes 2359304 | tf_op jit(solution)/shard_map/ppermute | solution.py:55
  108.4 35.7 %collective-permute-start.14 = (bf16[128,3072]{1,0:T(8,128)(2,1)S(1)}, bf16[128,3072]{1,0:T(8,128)(2,1)S(1)}, u32[]{:S(2)}, u32[]{:S(2)}) collective-permute-start(bf16[128,3072]{1,0:T(8,128)(2,1)S(1)} %constant_dynamic-update-slice_fusion.refs_0_), channel_id=1, source_target_pairs={{0,8},{8,16},{16,24},{24,0},{32,96},{40,104},{48,112},{56,120},{64... | collective-permute-start | bytes 2359304 | tf_op jit(solution)/shard_map/ppermute | solution.py:55
  117.4 0.7 copy-start.9
  118.1 22.6 %all-to-all-start.3 = ((bf16[8,32,384]{2,1,0:T(8,128)(2,1)}), bf16[8,32,384]{2,1,0:T(8,128)(2,1)}, u32[]{:S(2)}, u32[]{:S(2)}) async-start(bf16[8,32,384]{2,1,0:T(8,128)(2,1)} %bitcast.23), calls=%async_computation.3 | async-start | bytes 393216 | tf_op jit(solution)/shard_map/all_to_all | solution.py:337
  134.8 10.6 %collective-permute-start.16 = (bf16[128,3072]{1,0:T(8,128)(2,1)S(1)}, bf16[128,3072]{1,0:T(8,128)(2,1)}, u32[]{:S(2)}, u32[]{:S(2)}) collective-permute-start(bf16[128,3072]{1,0:T(8,128)(2,1)S(1)} %constant_dynamic-update-slice_fusion.refs_0_), channel_id=1, source_target_pairs={{0,32},{32,0},{1,33},{33,1},{2,34},{34,2},{3,35},{35,3},{4,36},{36... | collective-permute-start | bytes 2359304 | tf_op jit(solution)/shard_map/ppermute | solution.py:41
  135.0 10.4 %collective-permute-start.19 = (bf16[128,3072]{1,0:T(8,128)(2,1)S(1)}, bf16[128,3072]{1,0:T(8,128)(2,1)}, u32[]{:S(2)}, u32[]{:S(2)}) collective-permute-start(bf16[128,3072]{1,0:T(8,128)(2,1)S(1)} %collective-permute-done.13.after_ref.refs_3_), channel_id=1, source_target_pairs={{0,32},{32,0},{1,33},{33,1},{2,34},{34,2},{3,35},{35,3},{4,36},{36... | collective-permute-start | bytes 2359304 | tf_op jit(solution)/shard_map/ppermute | solution.py:41
  135.3 10.1 %collective-permute-start.18 = (bf16[128,3072]{1,0:T(8,128)(2,1)}, bf16[128,3072]{1,0:T(8,128)(2,1)}, u32[]{:S(2)}, u32[]{:S(2)}) collective-permute-start(bf16[128,3072]{1,0:T(8,128)(2,1)} %collective-permute-done.15.refs_2_), channel_id=1, source_target_pairs={{0,32},{32,0},{1,33},{33,1},{2,34},{34,2},{3,35},{35,3},{4,36},{36... | collective-permute-start | bytes 2359304 | tf_op jit(solution)/shard_map/ppermute | solution.py:41
  140.8 0.9 copy-start.8
  144.1 0.9 copy-start.2
  145.0 2.5 %collective-permute-start.17 = (bf16[128,3072]{1,0:T(8,128)(2,1)}, bf16[128,3072]{1,0:T(8,128)(2,1)S(1)}, u32[]{:S(2)}, u32[]{:S(2)}) collective-permute-start(bf16[128,3072]{1,0:T(8,128)(2,1)} %tie.1.refs_1_), channel_id=1, source_target_pairs={{0,32},{32,0},{1,33},{33,1},{2,34},{34,2},{3,35},{35,3},{4,36},{36... | collective-permute-start | bytes 2359304 | tf_op jit(solution)/shard_map/ppermute | solution.py:41
  147.5 4.1 %copy-start.1 = (bf16[448,12288]{1,0:T(8,128)(2,1)S(1)}, bf16[448,12288]{1,0:T(8,128)(2,1)}, u32[]{:S(2)}) copy-start(bf16[448,12288]{1,0:T(8,128)(2,1)} %copy-done) | copy-start | bytes 33030148
  151.6 1.1 copy-start.3

commit v5 on v3

--- a/solution.py
+++ b/solution.py
@@ -55,7 +55,7 @@
     return lax.ppermute(value, ("y", "core", "x"), pairs)
 
 
-VMEM_LIMIT = 24 * 2**20
+MIB = 2**20
 
 
 def in_hbm(value):
@@ -66,14 +66,14 @@
     return [pl.BlockSpec(memory_space=pltpu.VMEM)] * count
 
 
-def kernel_call(body, name, in_specs, out_shape, scratch=(), flops=0, moved=0):
+def kernel_call(body, name, in_specs, out_shape, scratch=(), flops=0, moved=0, vmem=8 * MIB):
     return pl.pallas_call(
         body,
         in_specs=in_specs,
         out_specs=in_vmem(len(out_shape)),
         out_shape=out_shape,
         scratch_shapes=list(scratch),
-        compiler_params=pltpu.CompilerParams(vmem_limit_bytes=VMEM_LIMIT),
+        compiler_params=pltpu.CompilerParams(vmem_limit_bytes=vmem),
         cost_estimate=pl.CostEstimate(flops=flops, bytes_accessed=moved, transcendentals=0),
         name=name,
     )
@@ -149,6 +149,7 @@
         ],
         2 * cols * count * width,
         2 * (count * width + cols * width + cols * count),
+        16 * MIB,
     )(place, in_hbm(cotangent), in_hbm(tokens))
     return out[:NX], out[NX : 2 * NX], out[2 * NX]
 
@@ -202,6 +203,7 @@
         [pltpu.VMEM((NX, cols, width // NX), bf16), pltpu.VMEM((count, cols), f32)],
         2 * cols * count * width,
         2 * (count * width + cols * width + cols * count),
+        16 * MIB,
     )(place, held, *own, *other)[0]
 
 
@@ -226,7 +228,7 @@
 
 
 def weight_kernel(count, place_ref, piece_ref, squares_ref, *refs):
-    states, (out_ref, wide, turned) = refs[:3], refs[3:]
+    states, (out_ref, wide, turned) = refs[:3], refs[4:]
     y, c = place_ref[0], place_ref[1]
     unit, rows = piece_ref.shape
     half = wide.shape[1]
@@ -243,49 +245,44 @@
         out_ref[z * unit : (z + 1) * unit, :] = mine
 
 
-def weight_piece(place, piece, squares, states, count):
+def weight_piece(place, piece, squares, states, after, count):
     unit, rows = piece.shape
     half = states[0].shape[1] // 2
     return kernel_call(
         functools.partial(weight_kernel, count),
         "weight_piece",
-        [pl.BlockSpec(memory_space=pltpu.SMEM)] + in_vmem(2 + len(states)),
+        [pl.BlockSpec(memory_space=pltpu.SMEM)]
+        + in_vmem(2 + len(states))
+        + [pl.BlockSpec(memory_space=pl.ANY)],
         [jax.ShapeDtypeStruct((NZ * unit, rows), bf16)],
         [pltpu.VMEM((rows, half), f32), pltpu.VMEM((half, rows), f32)],
-    )(place, piece, squares, *states)[0]
-
-
-def spread_kernel(piece_ref, after_ref, out_ref):
-    del after_ref
-    unit = piece_ref.shape[0]
-    for i in range(out_ref.shape[0] // unit):
-        out_ref[i * unit : (i + 1) * unit, :] = piece_ref[...]
-
-
-def spread(piece, copies, after):
-    unit, rows = piece.shape
-    return kernel_call(
-        spread_kernel,
-        "spread",
-        in_vmem(1) + [pl.BlockSpec(memory_space=pl.ANY)],
-        [jax.ShapeDtypeStruct((copies * unit, rows), bf16)],
-    )(piece, after)[0]
-
-
-def update_kernel(count, grads_ref, squares_ref, *refs):
+    )(place, piece, squares, *states, after)[0]
+
+
+def update_kernel(count, place_ref, own_ref, other_ref, squares_ref, *refs):
+    states, outs, turned = refs[:3], refs[3:6], refs[6]
+    y, c = place_ref[0], place_ref[1]
+    half = turned.shape[0] // 2
+    unit = half // NY
+    for ref, core in ((own_ref, c), (other_ref, 1 - c)):
+        for e in range(NY):
+            at = pl.multiple_of(core * half + lax.rem(y + NY - e, NY) * unit, unit)
+            turned[pl.ds(at, unit), :] = ref[e * unit : (e + 1) * unit, :].astype(f32)
     total = jnp.sum(squares_ref[:, :1])
-    new = apply_update(grads_ref[...].astype(f32).T, *[ref[...] for ref in refs[:3]], total, count)
-    for ref, value in zip(refs[3:], new):
+    new = apply_update(turned[...].T, *[ref[...] for ref in states], total, count)
+    for ref, value in zip(outs, new):
         ref[...] = value
 
 
-def update(grads, squares, states, count):
+def update(place, own, other, squares, states, count):
+    rows, cols = states[0].shape
     return kernel_call(
         functools.partial(update_kernel, count),
         "update",
-        in_vmem(2 + len(states)),
+        [pl.BlockSpec(memory_space=pltpu.SMEM)] + in_vmem(3 + len(states)),
         [jax.ShapeDtypeStruct(states[0].shape, f32)] * 3,
-    )(grads, squares, *states)
+        [pltpu.VMEM((cols, rows), f32)],
+    )(place, own, other, squares, *states)
 
 
 def add(*parts):
@@ -313,16 +310,17 @@
     plane = add(line[:unit], *got).astype(bf16)
     planes = lax.all_to_all(plane, "z", 1, 0, tiled=True)
     piece, squares = plane_sum(planes)
+    grads = jnp.concatenate([piece] + [send(piece, "y", d) for d in (1, 2, 3)], 0)
     squares = lax.all_to_all(squares, NAMES, 0, 0, tiled=True)
 
-    weight = weight_piece(place, piece, squares, states, count)
+    weight = weight_piece(place, piece, squares, states, grads, count)
+    grads_other = send(grads, "core", 1)
     plane = lax.all_to_all(weight, "z", 0, 1, tiled=True)
     line = jnp.concatenate([plane] + [routed(plane, d, False) for d in (1, 2, 3)], 0)
     own = [line] + [routed(line, d, True) for d in (1, 2, 3)]
     other = [send(part, "core", 1) for part in own]
 
-    grads = lax.all_to_all(spread(piece, NC * NY, other[0]), ("core", "y"), 0, 0, tiled=True)
-    master_new, first_new, second_new = update(grads, squares, states, count)
+    master_new, first_new, second_new = update(place, grads, grads_other, squares, states, count)
     activations = forward(place, held, own, other)
     return (master_new, first_new, second_new, activations)
 

time: 146 us -> 154 us (1.055)
  blocking collectives: 59.2 us -> 28.6 us
  waiting for transfers between devices: 39.6 us -> 54.7 us
  starting transfers between devices: 29.9 us -> 43.6 us
  local copies, waits for them, and re-layouts: 0.16 us -> 8.51 us
    all_to_all x2 -> x0, blocking collectives: 30.6 us -> none  [the longest x1 21.9 us: body(): squares = lax.all_to_all(squares, NAMES, 0, 0, tiled=True)]
    all_to_all x0 -> x1, waiting for transfers between devices: none -> 12.9 us  [body(): squares = lax.all_to_all(squares, NAMES, 0, 0, tiled=True)]
    all_to_all x0 -> x1, starting transfers between devices: none -> 11.2 us  [body(): squares = lax.all_to_all(squares, NAMES, 0, 0, tiled=True)]
    unnamed x9 -> x16, local copies, waits for them, and re-layouts: 0.06 us -> 8.4 us
    ppermute x8 -> x12, starting transfers between devices: 19.8 us -> 22.4 us  [send(): return lax.ppermute(value, axis, [(i, (i + step) % n) for i in range(n)])]
    ppermute x8 -> x12, waiting for transfers between devices: 2.54 us -> 4.72 us  [send(): return lax.ppermute(value, axis, [(i, (i + step) % n) for i in range(n)])]
  transfers between devices with their start and end apart: 20 -> 25, of which waited for: 10 -> 12; matrix products, arithmetic and copies ran while one was open for 0% -> 0% of each run, Pallas kernels for 1% -> 1%
where the time goes in v5:
time: 154 us; the launch traced here: 153 us
  waiting for transfers between devices  54.7 us (36%)
  starting transfers between devices  43.6 us (28%)
  blocking collectives  28.6 us (19%)
  Pallas kernels  15.7 us (10%)
  local copies, waits for them, and re-layouts  8.51 us (6%)
    ppermute x12, waiting for transfers between devices, routed(): return lax.ppermute(value, ('y', 'core', 'x'), pairs)  37.1 us
    ppermute x12, starting transfers between devices, send(): return lax.ppermute(value, axis, [(i, (i + step) % n) for i in range(n)])  22.4 us
    all_to_all x1, blocking collectives, body(): planes = lax.all_to_all(plane, 'z', 1, 0, tiled=True)  16.6 us
    all_to_all x1, waiting for transfers between devices, body(): squares = lax.all_to_all(squares, NAMES, 0, 0, tiled=True)  12.9 us
    all_to_all x1, blocking collectives, body(): plane = lax.all_to_all(weight, 'z', 0, 1, tiled=True)  12 us
    all_to_all x1, starting transfers between devices, body(): squares = lax.all_to_all(squares, NAMES, 0, 0, tiled=True)  11.2 us
    ppermute x12, starting transfers between devices, routed(): return lax.ppermute(value, ('y', 'core', 'x'), pairs)  10 us
    unnamed x16, local copies, waits for them, and re-layouts  8.4 us
  transfers between devices with their start and end apart: 25, of which 12 were waited for; matrix products, arithmetic and copies ran while one was open for 0% of the time, Pallas kernels for 1%

profile of v5, /device:TPU:1, one launch (start us, length us, event | category | flops | bytes accessed | tf_op | source)
XLA Modules:
  0.0 153.4 jit_solution(2678761914044272914)
XLA Ops:
  0.7 6.6 %partial_terms.1 = (bf16[128,3072]{1,0:T(8,128)(2,1)S(1)}, bf16[128,3072]{1,0:T(8,128)(2,1)S(1)}, bf16[128,3072]{1,0:T(8,128)(2,1)S(1)}, bf16[128,3072]{1,0:T(8,...) custom-call(s32[3]{0:T(128)S(1)} %pad_add_fusion.place_ref, ...), custom_call_target="tpu_custom_call" | custom-call | flops 2818572288 | bytes 17530880 | tf_op jit(solution)/shard_map/partial_terms/pallas_call | solution.py:135
  7.3 4.2 %copy-done = bf16[448,12288]{1,0:T(8,128)(2,1)} copy-done((bf16[448,12288]{1,0:T(8,128)(2,1)}, bf16[448,12288]{1,0:T(8,128)(2,1)S(1)}, u32[]{:S(2)}) %copy-start) | copy-done | bytes 11010072
  11.5 3.2 %collective-permute-start.1 = (bf16[128,3072]{1,0:T(8,128)(2,1)S(1)}, bf16[128,3072]{1,0:T(8,128)(2,1)S(1)}, u32[]{:S(2)}, u32[]{:S(2)}) collective-permute-start(bf16[128,3072]{1,0:T(8,128)(2,1)S(1)} %get-tuple-element.21), channel_id=1, source_target_pairs={{0,32},{32,0},{1,33},{33,1},{2,34},{34,2},{3,35},{35,3},{4,36},{36... | collective-permute-start | bytes 2359304 | tf_op jit(solution)/shard_map/ppermute | solution.py:41
  15.2 1.4 collective-permute-done.1
  16.8 1.3 collective-permute-start.2
  18.8 1.2 collective-permute-done.5
  20.2 1.1 collective-permute-start.6
  21.3 8.3 %collective-permute-done.2 = bf16[128,3072]{1,0:T(8,128)(2,1)S(1)} collective-permute-done((bf16[128,3072]{1,0:T(8,128)(2,1)S(1)}, bf16[128,3072]{1,0:T(8,128)(2,1)S(1)}, u32[]{:S(2)}, u32[]{:S(2)}) %collective-permute-start.2) | collective-permute-done | bytes 786464 | tf_op jit(solution)/shard_map/ppermute | solution.py:55
  29.6 8.4 %collective-permute-done.4 = bf16[128,3072]{1,0:T(8,128)(2,1)S(1)} collective-permute-done((bf16[128,3072]{1,0:T(8,128)(2,1)S(1)}, bf16[128,3072]{1,0:T(8,128)(2,1)S(1)}, u32[]{:S(2)}, u32[]{:S(2)}) %collective-permute-start.4) | collective-permute-done | bytes 786464 | tf_op jit(solution)/shard_map/ppermute | solution.py:55
  38.7 1.5 collective-permute-start.7
  40.2 0.9 collective-permute-start.9
  41.6 3.5 %collective-permute-done.7 = bf16[32,3072]{1,0:T(8,128)(2,1)S(1)} collective-permute-done((bf16[32,3072]{1,0:T(8,128)(2,1)S(1)}, bf16[32,3072]{1,0:T(8,128)(2,1)S(1)}, u32[]{:S(2)}, u32[]{:S(2)}) %collective-permute-start.7) | collective-permute-done | bytes 196640 | tf_op jit(solution)/shard_map/ppermute | solution.py:55
  45.9 1.3 collective-permute-done.8
  47.4 16.6 %all_to_all.49 = bf16[32,8,384]{2,0,1:T(8,128)(2,1)S(1)} all-to-all(bf16[32,8,384]{2,0,1:T(8,128)(2,1)S(1)} %bitcast.26), channel_id=1, replica_groups=mesh['y'=4,'core'=2,'x'=4,'z'=8] {'z'}, dimensions={1} | all-to-all | bytes 393216 | tf_op jit(solution)/shard_map/all_to_all | solution.py:311
  64.7 1.9 %collective-permute-start.12 = (bf16[32,384]{1,0:T(8,128)(2,1)S(1)}, bf16[32,384]{1,0:T(8,128)(2,1)S(1)}, u32[]{:S(2)}, u32[]{:S(2)}) collective-permute-start(bf16[32,384]{1,0:T(8,128)(2,1)S(1)} %get-tuple-element.26.piece_ref), channel_id=1, source_target_pairs={{0,192},{64,0},{128,64},{192,128},{1,193},{65,1},{129,65},{193,129... | collective-permute-start | bytes 73736 | tf_op jit(solution)/shard_map/ppermute | solution.py:41
  67.5 11.2 %all-to-all-start.1 = ((f32[256,1,128]{2,1,0:T(1,128)}), f32[256,1,128]{2,1,0:T(1,128)S(1)}, u32[]{:S(2)}, u32[]{:S(2)}) async-start(f32[256,1,128]{2,1,0:T(1,128)} %bitcast.6), calls=%async_computation.1 | async-start | bytes 262144 | tf_op jit(solution)/shard_map/all_to_all | solution.py:314
  78.7 12.9 %all-to-all-done.1 = f32[256,1,128]{2,1,0:T(1,128)S(1)} async-done(((f32[256,1,128]{2,1,0:T(1,128)}), f32[256,1,128]{2,1,0:T(1,128)S(1)}, u32[]{:S(2)}, u32[]{:S(2)}) %all-to-all-start.1) | async-done | bytes 131104 | tf_op jit(solution)/shard_map/all_to_all | solution.py:314
  91.6 1.1 weight_piece.1
  92.7 12.0 %all_to_all.50 = bf16[8,32,384]{2,1,0:T(8,128)(2,1)S(1)} all-to-all(bf16[8,32,384]{2,1,0:T(8,128)(2,1)S(1)} %bitcast.20), channel_id=1, replica_groups=mesh['y'=4,'core'=2,'x'=4,'z'=8] {'z'}, dimensions={0} | all-to-all | bytes 393216 | tf_op jit(solution)/shard_map/all_to_all | solution.py:318
  104.8 2.1 %collective-permute-start.15 = (bf16[32,3072]{1,0:T(8,128)(2,1)S(1)}, bf16[32,3072]{1,0:T(8,128)(2,1)S(1)}, u32[]{:S(2)}, u32[]{:S(2)}) collective-permute-start(bf16[32,3072]{1,0:T(8,128)(2,1)S(1)} %bitcast.23), channel_id=1, source_target_pairs={{0,128},{8,136},{16,144},{24,152},{32,48},{40,56},{48,32},{56,40},... | collective-permute-start | bytes 589832 | tf_op jit(solution)/shard_map/ppermute | solution.py:55
  106.9 6.4 %collective-permute-done.14 = bf16[32,3072]{1,0:T(8,128)(2,1)S(1)} collective-permute-done((bf16[32,3072]{1,0:T(8,128)(2,1)S(1)}, bf16[32,3072]{1,0:T(8,128)(2,1)S(1)}, u32[]{:S(2)}, u32[]{:S(2)}) %collective-permute-start.14) | collective-permute-done | bytes 196640 | tf_op jit(solution)/shard_map/ppermute | solution.py:55
  114.1 1.4 collective-permute-start.18
  115.5 4.3 %collective-permute-start.20 = (bf16[128,3072]{1,0:T(8,128)(2,1)S(1)}, bf16[128,3072]{1,0:T(8,128)(2,1)S(1)}, u32[]{:S(2)}, u32[]{:S(2)}) collective-permute-start(bf16[128,3072]{1,0:T(8,128)(2,1)S(1)} %constant_dynamic-update-slice_fusion.4.refs_0_), channel_id=1, source_target_pairs={{0,32},{32,0},{1,33},{33,1},{2,34},{34,2},{3,35},{35,3},{4,36},{36... | collective-permute-start | bytes 2359304 | tf_op jit(solution)/shard_map/ppermute | solution.py:41
  119.8 4.8 %collective-permute-done.19.refs_3_ = bf16[128,3072]{1,0:T(8,128)(2,1)S(1)} collective-permute-done((bf16[128,3072]{1,0:T(8,128)(2,1)S(1)}, bf16[128,3072]{1,0:T(8,128)(2,1)S(1)}, u32[]{:S(2)}, u32[]{:S(2)}) %collective-permute-start.19) | collective-permute-done | bytes 786464 | tf_op jit(solution)/shard_map/ppermute | solution.py:55
  124.6 4.5 %collective-permute-start.23 = (bf16[128,3072]{1,0:T(8,128)(2,1)S(1)}, bf16[128,3072]{1,0:T(8,128)(2,1)S(1)}, u32[]{:S(2)}, u32[]{:S(2)}) collective-permute-start(bf16[128,3072]{1,0:T(8,128)(2,1)S(1)} %collective-permute-done.19.refs_3_), channel_id=1, source_target_pairs={{0,32},{32,0},{1,33},{33,1},{2,34},{34,2},{3,35},{35,3},{4,36},{36... | collective-permute-start | bytes 2359304 | tf_op jit(solution)/shard_map/ppermute | solution.py:41
  129.2 2.4 %collective-permute-start.22 = (bf16[128,3072]{1,0:T(8,128)(2,1)S(1)}, bf16[128,3072]{1,0:T(8,128)(2,1)S(1)}, u32[]{:S(2)}, u32[]{:S(2)}) collective-permute-start(bf16[128,3072]{1,0:T(8,128)(2,1)S(1)} %collective-permute-done.18.refs_2_), channel_id=1, source_target_pairs={{0,32},{32,0},{1,33},{33,1},{2,34},{34,2},{3,35},{35,3},{4,36},{36... | collective-permute-start | bytes 2359304 | tf_op jit(solution)/shard_map/ppermute | solution.py:41
  131.5 3.6 %collective-permute-done.17.refs_1_ = bf16[128,3072]{1,0:T(8,128)(2,1)S(1)} collective-permute-done((bf16[128,3072]{1,0:T(8,128)(2,1)S(1)}, bf16[128,3072]{1,0:T(8,128)(2,1)S(1)}, u32[]{:S(2)}, u32[]{:S(2)}) %collective-permute-start.17) | collective-permute-done | bytes 786464 | tf_op jit(solution)/shard_map/ppermute | solution.py:55
  135.2 4.7 %collective-permute-start.21 = (bf16[128,3072]{1,0:T(8,128)(2,1)S(1)}, bf16[128,3072]{1,0:T(8,128)(2,1)S(1)}, u32[]{:S(2)}, u32[]{:S(2)}) collective-permute-start(bf16[128,3072]{1,0:T(8,128)(2,1)S(1)} %collective-permute-done.17.refs_1_), channel_id=1, source_target_pairs={{0,32},{32,0},{1,33},{33,1},{2,34},{34,2},{3,35},{35,3},{4,36},{36... | collective-permute-start | bytes 2359304 | tf_op jit(solution)/shard_map/ppermute | solution.py:41
  139.9 2.0 %collective-permute-done.13.other_ref = bf16[128,384]{1,0:T(8,128)(2,1)S(1)} collective-permute-done((bf16[128,384]{1,0:T(8,128)(2,1)S(1)}, bf16[128,384]{1,0:T(8,128)(2,1)S(1)}, u32[]{:S(2)}, u32[]{:S(2)}) %collective-permute-start.13) | collective-permute-done | bytes 98336 | tf_op jit(solution)/shard_map/ppermute | solution.py:41
  141.9 2.2 %update.1 = (f32[384,256]{1,0:T(8,128)}, f32[384,256]{1,0:T(8,128)}, f32[384,256]{1,0:T(8,128)}) custom-call(s32[3]{0:T(128)S(1)} %pad_add_fusion.place_ref, bf16[128,384]{1,0:T(8,128)(2,1)S(1)} %constant_dynamic-update-slice_fusion.own_ref.refs_3_, bf16[128,384]{1,0:T(8,128)(2,1)S(1)} %collective-permute-done.13.other_ref, f32[256,128]{1,0:T(8,128)S(1)} %bitcast.19, ...), custom_call_target="tpu_custom_call" | custom-call | tf_op jit(solution)/shard_map/update/pallas_call | solution.py:279
  144.2 4.1 %copy-done.1 = bf16[448,12288]{1,0:T(8,128)(2,1)S(1)} copy-done((bf16[448,12288]{1,0:T(8,128)(2,1)S(1)}, bf16[448,12288]{1,0:T(8,128)(2,1)}, u32[]{:S(2)}) %copy-start.1) | copy-done | bytes 11010072
  148.3 5.1 %forward.1 = bf16[448,256]{1,0:T(8,128)(2,1)} custom-call(s32[3]{0:T(128)S(1)} %pad_add_fusion.place_ref, bf16[448,12288]{1,0:T(8,128)(2,1)S(1)} %copy-done.1, bf16[128,3072]{1,0:T(8,128)(2,1)S(1)} %constant_dynamic-update-slice_fusion.4.refs_0_, bf16[128,3072]{1,0:T(8,128)(2,1)S(1)} %collective-permute-done.17.refs_1_, ...), custom_call_target="tpu_custom_call" | custom-call | flops 2818572288 | bytes 17530880 | tf_op jit(solution)/shard_map/forward/pallas_call | solution.py:198
  (52 shorter events, 6.4 us)
Async XLA Ops:
  7.3 4.2 %copy-start = (bf16[448,12288]{1,0:T(8,128)(2,1)}, bf16[448,12288]{1,0:T(8,128)(2,1)S(1)}, u32[]{:S(2)}) copy-start(bf16[448,12288]{1,0:T(8,128)(2,1)S(1)} %get-tuple-element.31.held) | copy-start | bytes 33030148
  11.5 5.2 %collective-permute-start.1 = (bf16[128,3072]{1,0:T(8,128)(2,1)S(1)}, bf16[128,3072]{1,0:T(8,128)(2,1)S(1)}, u32[]{:S(2)}, u32[]{:S(2)}) collective-permute-start(bf16[128,3072]{1,0:T(8,128)(2,1)S(1)} %get-tuple-element.21), channel_id=1, source_target_pairs={{0,32},{32,0},{1,33},{33,1},{2,34},{34,2},{3,35},{35,3},{4,36},{36... | collective-permute-start | bytes 2359304 | tf_op jit(solution)/shard_map/ppermute | solution.py:41
  14.7 3.4 %collective-permute-start.3 = (bf16[128,3072]{1,0:T(8,128)(2,1)S(1)}, bf16[128,3072]{1,0:T(8,128)(2,1)S(1)}, u32[]{:S(2)}, u32[]{:S(2)}) collective-permute-start(bf16[128,3072]{1,0:T(8,128)(2,1)S(1)} %get-tuple-element.23), channel_id=1, source_target_pairs={{0,32},{32,0},{1,33},{33,1},{2,34},{34,2},{3,35},{35,3},{4,36},{36... | collective-permute-start | bytes 2359304 | tf_op jit(solution)/shard_map/ppermute | solution.py:41
  14.7 6.6 %collective-permute-start = (bf16[128,3072]{1,0:T(8,128)(2,1)S(1)}, bf16[128,3072]{1,0:T(8,128)(2,1)S(1)}, u32[]{:S(2)}, u32[]{:S(2)}) collective-permute-start(bf16[128,3072]{1,0:T(8,128)(2,1)S(1)} %get-tuple-element.19), channel_id=1, source_target_pairs={{0,32},{32,0},{1,33},{33,1},{2,34},{34,2},{3,35},{35,3},{4,36},{36... | collective-permute-start | bytes 2359304 | tf_op jit(solution)/shard_map/ppermute | solution.py:41
  15.2 4.8 %collective-permute-start.5 = (bf16[128,3072]{1,0:T(8,128)(2,1)S(1)}, bf16[128,3072]{1,0:T(8,128)(2,1)S(1)}, u32[]{:S(2)}, u32[]{:S(2)}) collective-permute-start(bf16[128,3072]{1,0:T(8,128)(2,1)S(1)} %get-tuple-element.25), channel_id=1, source_target_pairs={{0,32},{32,0},{1,33},{33,1},{2,34},{34,2},{3,35},{35,3},{4,36},{36... | collective-permute-start | bytes 2359304 | tf_op jit(solution)/shard_map/ppermute | solution.py:41
  16.8 12.8 %collective-permute-start.2 = (bf16[128,3072]{1,0:T(8,128)(2,1)S(1)}, bf16[128,3072]{1,0:T(8,128)(2,1)S(1)}, u32[]{:S(2)}, u32[]{:S(2)}) collective-permute-start(bf16[128,3072]{1,0:T(8,128)(2,1)S(1)} %add_convert_fusion.3), channel_id=1, source_target_pairs={{0,16},{8,24},{16,0},{24,8},{32,160},{40,168},{48,176},{56,184},{6... | collective-permute-start | bytes 2359304 | tf_op jit(solution)/shard_map/ppermute | solution.py:55
  18.3 19.7 %collective-permute-start.4 = (bf16[128,3072]{1,0:T(8,128)(2,1)S(1)}, bf16[128,3072]{1,0:T(8,128)(2,1)S(1)}, u32[]{:S(2)}, u32[]{:S(2)}) collective-permute-start(bf16[128,3072]{1,0:T(8,128)(2,1)S(1)} %add_convert_fusion.2), channel_id=1, source_target_pairs={{0,8},{8,16},{16,24},{24,0},{32,96},{40,104},{48,112},{56,120},{64... | collective-permute-start | bytes 2359304 | tf_op jit(solution)/shard_map/ppermute | solution.py:55
  20.2 17.8 %collective-permute-start.6 = (bf16[128,3072]{1,0:T(8,128)(2,1)S(1)}, bf16[128,3072]{1,0:T(8,128)(2,1)S(1)}, u32[]{:S(2)}, u32[]{:S(2)}) collective-permute-start(bf16[128,3072]{1,0:T(8,128)(2,1)S(1)} %add_convert_fusion.1), channel_id=1, source_target_pairs={{0,24},{8,0},{16,8},{24,16},{32,224},{40,232},{48,240},{56,248},{6... | collective-permute-start | bytes 2359304 | tf_op jit(solution)/shard_map/ppermute | solution.py:55
  38.6 53.0 %copy-start.2 = (f32[384,256]{1,0:T(8,128)S(1)}, f32[384,256]{1,0:T(8,128)}, u32[]{:S(2)}) copy-start(f32[384,256]{1,0:T(8,128)} %refs_0_.3) | copy-start | bytes 1179652
  38.6 53.0 %copy-start.3 = (f32[384,256]{1,0:T(8,128)S(1)}, f32[384,256]{1,0:T(8,128)}, u32[]{:S(2)}) copy-start(f32[384,256]{1,0:T(8,128)} %refs_1_.3) | copy-start | bytes 1179652
  38.6 53.0 %copy-start.4 = (f32[384,256]{1,0:T(8,128)S(1)}, f32[384,256]{1,0:T(8,128)}, u32[]{:S(2)}) copy-start(f32[384,256]{1,0:T(8,128)} %refs_2_.3) | copy-start | bytes 1179652
  38.7 6.4 %collective-permute-start.7 = (bf16[32,3072]{1,0:T(8,128)(2,1)S(1)}, bf16[32,3072]{1,0:T(8,128)(2,1)S(1)}, u32[]{:S(2)}, u32[]{:S(2)}) collective-permute-start(bf16[32,3072]{1,0:T(8,128)(2,1)S(1)} %get-tuple-element.32), channel_id=1, source_target_pairs={{0,128},{8,136},{16,144},{24,152},{32,48},{40,56},{48,32},{56,40},... | collective-permute-start | bytes 589832 | tf_op jit(solution)/shard_map/ppermute | solution.py:55
  40.2 5.8 %collective-permute-start.9 = (bf16[32,3072]{1,0:T(8,128)(2,1)S(1)}, bf16[32,3072]{1,0:T(8,128)(2,1)S(1)}, u32[]{:S(2)}, u32[]{:S(2)}) collective-permute-start(bf16[32,3072]{1,0:T(8,128)(2,1)S(1)} %get-tuple-element.33), channel_id=1, source_target_pairs={{0,192},{8,200},{16,208},{24,216},{32,56},{40,32},{48,40},{56,48},... | collective-permute-start | bytes 589832 | tf_op jit(solution)/shard_map/ppermute | solution.py:55
  41.0 6.2 %collective-permute-start.8 = (bf16[32,3072]{1,0:T(8,128)(2,1)S(1)}, bf16[32,3072]{1,0:T(8,128)(2,1)S(1)}, u32[]{:S(2)}, u32[]{:S(2)}) collective-permute-start(bf16[32,3072]{1,0:T(8,128)(2,1)S(1)} %get-tuple-element.34), channel_id=1, source_target_pairs={{0,64},{8,72},{16,80},{24,88},{32,40},{40,48},{48,56},{56,32},{64,... | collective-permute-start | bytes 589832 | tf_op jit(solution)/shard_map/ppermute | solution.py:55
  64.7 14.0 %collective-permute-start.12 = (bf16[32,384]{1,0:T(8,128)(2,1)S(1)}, bf16[32,384]{1,0:T(8,128)(2,1)S(1)}, u32[]{:S(2)}, u32[]{:S(2)}) collective-permute-start(bf16[32,384]{1,0:T(8,128)(2,1)S(1)} %get-tuple-element.26.piece_ref), channel_id=1, source_target_pairs={{0,192},{64,0},{128,64},{192,128},{1,193},{65,1},{129,65},{193,129... | collective-permute-start | bytes 73736 | tf_op jit(solution)/shard_map/ppermute | solution.py:41
  66.6 12.0 %collective-permute-start.11 = (bf16[32,384]{1,0:T(8,128)(2,1)S(1)}, bf16[32,384]{1,0:T(8,128)(2,1)S(1)}, u32[]{:S(2)}, u32[]{:S(2)}) collective-permute-start(bf16[32,384]{1,0:T(8,128)(2,1)S(1)} %get-tuple-element.26.piece_ref), channel_id=1, source_target_pairs={{0,128},{64,192},{128,0},{192,64},{1,129},{65,193},{129,1},{193,65... | collective-permute-start | bytes 73736 | tf_op jit(solution)/shard_map/ppermute | solution.py:41
  67.0 11.6 %collective-permute-start.10 = (bf16[32,384]{1,0:T(8,128)(2,1)S(1)}, bf16[32,384]{1,0:T(8,128)(2,1)S(1)}, u32[]{:S(2)}, u32[]{:S(2)}) collective-permute-start(bf16[32,384]{1,0:T(8,128)(2,1)S(1)} %get-tuple-element.26.piece_ref), channel_id=1, source_target_pairs={{0,64},{64,128},{128,192},{192,0},{1,65},{65,129},{129,193},{193,1... | collective-permute-start | bytes 73736 | tf_op jit(solution)/shard_map/ppermute | solution.py:41
  67.5 24.2 %all-to-all-start.1 = ((f32[256,1,128]{2,1,0:T(1,128)}), f32[256,1,128]{2,1,0:T(1,128)S(1)}, u32[]{:S(2)}, u32[]{:S(2)}) async-start(f32[256,1,128]{2,1,0:T(1,128)} %bitcast.6), calls=%async_computation.1 | async-start | bytes 262144 | tf_op jit(solution)/shard_map/all_to_all | solution.py:314
  104.7 8.7 %collective-permute-start.16 = (bf16[32,3072]{1,0:T(8,128)(2,1)S(1)}, bf16[32,3072]{1,0:T(8,128)(2,1)S(1)}, u32[]{:S(2)}, u32[]{:S(2)}) collective-permute-start(bf16[32,3072]{1,0:T(8,128)(2,1)S(1)} %bitcast.22), channel_id=1, source_target_pairs={{0,192},{8,200},{16,208},{24,216},{32,56},{40,32},{48,40},{56,48},... | collective-permute-start | bytes 589832 | tf_op jit(solution)/shard_map/ppermute | solution.py:55
  104.8 8.5 %collective-permute-start.15 = (bf16[32,3072]{1,0:T(8,128)(2,1)S(1)}, bf16[32,3072]{1,0:T(8,128)(2,1)S(1)}, u32[]{:S(2)}, u32[]{:S(2)}) collective-permute-start(bf16[32,3072]{1,0:T(8,128)(2,1)S(1)} %bitcast.23), channel_id=1, source_target_pairs={{0,128},{8,136},{16,144},{24,152},{32,48},{40,56},{48,32},{56,40},... | collective-permute-start | bytes 589832 | tf_op jit(solution)/shard_map/ppermute | solution.py:55
  106.9 6.4 %collective-permute-start.14 = (bf16[32,3072]{1,0:T(8,128)(2,1)S(1)}, bf16[32,3072]{1,0:T(8,128)(2,1)S(1)}, u32[]{:S(2)}, u32[]{:S(2)}) collective-permute-start(bf16[32,3072]{1,0:T(8,128)(2,1)S(1)} %bitcast.24), channel_id=1, source_target_pairs={{0,64},{8,72},{16,80},{24,88},{32,40},{40,48},{48,56},{56,32},{64,... | collective-permute-start | bytes 589832 | tf_op jit(solution)/shard_map/ppermute | solution.py:55
  113.4 11.2 %collective-permute-start.19 = (bf16[128,3072]{1,0:T(8,128)(2,1)S(1)}, bf16[128,3072]{1,0:T(8,128)(2,1)S(1)}, u32[]{:S(2)}, u32[]{:S(2)}) collective-permute-start(bf16[128,3072]{1,0:T(8,128)(2,1)S(1)} %constant_dynamic-update-slice_fusion.4.refs_0_), channel_id=1, source_target_pairs={{0,24},{8,0},{16,8},{24,16},{32,224},{40,232},{48,240},{56,248},{6... | collective-permute-start | bytes 2359304 | tf_op jit(solution)/shard_map/ppermute | solution.py:55
  114.1 15.1 %collective-permute-start.18 = (bf16[128,3072]{1,0:T(8,128)(2,1)S(1)}, bf16[128,3072]{1,0:T(8,128)(2,1)S(1)}, u32[]{:S(2)}, u32[]{:S(2)}) collective-permute-start(bf16[128,3072]{1,0:T(8,128)(2,1)S(1)} %constant_dynamic-update-slice_fusion.4.refs_0_), channel_id=1, source_target_pairs={{0,16},{8,24},{16,0},{24,8},{32,160},{40,168},{48,176},{56,184},{6... | collective-permute-start | bytes 2359304 | tf_op jit(solution)/shard_map/ppermute | solution.py:55
  115.5 19.7 %collective-permute-start.17 = (bf16[128,3072]{1,0:T(8,128)(2,1)S(1)}, bf16[128,3072]{1,0:T(8,128)(2,1)S(1)}, u32[]{:S(2)}, u32[]{:S(2)}) collective-permute-start(bf16[128,3072]{1,0:T(8,128)(2,1)S(1)} %constant_dynamic-update-slice_fusion.4.refs_0_), channel_id=1, source_target_pairs={{0,8},{8,16},{16,24},{24,0},{32,96},{40,104},{48,112},{56,120},{64... | collective-permute-start | bytes 2359304 | tf_op jit(solution)/shard_map/ppermute | solution.py:55
  115.5 28.6 %collective-permute-start.20 = (bf16[128,3072]{1,0:T(8,128)(2,1)S(1)}, bf16[128,3072]{1,0:T(8,128)(2,1)S(1)}, u32[]{:S(2)}, u32[]{:S(2)}) collective-permute-start(bf16[128,3072]{1,0:T(8,128)(2,1)S(1)} %constant_dynamic-update-slice_fusion.4.refs_0_), channel_id=1, source_target_pairs={{0,32},{32,0},{1,33},{33,1},{2,34},{34,2},{3,35},{35,3},{4,36},{36... | collective-permute-start | bytes 2359304 | tf_op jit(solution)/shard_map/ppermute | solution.py:41
  124.6 19.5 %collective-permute-start.23 = (bf16[128,3072]{1,0:T(8,128)(2,1)S(1)}, bf16[128,3072]{1,0:T(8,128)(2,1)S(1)}, u32[]{:S(2)}, u32[]{:S(2)}) collective-permute-start(bf16[128,3072]{1,0:T(8,128)(2,1)S(1)} %collective-permute-done.19.refs_3_), channel_id=1, source_target_pairs={{0,32},{32,0},{1,33},{33,1},{2,34},{34,2},{3,35},{35,3},{4,36},{36... | collective-permute-start | bytes 2359304 | tf_op jit(solution)/shard_map/ppermute | solution.py:41
  129.2 15.0 %collective-permute-start.22 = (bf16[128,3072]{1,0:T(8,128)(2,1)S(1)}, bf16[128,3072]{1,0:T(8,128)(2,1)S(1)}, u32[]{:S(2)}, u32[]{:S(2)}) collective-permute-start(bf16[128,3072]{1,0:T(8,128)(2,1)S(1)} %collective-permute-done.18.refs_2_), channel_id=1, source_target_pairs={{0,32},{32,0},{1,33},{33,1},{2,34},{34,2},{3,35},{35,3},{4,36},{36... | collective-permute-start | bytes 2359304 | tf_op jit(solution)/shard_map/ppermute | solution.py:41
  135.2 9.0 %collective-permute-start.21 = (bf16[128,3072]{1,0:T(8,128)(2,1)S(1)}, bf16[128,3072]{1,0:T(8,128)(2,1)S(1)}, u32[]{:S(2)}, u32[]{:S(2)}) collective-permute-start(bf16[128,3072]{1,0:T(8,128)(2,1)S(1)} %collective-permute-done.17.refs_1_), channel_id=1, source_target_pairs={{0,32},{32,0},{1,33},{33,1},{2,34},{34,2},{3,35},{35,3},{4,36},{36... | collective-permute-start | bytes 2359304 | tf_op jit(solution)/shard_map/ppermute | solution.py:41
  139.9 2.1 %collective-permute-start.13 = (bf16[128,384]{1,0:T(8,128)(2,1)S(1)}, bf16[128,384]{1,0:T(8,128)(2,1)S(1)}, u32[]{:S(2)}, u32[]{:S(2)}) collective-permute-start(bf16[128,384]{1,0:T(8,128)(2,1)S(1)} %constant_dynamic-update-slice_fusion.own_ref.refs_3_), channel_id=1, source_target_pairs={{0,32},{32,0},{1,33},{33,1},{2,34},{34,2},{3,35},{35,3},{4,36},{36... | collective-permute-start | bytes 294920 | tf_op jit(solution)/shard_map/ppermute | solution.py:41
  144.2 4.1 %copy-start.1 = (bf16[448,12288]{1,0:T(8,128)(2,1)S(1)}, bf16[448,12288]{1,0:T(8,128)(2,1)}, u32[]{:S(2)}) copy-start(bf16[448,12288]{1,0:T(8,128)(2,1)} %copy-done) | copy-start | bytes 33030148

commit v6 on v3

--- a/solution.py
+++ b/solution.py
@@ -55,7 +55,7 @@
     return lax.ppermute(value, ("y", "core", "x"), pairs)
 
 
-VMEM_LIMIT = 24 * 2**20
+MIB = 2**20
 
 
 def in_hbm(value):
@@ -66,14 +66,14 @@
     return [pl.BlockSpec(memory_space=pltpu.VMEM)] * count
 
 
-def kernel_call(body, name, in_specs, out_shape, scratch=(), flops=0, moved=0):
+def kernel_call(body, name, in_specs, out_shape, scratch=(), flops=0, moved=0, vmem=8 * MIB):
     return pl.pallas_call(
         body,
         in_specs=in_specs,
         out_specs=in_vmem(len(out_shape)),
         out_shape=out_shape,
         scratch_shapes=list(scratch),
-        compiler_params=pltpu.CompilerParams(vmem_limit_bytes=VMEM_LIMIT),
+        compiler_params=pltpu.CompilerParams(vmem_limit_bytes=vmem),
         cost_estimate=pl.CostEstimate(flops=flops, bytes_accessed=moved, transcendentals=0),
         name=name,
     )
@@ -140,7 +140,7 @@
             pl.BlockSpec(memory_space=pltpu.HBM),
             pl.BlockSpec(memory_space=pltpu.HBM),
         ],
-        [part] * (2 * NX) + [jax.ShapeDtypeStruct((count, width), bf16)],
+        [part] * (2 * NX) + [pltpu.VMEM((count, width), bf16)],
         [
             pltpu.VMEM((count, cols), bf16),
             pltpu.VMEM((cols, count), bf16),
@@ -149,6 +149,7 @@
         ],
         2 * cols * count * width,
         2 * (count * width + cols * width + cols * count),
+        16 * MIB,
     )(place, in_hbm(cotangent), in_hbm(tokens))
     return out[:NX], out[NX : 2 * NX], out[2 * NX]
 
@@ -202,74 +203,61 @@
         [pltpu.VMEM((NX, cols, width // NX), bf16), pltpu.VMEM((count, cols), f32)],
         2 * cols * count * width,
         2 * (count * width + cols * width + cols * count),
-    )(place, held, *own, *other)[0]
-
-
-def plane_kernel(planes_ref, piece_ref, squares_ref):
-    unit = piece_ref.shape[0]
+        16 * MIB,
+    )(place, pltpu.with_memory_space_constraint(held, pltpu.VMEM), *own, *other)[0]
+
+
+def plane_kernel(planes_ref, out_ref):
+    unit = planes_ref.shape[0] // NZ
     total = planes_ref[:unit].astype(f32)
     for z in range(1, NZ):
         total += planes_ref[z * unit : (z + 1) * unit].astype(f32)
-    piece_ref[...] = total.astype(bf16)
-    squares_ref[...] = jnp.broadcast_to(jnp.sum(total * total), squares_ref.shape)
+    piece = total.astype(bf16)
+    for i in range(NC * NY):
+        out_ref[i * unit : (i + 1) * unit, :] = piece
 
 
 def plane_sum(planes):
     unit, rows = planes.shape[0] // NZ, planes.shape[1]
-    everyone = NY * NC * NX * NZ
-    return kernel_call(
-        plane_kernel,
-        "plane_sum",
-        in_vmem(1),
-        [jax.ShapeDtypeStruct((unit, rows), bf16), jax.ShapeDtypeStruct((everyone, 128), f32)],
-    )(planes)
-
-
-def weight_kernel(count, place_ref, piece_ref, squares_ref, *refs):
-    states, (out_ref, wide, turned) = refs[:3], refs[3:]
+    shape = jax.ShapeDtypeStruct((NC * NY * unit, rows), bf16)
+    return kernel_call(plane_kernel, "plane_sum", in_vmem(1), [shape])(planes)[0]
+
+
+def square_kernel(grads_ref, squares_ref):
+    grads = grads_ref[...].astype(f32)
+    squares_ref[...] = jnp.broadcast_to(jnp.sum(grads * grads), squares_ref.shape)
+
+
+def square_sum(grads):
+    shape = jax.ShapeDtypeStruct((NX * NZ, 128), f32)
+    return kernel_call(square_kernel, "square_sum", in_vmem(1), [shape])(grads)[0]
+
+
+def weight_kernel(count, place_ref, grads_ref, squares_ref, *refs):
+    states, (out_ref, turned) = refs[:3], refs[3:]
     y, c = place_ref[0], place_ref[1]
-    unit, rows = piece_ref.shape
-    half = wide.shape[1]
-    at = pl.multiple_of(y * unit, unit)
-    lanes = pl.ds(pl.multiple_of(c * half, half), half)
+    half, rows = turned.shape
+    unit = half // NY
+    at = pl.multiple_of(c * half, half)
+    lanes = pl.ds(at, half)
     total = jnp.sum(squares_ref[:, :1])
-    turned[...] = jnp.zeros_like(turned)
-    turned[pl.ds(at, unit), :] = piece_ref[...].astype(f32)
-    wide[...] = turned[...].T
-    new = apply_update(wide[...], *[state[:, lanes] for state in states], total, count)[0]
+    grads = grads_ref[pl.ds(at, half), :].astype(f32).T
+    new = apply_update(grads, *[state[:, lanes] for state in states], total, count)[0]
     turned[...] = new.T
-    mine = turned[pl.ds(at, unit), :].astype(bf16)
+    mine = turned[pl.ds(pl.multiple_of(y * unit, unit), unit), :].astype(bf16)
     for z in range(NZ):
         out_ref[z * unit : (z + 1) * unit, :] = mine
 
 
-def weight_piece(place, piece, squares, states, count):
-    unit, rows = piece.shape
-    half = states[0].shape[1] // 2
+def weight_piece(place, grads, squares, states, count):
+    rows, cols = states[0].shape
     return kernel_call(
         functools.partial(weight_kernel, count),
         "weight_piece",
         [pl.BlockSpec(memory_space=pltpu.SMEM)] + in_vmem(2 + len(states)),
-        [jax.ShapeDtypeStruct((NZ * unit, rows), bf16)],
-        [pltpu.VMEM((rows, half), f32), pltpu.VMEM((half, rows), f32)],
-    )(place, piece, squares, *states)[0]
-
-
-def spread_kernel(piece_ref, after_ref, out_ref):
-    del after_ref
-    unit = piece_ref.shape[0]
-    for i in range(out_ref.shape[0] // unit):
-        out_ref[i * unit : (i + 1) * unit, :] = piece_ref[...]
-
-
-def spread(piece, copies, after):
-    unit, rows = piece.shape
-    return kernel_call(
-        spread_kernel,
-        "spread",
-        in_vmem(1) + [pl.BlockSpec(memory_space=pl.ANY)],
-        [jax.ShapeDtypeStruct((copies * unit, rows), bf16)],
-    )(piece, after)[0]
+        [jax.ShapeDtypeStruct((NZ * cols // (NC * NY), rows), bf16)],
+        [pltpu.VMEM((cols // 2, rows), f32)],
+    )(place, grads, squares, *states)[0]
 
 
 def update_kernel(count, grads_ref, squares_ref, *refs):
@@ -312,16 +300,15 @@
     got = [routed(line[d * unit : (d + 1) * unit], d, False) for d in FAR_FIRST]
     plane = add(line[:unit], *got).astype(bf16)
     planes = lax.all_to_all(plane, "z", 1, 0, tiled=True)
-    piece, squares = plane_sum(planes)
-    squares = lax.all_to_all(squares, NAMES, 0, 0, tiled=True)
-
-    weight = weight_piece(place, piece, squares, states, count)
+    grads = lax.all_to_all(plane_sum(planes), ("core", "y"), 0, 0, tiled=True)
+    squares = lax.all_to_all(square_sum(grads), ("x", "z"), 0, 0, tiled=True)
+
+    weight = weight_piece(place, grads, squares, states, count)
     plane = lax.all_to_all(weight, "z", 0, 1, tiled=True)
     line = jnp.concatenate([plane] + [routed(plane, d, False) for d in (1, 2, 3)], 0)
     own = [line] + [routed(line, d, True) for d in (1, 2, 3)]
     other = [send(part, "core", 1) for part in own]
 
-    grads = lax.all_to_all(spread(piece, NC * NY, other[0]), ("core", "y"), 0, 0, tiled=True)
     master_new, first_new, second_new = update(grads, squares, states, count)
     activations = forward(place, held, own, other)
     return (master_new, first_new, second_new, activations)

time: 146 us -> 142 us (0.973)
  blocking collectives: 59.2 us -> 52.3 us
  starting transfers between devices: 29.9 us -> 33.2 us
    all_to_all x2, blocking collectives: 30.6 us -> 24.6 us  [the longest x1 12.5 us: body(): squares = lax.all_to_all(square_sum(grads), ('x', 'z'), 0, 0, tiled=True)]
    ppermute x8, starting transfers between devices: 19.8 us -> 23 us  [send(): return lax.ppermute(value, axis, [(i, (i + step) % n) for i in range(n)])]
  transfers between devices with their start and end apart: 20 -> 20, of which waited for: 10 -> 11; matrix products, arithmetic and copies ran while one was open for 0% -> 0% of each run, Pallas kernels for 1% -> 1%
where the time goes in v6:
time: 142 us; the launch traced here: 141 us
  blocking collectives  52.3 us (37%)
  waiting for transfers between devices  38.8 us (27%)
  starting transfers between devices  33.2 us (23%)
  Pallas kernels  14.6 us (10%)
    ppermute x12, waiting for transfers between devices, routed(): return lax.ppermute(value, ('y', 'core', 'x'), pairs)  35.8 us
    ppermute x8, starting transfers between devices, send(): return lax.ppermute(value, axis, [(i, (i + step) % n) for i in range(n)])  23 us
    all_to_all x1, blocking collectives, body(): planes = lax.all_to_all(plane, 'z', 1, 0, tiled=True)  16.6 us
    all_to_all x1, blocking collectives, body(): squares = lax.all_to_all(square_sum(grads), ('x', 'z'), 0, 0, tiled=True)  12.5 us
    all_to_all x1, blocking collectives, body(): grads = lax.all_to_all(plane_sum(planes), ('core', 'y'), 0, 0, tiled=True)  12.1 us
    all_to_all x1, blocking collectives, body(): plane = lax.all_to_all(weight, 'z', 0, 1, tiled=True)  11.1 us
    ppermute x12, starting transfers between devices, routed(): return lax.ppermute(value, ('y', 'core', 'x'), pairs)  10.3 us
    pallas_call x1, Pallas kernels, partial_terms(): kernel_call(partial_kernel, 'partial_terms', [pl.BlockSpec(memory_space=p...  6.55 us
  transfers between devices with their start and end apart: 20, of which 11 were waited for; matrix products, arithmetic and copies ran while one was open for 0% of the time, Pallas kernels for 1%

profile of v6, /device:TPU:1, one launch (start us, length us, event | category | flops | bytes accessed | tf_op | source)
XLA Modules:
  0.0 141.3 jit_solution(4011639956938049940)
XLA Ops:
  0.7 6.6 %partial_terms.1 = (bf16[128,3072]{1,0:T(8,128)(2,1)S(1)}, bf16[128,3072]{1,0:T(8,128)(2,1)S(1)}, bf16[128,3072]{1,0:T(8,128)(2,1)S(1)}, bf16[128,3072]{1,0:T(8,...) custom-call(s32[3]{0:T(128)S(1)} %pad_add_fusion.place_ref, ...), custom_call_target="tpu_custom_call" | custom-call | flops 2818572288 | bytes 17530880 | tf_op jit(solution)/shard_map/partial_terms/pallas_call | solution.py:135
  7.3 3.3 %collective-permute-start.1 = (bf16[128,3072]{1,0:T(8,128)(2,1)S(1)}, bf16[128,3072]{1,0:T(8,128)(2,1)S(1)}, u32[]{:S(2)}, u32[]{:S(2)}) collective-permute-start(bf16[128,3072]{1,0:T(8,128)(2,1)S(1)} %get-tuple-element.19), channel_id=1, source_target_pairs={{0,32},{32,0},{1,33},{33,1},{2,34},{34,2},{3,35},{35,3},{4,36},{36... | collective-permute-start | bytes 2359304 | tf_op jit(solution)/shard_map/ppermute | solution.py:41
  11.2 1.3 collective-permute-done.1
  12.7 1.3 collective-permute-start.2
  14.7 1.2 collective-permute-done.5
  16.1 1.1 collective-permute-start.6
  17.2 8.3 %collective-permute-done.2 = bf16[128,3072]{1,0:T(8,128)(2,1)S(1)} collective-permute-done((bf16[128,3072]{1,0:T(8,128)(2,1)S(1)}, bf16[128,3072]{1,0:T(8,128)(2,1)S(1)}, u32[]{:S(2)}, u32[]{:S(2)}) %collective-permute-start.2) | collective-permute-done | bytes 786464 | tf_op jit(solution)/shard_map/ppermute | solution.py:55
  25.5 8.4 %collective-permute-done.4 = bf16[128,3072]{1,0:T(8,128)(2,1)S(1)} collective-permute-done((bf16[128,3072]{1,0:T(8,128)(2,1)S(1)}, bf16[128,3072]{1,0:T(8,128)(2,1)S(1)}, u32[]{:S(2)}, u32[]{:S(2)}) %collective-permute-start.4) | collective-permute-done | bytes 786464 | tf_op jit(solution)/shard_map/ppermute | solution.py:55
  33.9 0.6 add_convert_fusion
  34.6 1.5 %collective-permute-start.7 = (bf16[32,3072]{1,0:T(8,128)(2,1)S(1)}, bf16[32,3072]{1,0:T(8,128)(2,1)S(1)}, u32[]{:S(2)}, u32[]{:S(2)}) collective-permute-start(bf16[32,3072]{1,0:T(8,128)(2,1)S(1)} %get-tuple-element.28), channel_id=1, source_target_pairs={{0,128},{8,136},{16,144},{24,152},{32,48},{40,56},{48,32},{56,40},... | collective-permute-start | bytes 589832 | tf_op jit(solution)/shard_map/ppermute | solution.py:55
  36.1 0.9 collective-permute-start.9
  37.5 3.5 %collective-permute-done.7 = bf16[32,3072]{1,0:T(8,128)(2,1)S(1)} collective-permute-done((bf16[32,3072]{1,0:T(8,128)(2,1)S(1)}, bf16[32,3072]{1,0:T(8,128)(2,1)S(1)}, u32[]{:S(2)}, u32[]{:S(2)}) %collective-permute-start.7) | collective-permute-done | bytes 196640 | tf_op jit(solution)/shard_map/ppermute | solution.py:55
  41.0 0.8 collective-permute-done.9
  41.8 1.3 collective-permute-done.8
  43.2 16.6 %all_to_all.60 = bf16[32,8,384]{2,0,1:T(8,128)(2,1)S(1)} all-to-all(bf16[32,8,384]{2,0,1:T(8,128)(2,1)S(1)} %bitcast.33), channel_id=1, replica_groups=mesh['y'=4,'core'=2,'x'=4,'z'=8] {'z'}, dimensions={1} | all-to-all | bytes 393216 | tf_op jit(solution)/shard_map/all_to_all | solution.py:302
  59.9 12.1 %all_to_all.61 = bf16[8,32,384]{2,1,0:T(8,128)(2,1)S(1)} all-to-all(bf16[8,32,384]{2,1,0:T(8,128)(2,1)S(1)} %bitcast.24), channel_id=1, replica_groups=mesh['y'=4,'core'=2,'x'=4,'z'=8] {'core','y'}, dimensions={0} | all-to-all | bytes 393216 | tf_op jit(solution)/shard_map/all_to_all | solution.py:303
  72.2 12.5 %all_to_all.62 = f32[32,1,128]{2,1,0:T(1,128)S(1)} all-to-all(f32[32,1,128]{2,1,0:T(1,128)S(1)} %bitcast.28), channel_id=1, replica_groups=mesh['y'=4,'core'=2,'x'=4,'z'=8] {'x','z'}, dimensions={0} | all-to-all | bytes 32768 | tf_op jit(solution)/shard_map/all_to_all | solution.py:304
  84.6 1.0 weight_piece.1
  85.7 11.1 %all_to_all.63 = bf16[8,32,384]{2,1,0:T(8,128)(2,1)S(1)} all-to-all(bf16[8,32,384]{2,1,0:T(8,128)(2,1)S(1)} %bitcast.25), channel_id=1, replica_groups=mesh['y'=4,'core'=2,'x'=4,'z'=8] {'z'}, dimensions={0} | all-to-all | bytes 393216 | tf_op jit(solution)/shard_map/all_to_all | solution.py:307
  96.9 1.0 collective-permute-start.12
  97.8 1.2 collective-permute-start.11
  99.1 7.2 %collective-permute-done.10 = bf16[32,3072]{1,0:T(8,128)(2,1)S(1)} collective-permute-done((bf16[32,3072]{1,0:T(8,128)(2,1)S(1)}, bf16[32,3072]{1,0:T(8,128)(2,1)S(1)}, u32[]{:S(2)}, u32[]{:S(2)}) %collective-permute-start.10) | collective-permute-done | bytes 196640 | tf_op jit(solution)/shard_map/ppermute | solution.py:55
  106.3 0.9 collective-permute-start.15
  107.2 1.4 collective-permute-start.14
  108.6 5.0 %collective-permute-start.16 = (bf16[128,3072]{1,0:T(8,128)(2,1)S(1)}, bf16[128,3072]{1,0:T(8,128)(2,1)S(1)}, u32[]{:S(2)}, u32[]{:S(2)}) collective-permute-start(bf16[128,3072]{1,0:T(8,128)(2,1)S(1)} %constant_dynamic-update-slice_fusion.refs_0_), channel_id=1, source_target_pairs={{0,32},{32,0},{1,33},{33,1},{2,34},{34,2},{3,35},{35,3},{4,36},{36... | collective-permute-start | bytes 2359304 | tf_op jit(solution)/shard_map/ppermute | solution.py:41
  113.7 3.9 %collective-permute-done.15.refs_3_ = bf16[128,3072]{1,0:T(8,128)(2,1)S(1)} collective-permute-done((bf16[128,3072]{1,0:T(8,128)(2,1)S(1)}, bf16[128,3072]{1,0:T(8,128)(2,1)S(1)}, u32[]{:S(2)}, u32[]{:S(2)}) %collective-permute-start.15) | collective-permute-done | bytes 786464 | tf_op jit(solution)/shard_map/ppermute | solution.py:55
  117.5 5.4 %collective-permute-start.19 = (bf16[128,3072]{1,0:T(8,128)(2,1)S(1)}, bf16[128,3072]{1,0:T(8,128)(2,1)S(1)}, u32[]{:S(2)}, u32[]{:S(2)}) collective-permute-start(bf16[128,3072]{1,0:T(8,128)(2,1)S(1)} %collective-permute-done.15.refs_3_), channel_id=1, source_target_pairs={{0,32},{32,0},{1,33},{33,1},{2,34},{34,2},{3,35},{35,3},{4,36},{36... | collective-permute-start | bytes 2359304 | tf_op jit(solution)/shard_map/ppermute | solution.py:41
  123.0 2.8 %collective-permute-start.18 = (bf16[128,3072]{1,0:T(8,128)(2,1)S(1)}, bf16[128,3072]{1,0:T(8,128)(2,1)S(1)}, u32[]{:S(2)}, u32[]{:S(2)}) collective-permute-start(bf16[128,3072]{1,0:T(8,128)(2,1)S(1)} %collective-permute-done.14.refs_2_), channel_id=1, source_target_pairs={{0,32},{32,0},{1,33},{33,1},{2,34},{34,2},{3,35},{35,3},{4,36},{36... | collective-permute-start | bytes 2359304 | tf_op jit(solution)/shard_map/ppermute | solution.py:41
  125.7 2.5 %collective-permute-done.13.refs_1_ = bf16[128,3072]{1,0:T(8,128)(2,1)S(1)} collective-permute-done((bf16[128,3072]{1,0:T(8,128)(2,1)S(1)}, bf16[128,3072]{1,0:T(8,128)(2,1)S(1)}, u32[]{:S(2)}, u32[]{:S(2)}) %collective-permute-start.13) | collective-permute-done | bytes 786464 | tf_op jit(solution)/shard_map/ppermute | solution.py:55
  128.3 5.8 %collective-permute-start.17 = (bf16[128,3072]{1,0:T(8,128)(2,1)S(1)}, bf16[128,3072]{1,0:T(8,128)(2,1)S(1)}, u32[]{:S(2)}, u32[]{:S(2)}) collective-permute-start(bf16[128,3072]{1,0:T(8,128)(2,1)S(1)} %collective-permute-done.13.refs_1_), channel_id=1, source_target_pairs={{0,32},{32,0},{1,33},{33,1},{2,34},{34,2},{3,35},{35,3},{4,36},{36... | collective-permute-start | bytes 2359304 | tf_op jit(solution)/shard_map/ppermute | solution.py:41
  134.1 1.5 %update.1 = (f32[384,256]{1,0:T(8,128)}, f32[384,256]{1,0:T(8,128)}, f32[384,256]{1,0:T(8,128)}) custom-call(bf16[256,384]{1,0:T(8,128)(2,1)S(1)} %bitcast.22, f32[32,128]{1,0:T(8,128)S(1)} %bitcast.27, f32[384,256]{1,0:T(8,128)S(1)} %copy-done, f32[384,256]{1,0:T(8,128)S(1)} %copy-done.1, f32[384,256]{1,0:T(8,128)S(1)} %copy-done.2), custom_call_target="tpu_custom_call" | custom-call | tf_op jit(solution)/shard_map/update/pallas_call | solution.py:271
  136.0 5.3 %forward.1 = bf16[448,256]{1,0:T(8,128)(2,1)} custom-call(s32[3]{0:T(128)S(1)} %pad_add_fusion.place_ref, bf16[448,12288]{1,0:T(8,128)(2,1)S(1)} %get-tuple-element.27.held, bf16[128,3072]{1,0:T(8,128)(2,1)S(1)} %constant_dynamic-update-slice_fusion.refs_0_, bf16[128,3072]{1,0:T(8,128)(2,1)S(1)} %collective-permute-done.13.refs_1_, ...), custom_call_target="tpu_custom_call" | custom-call | flops 2818572288 | bytes 17530880 | tf_op jit(solution)/shard_map/forward/pallas_call | solution.py:198
  (37 shorter events, 3.3 us)
Async XLA Ops:
  7.3 5.2 %collective-permute-start.1 = (bf16[128,3072]{1,0:T(8,128)(2,1)S(1)}, bf16[128,3072]{1,0:T(8,128)(2,1)S(1)}, u32[]{:S(2)}, u32[]{:S(2)}) collective-permute-start(bf16[128,3072]{1,0:T(8,128)(2,1)S(1)} %get-tuple-element.19), channel_id=1, source_target_pairs={{0,32},{32,0},{1,33},{33,1},{2,34},{34,2},{3,35},{35,3},{4,36},{36... | collective-permute-start | bytes 2359304 | tf_op jit(solution)/shard_map/ppermute | solution.py:41
  10.6 3.4 %collective-permute-start.3 = (bf16[128,3072]{1,0:T(8,128)(2,1)S(1)}, bf16[128,3072]{1,0:T(8,128)(2,1)S(1)}, u32[]{:S(2)}, u32[]{:S(2)}) collective-permute-start(bf16[128,3072]{1,0:T(8,128)(2,1)S(1)} %get-tuple-element.21), channel_id=1, source_target_pairs={{0,32},{32,0},{1,33},{33,1},{2,34},{34,2},{3,35},{35,3},{4,36},{36... | collective-permute-start | bytes 2359304 | tf_op jit(solution)/shard_map/ppermute | solution.py:41
  10.7 6.5 %collective-permute-start = (bf16[128,3072]{1,0:T(8,128)(2,1)S(1)}, bf16[128,3072]{1,0:T(8,128)(2,1)S(1)}, u32[]{:S(2)}, u32[]{:S(2)}) collective-permute-start(bf16[128,3072]{1,0:T(8,128)(2,1)S(1)} %get-tuple-element.17), channel_id=1, source_target_pairs={{0,32},{32,0},{1,33},{33,1},{2,34},{34,2},{3,35},{35,3},{4,36},{36... | collective-permute-start | bytes 2359304 | tf_op jit(solution)/shard_map/ppermute | solution.py:41
  11.1 4.8 %collective-permute-start.5 = (bf16[128,3072]{1,0:T(8,128)(2,1)S(1)}, bf16[128,3072]{1,0:T(8,128)(2,1)S(1)}, u32[]{:S(2)}, u32[]{:S(2)}) collective-permute-start(bf16[128,3072]{1,0:T(8,128)(2,1)S(1)} %get-tuple-element.23), channel_id=1, source_target_pairs={{0,32},{32,0},{1,33},{33,1},{2,34},{34,2},{3,35},{35,3},{4,36},{36... | collective-permute-start | bytes 2359304 | tf_op jit(solution)/shard_map/ppermute | solution.py:41
  12.7 12.8 %collective-permute-start.2 = (bf16[128,3072]{1,0:T(8,128)(2,1)S(1)}, bf16[128,3072]{1,0:T(8,128)(2,1)S(1)}, u32[]{:S(2)}, u32[]{:S(2)}) collective-permute-start(bf16[128,3072]{1,0:T(8,128)(2,1)S(1)} %add_convert_fusion.3), channel_id=1, source_target_pairs={{0,16},{8,24},{16,0},{24,8},{32,160},{40,168},{48,176},{56,184},{6... | collective-permute-start | bytes 2359304 | tf_op jit(solution)/shard_map/ppermute | solution.py:55
  14.2 19.7 %collective-permute-start.4 = (bf16[128,3072]{1,0:T(8,128)(2,1)S(1)}, bf16[128,3072]{1,0:T(8,128)(2,1)S(1)}, u32[]{:S(2)}, u32[]{:S(2)}) collective-permute-start(bf16[128,3072]{1,0:T(8,128)(2,1)S(1)} %add_convert_fusion.2), channel_id=1, source_target_pairs={{0,8},{8,16},{16,24},{24,0},{32,96},{40,104},{48,112},{56,120},{64... | collective-permute-start | bytes 2359304 | tf_op jit(solution)/shard_map/ppermute | solution.py:55
  16.1 17.8 %collective-permute-start.6 = (bf16[128,3072]{1,0:T(8,128)(2,1)S(1)}, bf16[128,3072]{1,0:T(8,128)(2,1)S(1)}, u32[]{:S(2)}, u32[]{:S(2)}) collective-permute-start(bf16[128,3072]{1,0:T(8,128)(2,1)S(1)} %add_convert_fusion.1), channel_id=1, source_target_pairs={{0,24},{8,0},{16,8},{24,16},{32,224},{40,232},{48,240},{56,248},{6... | collective-permute-start | bytes 2359304 | tf_op jit(solution)/shard_map/ppermute | solution.py:55
  34.6 50.1 %copy-start = (f32[384,256]{1,0:T(8,128)S(1)}, f32[384,256]{1,0:T(8,128)}, u32[]{:S(2)}) copy-start(f32[384,256]{1,0:T(8,128)} %refs_0_.3) | copy-start | bytes 1179652
  34.6 50.1 %copy-start.1 = (f32[384,256]{1,0:T(8,128)S(1)}, f32[384,256]{1,0:T(8,128)}, u32[]{:S(2)}) copy-start(f32[384,256]{1,0:T(8,128)} %refs_1_.3) | copy-start | bytes 1179652
  34.6 50.1 %copy-start.2 = (f32[384,256]{1,0:T(8,128)S(1)}, f32[384,256]{1,0:T(8,128)}, u32[]{:S(2)}) copy-start(f32[384,256]{1,0:T(8,128)} %refs_2_.3) | copy-start | bytes 1179652
  34.6 6.4 %collective-permute-start.7 = (bf16[32,3072]{1,0:T(8,128)(2,1)S(1)}, bf16[32,3072]{1,0:T(8,128)(2,1)S(1)}, u32[]{:S(2)}, u32[]{:S(2)}) collective-permute-start(bf16[32,3072]{1,0:T(8,128)(2,1)S(1)} %get-tuple-element.28), channel_id=1, source_target_pairs={{0,128},{8,136},{16,144},{24,152},{32,48},{40,56},{48,32},{56,40},... | collective-permute-start | bytes 589832 | tf_op jit(solution)/shard_map/ppermute | solution.py:55
  36.1 5.8 %collective-permute-start.9 = (bf16[32,3072]{1,0:T(8,128)(2,1)S(1)}, bf16[32,3072]{1,0:T(8,128)(2,1)S(1)}, u32[]{:S(2)}, u32[]{:S(2)}) collective-permute-start(bf16[32,3072]{1,0:T(8,128)(2,1)S(1)} %get-tuple-element.29), channel_id=1, source_target_pairs={{0,192},{8,200},{16,208},{24,216},{32,56},{40,32},{48,40},{56,48},... | collective-permute-start | bytes 589832 | tf_op jit(solution)/shard_map/ppermute | solution.py:55
  36.9 6.2 %collective-permute-start.8 = (bf16[32,3072]{1,0:T(8,128)(2,1)S(1)}, bf16[32,3072]{1,0:T(8,128)(2,1)S(1)}, u32[]{:S(2)}, u32[]{:S(2)}) collective-permute-start(bf16[32,3072]{1,0:T(8,128)(2,1)S(1)} %get-tuple-element.30), channel_id=1, source_target_pairs={{0,64},{8,72},{16,80},{24,88},{32,40},{40,48},{48,56},{56,32},{64,... | collective-permute-start | bytes 589832 | tf_op jit(solution)/shard_map/ppermute | solution.py:55
  96.9 9.4 %collective-permute-start.12 = (bf16[32,3072]{1,0:T(8,128)(2,1)S(1)}, bf16[32,3072]{1,0:T(8,128)(2,1)S(1)}, u32[]{:S(2)}, u32[]{:S(2)}) collective-permute-start(bf16[32,3072]{1,0:T(8,128)(2,1)S(1)} %bitcast.29), channel_id=1, source_target_pairs={{0,192},{8,200},{16,208},{24,216},{32,56},{40,32},{48,40},{56,48},... | collective-permute-start | bytes 589832 | tf_op jit(solution)/shard_map/ppermute | solution.py:55
  97.8 8.4 %collective-permute-start.11 = (bf16[32,3072]{1,0:T(8,128)(2,1)S(1)}, bf16[32,3072]{1,0:T(8,128)(2,1)S(1)}, u32[]{:S(2)}, u32[]{:S(2)}) collective-permute-start(bf16[32,3072]{1,0:T(8,128)(2,1)S(1)} %bitcast.30), channel_id=1, source_target_pairs={{0,128},{8,136},{16,144},{24,152},{32,48},{40,56},{48,32},{56,40},... | collective-permute-start | bytes 589832 | tf_op jit(solution)/shard_map/ppermute | solution.py:55
  99.1 7.2 %collective-permute-start.10 = (bf16[32,3072]{1,0:T(8,128)(2,1)S(1)}, bf16[32,3072]{1,0:T(8,128)(2,1)S(1)}, u32[]{:S(2)}, u32[]{:S(2)}) collective-permute-start(bf16[32,3072]{1,0:T(8,128)(2,1)S(1)} %bitcast.31), channel_id=1, source_target_pairs={{0,64},{8,72},{16,80},{24,88},{32,40},{40,48},{48,56},{56,32},{64,... | collective-permute-start | bytes 589832 | tf_op jit(solution)/shard_map/ppermute | solution.py:55
  106.3 11.2 %collective-permute-start.15 = (bf16[128,3072]{1,0:T(8,128)(2,1)S(1)}, bf16[128,3072]{1,0:T(8,128)(2,1)S(1)}, u32[]{:S(2)}, u32[]{:S(2)}) collective-permute-start(bf16[128,3072]{1,0:T(8,128)(2,1)S(1)} %constant_dynamic-update-slice_fusion.refs_0_), channel_id=1, source_target_pairs={{0,24},{8,0},{16,8},{24,16},{32,224},{40,232},{48,240},{56,248},{6... | collective-permute-start | bytes 2359304 | tf_op jit(solution)/shard_map/ppermute | solution.py:55
  107.2 15.8 %collective-permute-start.14 = (bf16[128,3072]{1,0:T(8,128)(2,1)S(1)}, bf16[128,3072]{1,0:T(8,128)(2,1)S(1)}, u32[]{:S(2)}, u32[]{:S(2)}) collective-permute-start(bf16[128,3072]{1,0:T(8,128)(2,1)S(1)} %constant_dynamic-update-slice_fusion.refs_0_), channel_id=1, source_target_pairs={{0,16},{8,24},{16,0},{24,8},{32,160},{40,168},{48,176},{56,184},{6... | collective-permute-start | bytes 2359304 | tf_op jit(solution)/shard_map/ppermute | solution.py:55
  108.6 19.7 %collective-permute-start.13 = (bf16[128,3072]{1,0:T(8,128)(2,1)S(1)}, bf16[128,3072]{1,0:T(8,128)(2,1)S(1)}, u32[]{:S(2)}, u32[]{:S(2)}) collective-permute-start(bf16[128,3072]{1,0:T(8,128)(2,1)S(1)} %constant_dynamic-update-slice_fusion.refs_0_), channel_id=1, source_target_pairs={{0,8},{8,16},{16,24},{24,0},{32,96},{40,104},{48,112},{56,120},{64... | collective-permute-start | bytes 2359304 | tf_op jit(solution)/shard_map/ppermute | solution.py:55
  108.6 26.9 %collective-permute-start.16 = (bf16[128,3072]{1,0:T(8,128)(2,1)S(1)}, bf16[128,3072]{1,0:T(8,128)(2,1)S(1)}, u32[]{:S(2)}, u32[]{:S(2)}) collective-permute-start(bf16[128,3072]{1,0:T(8,128)(2,1)S(1)} %constant_dynamic-update-slice_fusion.refs_0_), channel_id=1, source_target_pairs={{0,32},{32,0},{1,33},{33,1},{2,34},{34,2},{3,35},{35,3},{4,36},{36... | collective-permute-start | bytes 2359304 | tf_op jit(solution)/shard_map/ppermute | solution.py:41
  117.5 18.0 %collective-permute-start.19 = (bf16[128,3072]{1,0:T(8,128)(2,1)S(1)}, bf16[128,3072]{1,0:T(8,128)(2,1)S(1)}, u32[]{:S(2)}, u32[]{:S(2)}) collective-permute-start(bf16[128,3072]{1,0:T(8,128)(2,1)S(1)} %collective-permute-done.15.refs_3_), channel_id=1, source_target_pairs={{0,32},{32,0},{1,33},{33,1},{2,34},{34,2},{3,35},{35,3},{4,36},{36... | collective-permute-start | bytes 2359304 | tf_op jit(solution)/shard_map/ppermute | solution.py:41
  123.0 12.6 %collective-permute-start.18 = (bf16[128,3072]{1,0:T(8,128)(2,1)S(1)}, bf16[128,3072]{1,0:T(8,128)(2,1)S(1)}, u32[]{:S(2)}, u32[]{:S(2)}) collective-permute-start(bf16[128,3072]{1,0:T(8,128)(2,1)S(1)} %collective-permute-done.14.refs_2_), channel_id=1, source_target_pairs={{0,32},{32,0},{1,33},{33,1},{2,34},{34,2},{3,35},{35,3},{4,36},{36... | collective-permute-start | bytes 2359304 | tf_op jit(solution)/shard_map/ppermute | solution.py:41
  128.3 7.7 %collective-permute-start.17 = (bf16[128,3072]{1,0:T(8,128)(2,1)S(1)}, bf16[128,3072]{1,0:T(8,128)(2,1)S(1)}, u32[]{:S(2)}, u32[]{:S(2)}) collective-permute-start(bf16[128,3072]{1,0:T(8,128)(2,1)S(1)} %collective-permute-done.13.refs_1_), channel_id=1, source_target_pairs={{0,32},{32,0},{1,33},{33,1},{2,34},{34,2},{3,35},{35,3},{4,36},{36... | collective-permute-start | bytes 2359304 | tf_op jit(solution)/shard_map/ppermute | solution.py:41

commit v7 on v6

--- a/solution.py
+++ b/solution.py
@@ -56,6 +56,7 @@
 
 
 MIB = 2**20
+PARTS = 2
 
 
 def in_hbm(value):
@@ -86,19 +87,21 @@
     chunk = tokens_ref.shape[1] // NX
     half = rows.shape[0] // 2
     unit = half // NY
-    cot_copy = pltpu.make_async_copy(cot_ref, cot, sems.at[NX])
+    cot_copy = pltpu.make_async_copy(cot_ref, cot, sems.at[NX * PARTS])
     cot_copy.start()
+    part = chunk // PARTS
     copies = []
     for d in range(NX):
-        source = pl.multiple_of(lax.rem(x + d, NX) * chunk, chunk)
-        copies.append(
-            pltpu.make_async_copy(
-                tokens_ref.at[:, pl.ds(source, chunk)],
-                held.at[:, pl.ds(d * chunk, chunk)],
-                sems.at[d],
+        for h in range(PARTS):
+            source = pl.multiple_of(lax.rem(x + d, NX) * chunk + h * part, part)
+            copies.append(
+                pltpu.make_async_copy(
+                    tokens_ref.at[:, pl.ds(source, part)],
+                    held.at[:, pl.ds(d * chunk + h * part, part)],
+                    sems.at[d * PARTS + h],
+                )
             )
-        )
-        copies[-1].start()
+            copies[-1].start()
     cot_copy.wait()
     rows_t[...] = cot[...].astype(f32).T.astype(bf16)
     for k, core in enumerate((c, 1 - c)):
@@ -106,18 +109,19 @@
             at = pl.multiple_of(core * half + lax.rem(y + e, NY) * unit, unit)
             rows[pl.ds(k * half + e * unit, unit), :] = rows_t[pl.ds(at, unit), :]
 
-    for d in range(NX):
-        copies[d].wait()
+    for i in range(NX * PARTS):
+        copies[i].wait()
+        d, lanes = i // PARTS, slice(i % PARTS * part, (i % PARTS + 1) * part)
 
         def run(by_x, by_y):
             terms = jnp.dot(
-                rows[...], held[:, d * chunk : (d + 1) * chunk], preferred_element_type=f32
+                rows[...], held[:, i * part : (i + 1) * part], preferred_element_type=f32
             ).astype(bf16)
             mine, theirs = terms[:half], terms[half:]
             for_x, for_y = (mine, theirs) if by_x is own else (theirs, mine)
-            by_x[d][...] = for_x
+            by_x[d][:, lanes] = for_x
             for e in range(NY):
-                by_y[e][d * unit : (d + 1) * unit, :] = for_y[e * unit : (e + 1) * unit]
+                by_y[e][d * unit : (d + 1) * unit, lanes] = for_y[e * unit : (e + 1) * unit]
 
         @pl.when(c == 0)
         def _():
@@ -145,7 +149,7 @@
             pltpu.VMEM((count, cols), bf16),
             pltpu.VMEM((cols, count), bf16),
             pltpu.VMEM((cols, count), bf16),
-            pltpu.SemaphoreType.DMA((NX + 1,)),
+            pltpu.SemaphoreType.DMA((NX * PARTS + 1,)),
         ],
         2 * cols * count * width,
         2 * (count * width + cols * width + cols * count),

time: 142 us -> 142 us (level)
  no operation moved by 1% of the time
where the time goes in v7:
time: 142 us
  blocking collectives  52.3 us (37%)
  waiting for transfers between devices  38.8 us (27%)
  starting transfers between devices  33.4 us (24%)
  Pallas kernels  14.8 us (10%)
    ppermute x12, waiting for transfers between devices, routed(): return lax.ppermute(value, ('y', 'core', 'x'), pairs)  35.8 us
    ppermute x8, starting transfers between devices, send(): return lax.ppermute(value, axis, [(i, (i + step) % n) for i in range(n)])  23 us
    all_to_all x1, blocking collectives, body(): planes = lax.all_to_all(plane, 'z', 1, 0, tiled=True)  16.6 us
    all_to_all x1, blocking collectives, body(): squares = lax.all_to_all(square_sum(grads), ('x', 'z'), 0, 0, tiled=True)  12.5 us
    all_to_all x1, blocking collectives, body(): grads = lax.all_to_all(plane_sum(planes), ('core', 'y'), 0, 0, tiled=True)  12.1 us
    all_to_all x1, blocking collectives, body(): plane = lax.all_to_all(weight, 'z', 0, 1, tiled=True)  11.1 us
    ppermute x12, starting transfers between devices, routed(): return lax.ppermute(value, ('y', 'core', 'x'), pairs)  10.5 us
    pallas_call x1, Pallas kernels, partial_terms(): kernel_call(partial_kernel, 'partial_terms', [pl.BlockSpec(memory_space=p...  6.76 us
  transfers between devices with their start and end apart: 20, of which 11 were waited for; matrix products, arithmetic and copies ran while one was open for 0% of the time, Pallas kernels for 1%

profile of v7, /device:TPU:1, one launch (start us, length us, event | category | flops | bytes accessed | tf_op | source)
XLA Modules:
  0.0 141.6 jit_solution(3817580936450948393)
XLA Ops:
  0.7 6.8 %partial_terms.1 = (bf16[128,3072]{1,0:T(8,128)(2,1)S(1)}, bf16[128,3072]{1,0:T(8,128)(2,1)S(1)}, bf16[128,3072]{1,0:T(8,128)(2,1)S(1)}, bf16[128,3072]{1,0:T(8,...) custom-call(s32[3]{0:T(128)S(1)} %pad_add_fusion.place_ref, ...), custom_call_target="tpu_custom_call" | custom-call | flops 2818572288 | bytes 17530880 | tf_op jit(solution)/shard_map/partial_terms/pallas_call | solution.py:139
  7.5 3.3 %collective-permute-start.1 = (bf16[128,3072]{1,0:T(8,128)(2,1)S(1)}, bf16[128,3072]{1,0:T(8,128)(2,1)S(1)}, u32[]{:S(2)}, u32[]{:S(2)}) collective-permute-start(bf16[128,3072]{1,0:T(8,128)(2,1)S(1)} %get-tuple-element.19), channel_id=1, source_target_pairs={{0,32},{32,0},{1,33},{33,1},{2,34},{34,2},{3,35},{35,3},{4,36},{36... | collective-permute-start | bytes 2359304 | tf_op jit(solution)/shard_map/ppermute | solution.py:41
  11.4 1.3 collective-permute-done.1
  12.9 1.3 collective-permute-start.2
  14.9 1.2 collective-permute-done.5
  16.3 1.1 collective-permute-start.6
  17.4 8.3 %collective-permute-done.2 = bf16[128,3072]{1,0:T(8,128)(2,1)S(1)} collective-permute-done((bf16[128,3072]{1,0:T(8,128)(2,1)S(1)}, bf16[128,3072]{1,0:T(8,128)(2,1)S(1)}, u32[]{:S(2)}, u32[]{:S(2)}) %collective-permute-start.2) | collective-permute-done | bytes 786464 | tf_op jit(solution)/shard_map/ppermute | solution.py:55
  25.7 8.4 %collective-permute-done.4 = bf16[128,3072]{1,0:T(8,128)(2,1)S(1)} collective-permute-done((bf16[128,3072]{1,0:T(8,128)(2,1)S(1)}, bf16[128,3072]{1,0:T(8,128)(2,1)S(1)}, u32[]{:S(2)}, u32[]{:S(2)}) %collective-permute-start.4) | collective-permute-done | bytes 786464 | tf_op jit(solution)/shard_map/ppermute | solution.py:55
  34.1 0.6 add_convert_fusion
  34.8 1.7 %collective-permute-start.7 = (bf16[32,3072]{1,0:T(8,128)(2,1)S(1)}, bf16[32,3072]{1,0:T(8,128)(2,1)S(1)}, u32[]{:S(2)}, u32[]{:S(2)}) collective-permute-start(bf16[32,3072]{1,0:T(8,128)(2,1)S(1)} %get-tuple-element.28), channel_id=1, source_target_pairs={{0,128},{8,136},{16,144},{24,152},{32,48},{40,56},{48,32},{56,40},... | collective-permute-start | bytes 589832 | tf_op jit(solution)/shard_map/ppermute | solution.py:55
  36.5 0.9 collective-permute-start.9
  37.9 3.5 %collective-permute-done.7 = bf16[32,3072]{1,0:T(8,128)(2,1)S(1)} collective-permute-done((bf16[32,3072]{1,0:T(8,128)(2,1)S(1)}, bf16[32,3072]{1,0:T(8,128)(2,1)S(1)}, u32[]{:S(2)}, u32[]{:S(2)}) %collective-permute-start.7) | collective-permute-done | bytes 196640 | tf_op jit(solution)/shard_map/ppermute | solution.py:55
  41.4 0.8 collective-permute-done.9
  42.2 1.3 collective-permute-done.8
  43.6 16.6 %all_to_all.60 = bf16[32,8,384]{2,0,1:T(8,128)(2,1)S(1)} all-to-all(bf16[32,8,384]{2,0,1:T(8,128)(2,1)S(1)} %bitcast.33), channel_id=1, replica_groups=mesh['y'=4,'core'=2,'x'=4,'z'=8] {'z'}, dimensions={1} | all-to-all | bytes 393216 | tf_op jit(solution)/shard_map/all_to_all | solution.py:306
  60.2 12.1 %all_to_all.61 = bf16[8,32,384]{2,1,0:T(8,128)(2,1)S(1)} all-to-all(bf16[8,32,384]{2,1,0:T(8,128)(2,1)S(1)} %bitcast.24), channel_id=1, replica_groups=mesh['y'=4,'core'=2,'x'=4,'z'=8] {'core','y'}, dimensions={0} | all-to-all | bytes 393216 | tf_op jit(solution)/shard_map/all_to_all | solution.py:307
  72.6 12.5 %all_to_all.62 = f32[32,1,128]{2,1,0:T(1,128)S(1)} all-to-all(f32[32,1,128]{2,1,0:T(1,128)S(1)} %bitcast.28), channel_id=1, replica_groups=mesh['y'=4,'core'=2,'x'=4,'z'=8] {'x','z'}, dimensions={0} | all-to-all | bytes 32768 | tf_op jit(solution)/shard_map/all_to_all | solution.py:308
  85.0 1.0 weight_piece.1
  86.1 11.1 %all_to_all.63 = bf16[8,32,384]{2,1,0:T(8,128)(2,1)S(1)} all-to-all(bf16[8,32,384]{2,1,0:T(8,128)(2,1)S(1)} %bitcast.25), channel_id=1, replica_groups=mesh['y'=4,'core'=2,'x'=4,'z'=8] {'z'}, dimensions={0} | all-to-all | bytes 393216 | tf_op jit(solution)/shard_map/all_to_all | solution.py:311
  97.2 1.0 collective-permute-start.12
  98.2 1.2 collective-permute-start.11
  99.5 7.2 %collective-permute-done.10 = bf16[32,3072]{1,0:T(8,128)(2,1)S(1)} collective-permute-done((bf16[32,3072]{1,0:T(8,128)(2,1)S(1)}, bf16[32,3072]{1,0:T(8,128)(2,1)S(1)}, u32[]{:S(2)}, u32[]{:S(2)}) %collective-permute-start.10) | collective-permute-done | bytes 196640 | tf_op jit(solution)/shard_map/ppermute | solution.py:55
  106.7 0.9 collective-permute-start.15
  107.6 1.4 collective-permute-start.14
  109.0 5.0 %collective-permute-start.16 = (bf16[128,3072]{1,0:T(8,128)(2,1)S(1)}, bf16[128,3072]{1,0:T(8,128)(2,1)S(1)}, u32[]{:S(2)}, u32[]{:S(2)}) collective-permute-start(bf16[128,3072]{1,0:T(8,128)(2,1)S(1)} %constant_dynamic-update-slice_fusion.refs_0_), channel_id=1, source_target_pairs={{0,32},{32,0},{1,33},{33,1},{2,34},{34,2},{3,35},{35,3},{4,36},{36... | collective-permute-start | bytes 2359304 | tf_op jit(solution)/shard_map/ppermute | solution.py:41
  114.0 3.9 %collective-permute-done.15.refs_3_ = bf16[128,3072]{1,0:T(8,128)(2,1)S(1)} collective-permute-done((bf16[128,3072]{1,0:T(8,128)(2,1)S(1)}, bf16[128,3072]{1,0:T(8,128)(2,1)S(1)}, u32[]{:S(2)}, u32[]{:S(2)}) %collective-permute-start.15) | collective-permute-done | bytes 786464 | tf_op jit(solution)/shard_map/ppermute | solution.py:55
  117.9 5.4 %collective-permute-start.19 = (bf16[128,3072]{1,0:T(8,128)(2,1)S(1)}, bf16[128,3072]{1,0:T(8,128)(2,1)S(1)}, u32[]{:S(2)}, u32[]{:S(2)}) collective-permute-start(bf16[128,3072]{1,0:T(8,128)(2,1)S(1)} %collective-permute-done.15.refs_3_), channel_id=1, source_target_pairs={{0,32},{32,0},{1,33},{33,1},{2,34},{34,2},{3,35},{35,3},{4,36},{36... | collective-permute-start | bytes 2359304 | tf_op jit(solution)/shard_map/ppermute | solution.py:41
  123.3 2.8 %collective-permute-start.18 = (bf16[128,3072]{1,0:T(8,128)(2,1)S(1)}, bf16[128,3072]{1,0:T(8,128)(2,1)S(1)}, u32[]{:S(2)}, u32[]{:S(2)}) collective-permute-start(bf16[128,3072]{1,0:T(8,128)(2,1)S(1)} %collective-permute-done.14.refs_2_), channel_id=1, source_target_pairs={{0,32},{32,0},{1,33},{33,1},{2,34},{34,2},{3,35},{35,3},{4,36},{36... | collective-permute-start | bytes 2359304 | tf_op jit(solution)/shard_map/ppermute | solution.py:41
  126.1 2.5 %collective-permute-done.13.refs_1_ = bf16[128,3072]{1,0:T(8,128)(2,1)S(1)} collective-permute-done((bf16[128,3072]{1,0:T(8,128)(2,1)S(1)}, bf16[128,3072]{1,0:T(8,128)(2,1)S(1)}, u32[]{:S(2)}, u32[]{:S(2)}) %collective-permute-start.13) | collective-permute-done | bytes 786464 | tf_op jit(solution)/shard_map/ppermute | solution.py:55
  128.6 5.8 %collective-permute-start.17 = (bf16[128,3072]{1,0:T(8,128)(2,1)S(1)}, bf16[128,3072]{1,0:T(8,128)(2,1)S(1)}, u32[]{:S(2)}, u32[]{:S(2)}) collective-permute-start(bf16[128,3072]{1,0:T(8,128)(2,1)S(1)} %collective-permute-done.13.refs_1_), channel_id=1, source_target_pairs={{0,32},{32,0},{1,33},{33,1},{2,34},{34,2},{3,35},{35,3},{4,36},{36... | collective-permute-start | bytes 2359304 | tf_op jit(solution)/shard_map/ppermute | solution.py:41
  134.4 1.5 %update.1 = (f32[384,256]{1,0:T(8,128)}, f32[384,256]{1,0:T(8,128)}, f32[384,256]{1,0:T(8,128)}) custom-call(bf16[256,384]{1,0:T(8,128)(2,1)S(1)} %bitcast.22, f32[32,128]{1,0:T(8,128)S(1)} %bitcast.27, f32[384,256]{1,0:T(8,128)S(1)} %copy-done, f32[384,256]{1,0:T(8,128)S(1)} %copy-done.1, f32[384,256]{1,0:T(8,128)S(1)} %copy-done.2), custom_call_target="tpu_custom_call" | custom-call | tf_op jit(solution)/shard_map/update/pallas_call | solution.py:275
  136.3 5.3 %forward.1 = bf16[448,256]{1,0:T(8,128)(2,1)} custom-call(s32[3]{0:T(128)S(1)} %pad_add_fusion.place_ref, bf16[448,12288]{1,0:T(8,128)(2,1)S(1)} %get-tuple-element.27.held, bf16[128,3072]{1,0:T(8,128)(2,1)S(1)} %constant_dynamic-update-slice_fusion.refs_0_, bf16[128,3072]{1,0:T(8,128)(2,1)S(1)} %collective-permute-done.13.refs_1_, ...), custom_call_target="tpu_custom_call" | custom-call | flops 2818572288 | bytes 17530880 | tf_op jit(solution)/shard_map/forward/pallas_call | solution.py:202
  (37 shorter events, 3.3 us)
Async XLA Ops:
  7.5 5.2 %collective-permute-start.1 = (bf16[128,3072]{1,0:T(8,128)(2,1)S(1)}, bf16[128,3072]{1,0:T(8,128)(2,1)S(1)}, u32[]{:S(2)}, u32[]{:S(2)}) collective-permute-start(bf16[128,3072]{1,0:T(8,128)(2,1)S(1)} %get-tuple-element.19), channel_id=1, source_target_pairs={{0,32},{32,0},{1,33},{33,1},{2,34},{34,2},{3,35},{35,3},{4,36},{36... | collective-permute-start | bytes 2359304 | tf_op jit(solution)/shard_map/ppermute | solution.py:41
  10.8 3.4 %collective-permute-start.3 = (bf16[128,3072]{1,0:T(8,128)(2,1)S(1)}, bf16[128,3072]{1,0:T(8,128)(2,1)S(1)}, u32[]{:S(2)}, u32[]{:S(2)}) collective-permute-start(bf16[128,3072]{1,0:T(8,128)(2,1)S(1)} %get-tuple-element.21), channel_id=1, source_target_pairs={{0,32},{32,0},{1,33},{33,1},{2,34},{34,2},{3,35},{35,3},{4,36},{36... | collective-permute-start | bytes 2359304 | tf_op jit(solution)/shard_map/ppermute | solution.py:41
  10.9 6.5 %collective-permute-start = (bf16[128,3072]{1,0:T(8,128)(2,1)S(1)}, bf16[128,3072]{1,0:T(8,128)(2,1)S(1)}, u32[]{:S(2)}, u32[]{:S(2)}) collective-permute-start(bf16[128,3072]{1,0:T(8,128)(2,1)S(1)} %get-tuple-element.17), channel_id=1, source_target_pairs={{0,32},{32,0},{1,33},{33,1},{2,34},{34,2},{3,35},{35,3},{4,36},{36... | collective-permute-start | bytes 2359304 | tf_op jit(solution)/shard_map/ppermute | solution.py:41
  11.3 4.8 %collective-permute-start.5 = (bf16[128,3072]{1,0:T(8,128)(2,1)S(1)}, bf16[128,3072]{1,0:T(8,128)(2,1)S(1)}, u32[]{:S(2)}, u32[]{:S(2)}) collective-permute-start(bf16[128,3072]{1,0:T(8,128)(2,1)S(1)} %get-tuple-element.23), channel_id=1, source_target_pairs={{0,32},{32,0},{1,33},{33,1},{2,34},{34,2},{3,35},{35,3},{4,36},{36... | collective-permute-start | bytes 2359304 | tf_op jit(solution)/shard_map/ppermute | solution.py:41
  12.9 12.8 %collective-permute-start.2 = (bf16[128,3072]{1,0:T(8,128)(2,1)S(1)}, bf16[128,3072]{1,0:T(8,128)(2,1)S(1)}, u32[]{:S(2)}, u32[]{:S(2)}) collective-permute-start(bf16[128,3072]{1,0:T(8,128)(2,1)S(1)} %add_convert_fusion.3), channel_id=1, source_target_pairs={{0,16},{8,24},{16,0},{24,8},{32,160},{40,168},{48,176},{56,184},{6... | collective-permute-start | bytes 2359304 | tf_op jit(solution)/shard_map/ppermute | solution.py:55
  14.4 19.7 %collective-permute-start.4 = (bf16[128,3072]{1,0:T(8,128)(2,1)S(1)}, bf16[128,3072]{1,0:T(8,128)(2,1)S(1)}, u32[]{:S(2)}, u32[]{:S(2)}) collective-permute-start(bf16[128,3072]{1,0:T(8,128)(2,1)S(1)} %add_convert_fusion.2), channel_id=1, source_target_pairs={{0,8},{8,16},{16,24},{24,0},{32,96},{40,104},{48,112},{56,120},{64... | collective-permute-start | bytes 2359304 | tf_op jit(solution)/shard_map/ppermute | solution.py:55
  16.3 17.8 %collective-permute-start.6 = (bf16[128,3072]{1,0:T(8,128)(2,1)S(1)}, bf16[128,3072]{1,0:T(8,128)(2,1)S(1)}, u32[]{:S(2)}, u32[]{:S(2)}) collective-permute-start(bf16[128,3072]{1,0:T(8,128)(2,1)S(1)} %add_convert_fusion.1), channel_id=1, source_target_pairs={{0,24},{8,0},{16,8},{24,16},{32,224},{40,232},{48,240},{56,248},{6... | collective-permute-start | bytes 2359304 | tf_op jit(solution)/shard_map/ppermute | solution.py:55
  34.8 50.3 %copy-start = (f32[384,256]{1,0:T(8,128)S(1)}, f32[384,256]{1,0:T(8,128)}, u32[]{:S(2)}) copy-start(f32[384,256]{1,0:T(8,128)} %refs_0_.3) | copy-start | bytes 1179652
  34.8 50.2 %copy-start.1 = (f32[384,256]{1,0:T(8,128)S(1)}, f32[384,256]{1,0:T(8,128)}, u32[]{:S(2)}) copy-start(f32[384,256]{1,0:T(8,128)} %refs_1_.3) | copy-start | bytes 1179652
  34.8 50.2 %copy-start.2 = (f32[384,256]{1,0:T(8,128)S(1)}, f32[384,256]{1,0:T(8,128)}, u32[]{:S(2)}) copy-start(f32[384,256]{1,0:T(8,128)} %refs_2_.3) | copy-start | bytes 1179652
  34.8 6.6 %collective-permute-start.7 = (bf16[32,3072]{1,0:T(8,128)(2,1)S(1)}, bf16[32,3072]{1,0:T(8,128)(2,1)S(1)}, u32[]{:S(2)}, u32[]{:S(2)}) collective-permute-start(bf16[32,3072]{1,0:T(8,128)(2,1)S(1)} %get-tuple-element.28), channel_id=1, source_target_pairs={{0,128},{8,136},{16,144},{24,152},{32,48},{40,56},{48,32},{56,40},... | collective-permute-start | bytes 589832 | tf_op jit(solution)/shard_map/ppermute | solution.py:55
  36.5 5.8 %collective-permute-start.9 = (bf16[32,3072]{1,0:T(8,128)(2,1)S(1)}, bf16[32,3072]{1,0:T(8,128)(2,1)S(1)}, u32[]{:S(2)}, u32[]{:S(2)}) collective-permute-start(bf16[32,3072]{1,0:T(8,128)(2,1)S(1)} %get-tuple-element.29), channel_id=1, source_target_pairs={{0,192},{8,200},{16,208},{24,216},{32,56},{40,32},{48,40},{56,48},... | collective-permute-start | bytes 589832 | tf_op jit(solution)/shard_map/ppermute | solution.py:55
  37.3 6.2 %collective-permute-start.8 = (bf16[32,3072]{1,0:T(8,128)(2,1)S(1)}, bf16[32,3072]{1,0:T(8,128)(2,1)S(1)}, u32[]{:S(2)}, u32[]{:S(2)}) collective-permute-start(bf16[32,3072]{1,0:T(8,128)(2,1)S(1)} %get-tuple-element.30), channel_id=1, source_target_pairs={{0,64},{8,72},{16,80},{24,88},{32,40},{40,48},{48,56},{56,32},{64,... | collective-permute-start | bytes 589832 | tf_op jit(solution)/shard_map/ppermute | solution.py:55
  97.2 9.4 %collective-permute-start.12 = (bf16[32,3072]{1,0:T(8,128)(2,1)S(1)}, bf16[32,3072]{1,0:T(8,128)(2,1)S(1)}, u32[]{:S(2)}, u32[]{:S(2)}) collective-permute-start(bf16[32,3072]{1,0:T(8,128)(2,1)S(1)} %bitcast.29), channel_id=1, source_target_pairs={{0,192},{8,200},{16,208},{24,216},{32,56},{40,32},{48,40},{56,48},... | collective-permute-start | bytes 589832 | tf_op jit(solution)/shard_map/ppermute | solution.py:55
  98.2 8.4 %collective-permute-start.11 = (bf16[32,3072]{1,0:T(8,128)(2,1)S(1)}, bf16[32,3072]{1,0:T(8,128)(2,1)S(1)}, u32[]{:S(2)}, u32[]{:S(2)}) collective-permute-start(bf16[32,3072]{1,0:T(8,128)(2,1)S(1)} %bitcast.30), channel_id=1, source_target_pairs={{0,128},{8,136},{16,144},{24,152},{32,48},{40,56},{48,32},{56,40},... | collective-permute-start | bytes 589832 | tf_op jit(solution)/shard_map/ppermute | solution.py:55
  99.4 7.2 %collective-permute-start.10 = (bf16[32,3072]{1,0:T(8,128)(2,1)S(1)}, bf16[32,3072]{1,0:T(8,128)(2,1)S(1)}, u32[]{:S(2)}, u32[]{:S(2)}) collective-permute-start(bf16[32,3072]{1,0:T(8,128)(2,1)S(1)} %bitcast.31), channel_id=1, source_target_pairs={{0,64},{8,72},{16,80},{24,88},{32,40},{40,48},{48,56},{56,32},{64,... | collective-permute-start | bytes 589832 | tf_op jit(solution)/shard_map/ppermute | solution.py:55
  106.7 11.2 %collective-permute-start.15 = (bf16[128,3072]{1,0:T(8,128)(2,1)S(1)}, bf16[128,3072]{1,0:T(8,128)(2,1)S(1)}, u32[]{:S(2)}, u32[]{:S(2)}) collective-permute-start(bf16[128,3072]{1,0:T(8,128)(2,1)S(1)} %constant_dynamic-update-slice_fusion.refs_0_), channel_id=1, source_target_pairs={{0,24},{8,0},{16,8},{24,16},{32,224},{40,232},{48,240},{56,248},{6... | collective-permute-start | bytes 2359304 | tf_op jit(solution)/shard_map/ppermute | solution.py:55
  107.6 15.8 %collective-permute-start.14 = (bf16[128,3072]{1,0:T(8,128)(2,1)S(1)}, bf16[128,3072]{1,0:T(8,128)(2,1)S(1)}, u32[]{:S(2)}, u32[]{:S(2)}) collective-permute-start(bf16[128,3072]{1,0:T(8,128)(2,1)S(1)} %constant_dynamic-update-slice_fusion.refs_0_), channel_id=1, source_target_pairs={{0,16},{8,24},{16,0},{24,8},{32,160},{40,168},{48,176},{56,184},{6... | collective-permute-start | bytes 2359304 | tf_op jit(solution)/shard_map/ppermute | solution.py:55
  109.0 19.7 %collective-permute-start.13 = (bf16[128,3072]{1,0:T(8,128)(2,1)S(1)}, bf16[128,3072]{1,0:T(8,128)(2,1)S(1)}, u32[]{:S(2)}, u32[]{:S(2)}) collective-permute-start(bf16[128,3072]{1,0:T(8,128)(2,1)S(1)} %constant_dynamic-update-slice_fusion.refs_0_), channel_id=1, source_target_pairs={{0,8},{8,16},{16,24},{24,0},{32,96},{40,104},{48,112},{56,120},{64... | collective-permute-start | bytes 2359304 | tf_op jit(solution)/shard_map/ppermute | solution.py:55
  109.0 26.9 %collective-permute-start.16 = (bf16[128,3072]{1,0:T(8,128)(2,1)S(1)}, bf16[128,3072]{1,0:T(8,128)(2,1)S(1)}, u32[]{:S(2)}, u32[]{:S(2)}) collective-permute-start(bf16[128,3072]{1,0:T(8,128)(2,1)S(1)} %constant_dynamic-update-slice_fusion.refs_0_), channel_id=1, source_target_pairs={{0,32},{32,0},{1,33},{33,1},{2,34},{34,2},{3,35},{35,3},{4,36},{36... | collective-permute-start | bytes 2359304 | tf_op jit(solution)/shard_map/ppermute | solution.py:41
  117.9 18.0 %collective-permute-start.19 = (bf16[128,3072]{1,0:T(8,128)(2,1)S(1)}, bf16[128,3072]{1,0:T(8,128)(2,1)S(1)}, u32[]{:S(2)}, u32[]{:S(2)}) collective-permute-start(bf16[128,3072]{1,0:T(8,128)(2,1)S(1)} %collective-permute-done.15.refs_3_), channel_id=1, source_target_pairs={{0,32},{32,0},{1,33},{33,1},{2,34},{34,2},{3,35},{35,3},{4,36},{36... | collective-permute-start | bytes 2359304 | tf_op jit(solution)/shard_map/ppermute | solution.py:41
  123.3 12.6 %collective-permute-start.18 = (bf16[128,3072]{1,0:T(8,128)(2,1)S(1)}, bf16[128,3072]{1,0:T(8,128)(2,1)S(1)}, u32[]{:S(2)}, u32[]{:S(2)}) collective-permute-start(bf16[128,3072]{1,0:T(8,128)(2,1)S(1)} %collective-permute-done.14.refs_2_), channel_id=1, source_target_pairs={{0,32},{32,0},{1,33},{33,1},{2,34},{34,2},{3,35},{35,3},{4,36},{36... | collective-permute-start | bytes 2359304 | tf_op jit(solution)/shard_map/ppermute | solution.py:41
  128.6 7.7 %collective-permute-start.17 = (bf16[128,3072]{1,0:T(8,128)(2,1)S(1)}, bf16[128,3072]{1,0:T(8,128)(2,1)S(1)}, u32[]{:S(2)}, u32[]{:S(2)}) collective-permute-start(bf16[128,3072]{1,0:T(8,128)(2,1)S(1)} %collective-permute-done.13.refs_1_), channel_id=1, source_target_pairs={{0,32},{32,0},{1,33},{33,1},{2,34},{34,2},{3,35},{35,3},{4,36},{36... | collective-permute-start | bytes 2359304 | tf_op jit(solution)/shard_map/ppermute | solution.py:41

commit v8 on v6

--- a/solution.py
+++ b/solution.py
@@ -305,8 +305,10 @@
 
     weight = weight_piece(place, grads, squares, states, count)
     plane = lax.all_to_all(weight, "z", 0, 1, tiled=True)
-    line = jnp.concatenate([plane] + [routed(plane, d, False) for d in (1, 2, 3)], 0)
-    own = [line] + [routed(line, d, True) for d in (1, 2, 3)]
+    rest = jnp.concatenate([routed(plane, d, False) for d in (1, 2, 3)], 0)
+    early = [plane] + [routed(plane, d, True) for d in (1, 2, 3)]
+    late = [rest] + [routed(rest, d, True) for d in (1, 2, 3)]
+    own = [jnp.concatenate(parts, 0) for parts in zip(early, late)]
     other = [send(part, "core", 1) for part in own]
 
     master_new, first_new, second_new = update(grads, squares, states, count)

time: 142 us -> 149 us (1.049)
  waiting for transfers between devices: 38.8 us -> 52.2 us
  starting transfers between devices: 33.2 us -> 27.3 us
    ppermute x12 -> x15, waiting for transfers between devices: 35.8 us -> 47.8 us  [routed(): return lax.ppermute(value, ('y', 'core', 'x'), pairs)]
    ppermute x8, starting transfers between devices: 23 us -> 12.8 us  [send(): return lax.ppermute(value, axis, [(i, (i + step) % n) for i in range(n)])]
    ppermute x12 -> x15, starting transfers between devices: 10.3 us -> 14.4 us  [routed(): return lax.ppermute(value, ('y', 'core', 'x'), pairs)]
    ppermute x8, waiting for transfers between devices: 2.95 us -> 4.44 us  [send(): return lax.ppermute(value, axis, [(i, (i + step) % n) for i in range(n)])]
  transfers between devices with their start and end apart: 20 -> 23, of which waited for: 11 -> 12; matrix products, arithmetic and copies ran while one was open for 0% -> 1% of each run, Pallas kernels for 1% -> 1%
where the time goes in v8:
time: 149 us
  blocking collectives  52.3 us (35%)
  waiting for transfers between devices  52.2 us (35%)
  starting transfers between devices  27.3 us (18%)
  Pallas kernels  14.6 us (10%)
    ppermute x15, waiting for transfers between devices, routed(): return lax.ppermute(value, ('y', 'core', 'x'), pairs)  47.8 us
    all_to_all x1, blocking collectives, body(): planes = lax.all_to_all(plane, 'z', 1, 0, tiled=True)  16.6 us
    ppermute x15, starting transfers between devices, routed(): return lax.ppermute(value, ('y', 'core', 'x'), pairs)  14.4 us
    ppermute x8, starting transfers between devices, send(): return lax.ppermute(value, axis, [(i, (i + step) % n) for i in range(n)])  12.8 us
    all_to_all x1, blocking collectives, body(): squares = lax.all_to_all(square_sum(grads), ('x', 'z'), 0, 0, tiled=True)  12.5 us
    all_to_all x1, blocking collectives, body(): grads = lax.all_to_all(plane_sum(planes), ('core', 'y'), 0, 0, tiled=True)  12.1 us
    all_to_all x1, blocking collectives, body(): plane = lax.all_to_all(weight, 'z', 0, 1, tiled=True)  11.1 us
    pallas_call x1, Pallas kernels, partial_terms(): kernel_call(partial_kernel, 'partial_terms', [pl.BlockSpec(memory_space=p...  6.55 us
  transfers between devices with their start and end apart: 23, of which 12 were waited for; matrix products, arithmetic and copies ran while one was open for 1% of the time, Pallas kernels for 1%

profile of v8, /device:TPU:1, one launch (start us, length us, event | category | flops | bytes accessed | tf_op | source)
XLA Modules:
  0.0 148.9 jit_solution(11300865206954256189)
XLA Ops:
  0.7 6.6 %partial_terms.1 = (bf16[128,3072]{1,0:T(8,128)(2,1)S(1)}, bf16[128,3072]{1,0:T(8,128)(2,1)S(1)}, bf16[128,3072]{1,0:T(8,128)(2,1)S(1)}, bf16[128,3072]{1,0:T(8,...) custom-call(s32[3]{0:T(128)S(1)} %pad_add_fusion.place_ref, ...), custom_call_target="tpu_custom_call" | custom-call | flops 2818572288 | bytes 17530880 | tf_op jit(solution)/shard_map/partial_terms/pallas_call | solution.py:135
  7.3 3.3 %collective-permute-start.1 = (bf16[128,3072]{1,0:T(8,128)(2,1)S(1)}, bf16[128,3072]{1,0:T(8,128)(2,1)S(1)}, u32[]{:S(2)}, u32[]{:S(2)}) collective-permute-start(bf16[128,3072]{1,0:T(8,128)(2,1)S(1)} %get-tuple-element.19), channel_id=1, source_target_pairs={{0,32},{32,0},{1,33},{33,1},{2,34},{34,2},{3,35},{35,3},{4,36},{36... | collective-permute-start | bytes 2359304 | tf_op jit(solution)/shard_map/ppermute | solution.py:41
  11.2 1.3 collective-permute-done.1
  12.7 1.3 collective-permute-start.2
  14.6 1.2 collective-permute-done.5
  16.1 1.1 collective-permute-start.6
  17.2 8.3 %collective-permute-done.2 = bf16[128,3072]{1,0:T(8,128)(2,1)S(1)} collective-permute-done((bf16[128,3072]{1,0:T(8,128)(2,1)S(1)}, bf16[128,3072]{1,0:T(8,128)(2,1)S(1)}, u32[]{:S(2)}, u32[]{:S(2)}) %collective-permute-start.2) | collective-permute-done | bytes 786464 | tf_op jit(solution)/shard_map/ppermute | solution.py:55
  25.5 8.4 %collective-permute-done.4 = bf16[128,3072]{1,0:T(8,128)(2,1)S(1)} collective-permute-done((bf16[128,3072]{1,0:T(8,128)(2,1)S(1)}, bf16[128,3072]{1,0:T(8,128)(2,1)S(1)}, u32[]{:S(2)}, u32[]{:S(2)}) %collective-permute-start.4) | collective-permute-done | bytes 786464 | tf_op jit(solution)/shard_map/ppermute | solution.py:55
  34.6 1.5 collective-permute-start.7
  36.1 0.9 collective-permute-start.9
  37.5 3.5 %collective-permute-done.7 = bf16[32,3072]{1,0:T(8,128)(2,1)S(1)} collective-permute-done((bf16[32,3072]{1,0:T(8,128)(2,1)S(1)}, bf16[32,3072]{1,0:T(8,128)(2,1)S(1)}, u32[]{:S(2)}, u32[]{:S(2)}) %collective-permute-start.7) | collective-permute-done | bytes 196640 | tf_op jit(solution)/shard_map/ppermute | solution.py:55
  41.0 0.8 collective-permute-done.9
  41.8 1.3 collective-permute-done.8
  43.2 16.6 %all_to_all.60 = bf16[32,8,384]{2,0,1:T(8,128)(2,1)S(1)} all-to-all(bf16[32,8,384]{2,0,1:T(8,128)(2,1)S(1)} %bitcast.36), channel_id=1, replica_groups=mesh['y'=4,'core'=2,'x'=4,'z'=8] {'z'}, dimensions={1} | all-to-all | bytes 393216 | tf_op jit(solution)/shard_map/all_to_all | solution.py:302
  59.8 12.1 %all_to_all.61 = bf16[8,32,384]{2,1,0:T(8,128)(2,1)S(1)} all-to-all(bf16[8,32,384]{2,1,0:T(8,128)(2,1)S(1)} %bitcast.24), channel_id=1, replica_groups=mesh['y'=4,'core'=2,'x'=4,'z'=8] {'core','y'}, dimensions={0} | all-to-all | bytes 393216 | tf_op jit(solution)/shard_map/all_to_all | solution.py:303
  72.2 12.5 %all_to_all.62 = f32[32,1,128]{2,1,0:T(1,128)S(1)} all-to-all(f32[32,1,128]{2,1,0:T(1,128)S(1)} %bitcast.28), channel_id=1, replica_groups=mesh['y'=4,'core'=2,'x'=4,'z'=8] {'x','z'}, dimensions={0} | all-to-all | bytes 32768 | tf_op jit(solution)/shard_map/all_to_all | solution.py:304
  84.6 1.0 weight_piece.1
  85.7 11.1 %all_to_all.63 = bf16[8,32,384]{2,1,0:T(8,128)(2,1)S(1)} all-to-all(bf16[8,32,384]{2,1,0:T(8,128)(2,1)S(1)} %bitcast.25), channel_id=1, replica_groups=mesh['y'=4,'core'=2,'x'=4,'z'=8] {'z'}, dimensions={0} | all-to-all | bytes 393216 | tf_op jit(solution)/shard_map/all_to_all | solution.py:307
  96.8 0.9 collective-permute-start.17
  97.7 1.6 %collective-permute-start.15 = (bf16[32,3072]{1,0:T(8,128)(2,1)S(1)}, bf16[32,3072]{1,0:T(8,128)(2,1)S(1)}, u32[]{:S(2)}, u32[]{:S(2)}) collective-permute-start(bf16[32,3072]{1,0:T(8,128)(2,1)S(1)} %bitcast.30), channel_id=1, source_target_pairs={{0,16},{8,24},{16,0},{24,8},{32,160},{40,168},{48,176},{56,184},{6... | collective-permute-start | bytes 589832 | tf_op jit(solution)/shard_map/ppermute | solution.py:55
  99.3 0.9 collective-permute-start.12
  100.8 7.9 %collective-permute-done.10 = bf16[32,3072]{1,0:T(8,128)(2,1)S(1)} collective-permute-done((bf16[32,3072]{1,0:T(8,128)(2,1)S(1)}, bf16[32,3072]{1,0:T(8,128)(2,1)S(1)}, u32[]{:S(2)}, u32[]{:S(2)}) %collective-permute-start.10) | collective-permute-done | bytes 196640 | tf_op jit(solution)/shard_map/ppermute | solution.py:55
  108.7 6.0 %collective-permute-done.11 = bf16[32,3072]{1,0:T(8,128)(2,1)S(1)} collective-permute-done((bf16[32,3072]{1,0:T(8,128)(2,1)S(1)}, bf16[32,3072]{1,0:T(8,128)(2,1)S(1)}, u32[]{:S(2)}, u32[]{:S(2)}) %collective-permute-start.11) | collective-permute-done | bytes 196640 | tf_op jit(solution)/shard_map/ppermute | solution.py:55
  114.8 3.4 %collective-permute-start.18 = (bf16[96,3072]{1,0:T(8,128)(2,1)S(1)}, bf16[96,3072]{1,0:T(8,128)(2,1)S(1)}, u32[]{:S(2)}, u32[]{:S(2)}) collective-permute-start(bf16[96,3072]{1,0:T(8,128)(2,1)S(1)} %get-tuple-element.31), channel_id=1, source_target_pairs={{0,24},{8,0},{16,8},{24,16},{32,224},{40,232},{48,240},{56,248},{6... | collective-permute-start | bytes 1769480 | tf_op jit(solution)/shard_map/ppermute | solution.py:55
  118.8 0.8 collective-permute-start.14
  119.6 3.9 %collective-permute-start.19 = (bf16[128,3072]{1,0:T(8,128)(2,1)S(1)}, bf16[128,3072]{1,0:T(8,128)(2,1)S(1)}, u32[]{:S(2)}, u32[]{:S(2)}) collective-permute-start(bf16[128,3072]{1,0:T(8,128)(2,1)S(1)} %get-tuple-element.32.refs_0_), channel_id=1, source_target_pairs={{0,32},{32,0},{1,33},{33,1},{2,34},{34,2},{3,35},{35,3},{4,36},{36... | collective-permute-start | bytes 2359304 | tf_op jit(solution)/shard_map/ppermute | solution.py:41
  123.5 11.6 %collective-permute-done.14 = bf16[96,3072]{1,0:T(8,128)(2,1)S(1)} collective-permute-done((bf16[96,3072]{1,0:T(8,128)(2,1)S(1)}, bf16[96,3072]{1,0:T(8,128)(2,1)S(1)}, u32[]{:S(2)}, u32[]{:S(2)}) %collective-permute-start.14) | collective-permute-done | bytes 589856 | tf_op jit(solution)/shard_map/ppermute | solution.py:55
  135.1 4.4 %collective-permute-start.20 = (bf16[128,3072]{1,0:T(8,128)(2,1)S(1)}, bf16[128,3072]{1,0:T(8,128)(2,1)S(1)}, u32[]{:S(2)}, u32[]{:S(2)}) collective-permute-start(bf16[128,3072]{1,0:T(8,128)(2,1)S(1)} %constant_dynamic-update-slice_fusion.7.refs_1_), channel_id=1, source_target_pairs={{0,32},{32,0},{1,33},{33,1},{2,34},{34,2},{3,35},{35,3},{4,36},{36... | collective-permute-start | bytes 2359304 | tf_op jit(solution)/shard_map/ppermute | solution.py:41
  140.3 1.5 update.1
  141.8 0.8 collective-permute-done.21.refs_6_
  142.5 1.1 collective-permute-done.22.refs_7_
  143.7 5.3 %forward.1 = bf16[448,256]{1,0:T(8,128)(2,1)} custom-call(s32[3]{0:T(128)S(1)} %pad_add_fusion.place_ref, bf16[448,12288]{1,0:T(8,128)(2,1)S(1)} %get-tuple-element.27.held, bf16[128,3072]{1,0:T(8,128)(2,1)S(1)} %get-tuple-element.32.refs_0_, bf16[128,3072]{1,0:T(8,128)(2,1)S(1)} %constant_dynamic-update-slice_fusion.7.refs_1_, ...), custom_call_target="tpu_custom_call" | custom-call | flops 2818572288 | bytes 17530880 | tf_op jit(solution)/shard_map/forward/pallas_call | solution.py:198
  (49 shorter events, 5.5 us)
Async XLA Ops:
  7.3 5.2 %collective-permute-start.1 = (bf16[128,3072]{1,0:T(8,128)(2,1)S(1)}, bf16[128,3072]{1,0:T(8,128)(2,1)S(1)}, u32[]{:S(2)}, u32[]{:S(2)}) collective-permute-start(bf16[128,3072]{1,0:T(8,128)(2,1)S(1)} %get-tuple-element.19), channel_id=1, source_target_pairs={{0,32},{32,0},{1,33},{33,1},{2,34},{34,2},{3,35},{35,3},{4,36},{36... | collective-permute-start | bytes 2359304 | tf_op jit(solution)/shard_map/ppermute | solution.py:41
  10.6 3.4 %collective-permute-start.3 = (bf16[128,3072]{1,0:T(8,128)(2,1)S(1)}, bf16[128,3072]{1,0:T(8,128)(2,1)S(1)}, u32[]{:S(2)}, u32[]{:S(2)}) collective-permute-start(bf16[128,3072]{1,0:T(8,128)(2,1)S(1)} %get-tuple-element.21), channel_id=1, source_target_pairs={{0,32},{32,0},{1,33},{33,1},{2,34},{34,2},{3,35},{35,3},{4,36},{36... | collective-permute-start | bytes 2359304 | tf_op jit(solution)/shard_map/ppermute | solution.py:41
  10.7 6.5 %collective-permute-start = (bf16[128,3072]{1,0:T(8,128)(2,1)S(1)}, bf16[128,3072]{1,0:T(8,128)(2,1)S(1)}, u32[]{:S(2)}, u32[]{:S(2)}) collective-permute-start(bf16[128,3072]{1,0:T(8,128)(2,1)S(1)} %get-tuple-element.17), channel_id=1, source_target_pairs={{0,32},{32,0},{1,33},{33,1},{2,34},{34,2},{3,35},{35,3},{4,36},{36... | collective-permute-start | bytes 2359304 | tf_op jit(solution)/shard_map/ppermute | solution.py:41
  11.1 4.8 %collective-permute-start.5 = (bf16[128,3072]{1,0:T(8,128)(2,1)S(1)}, bf16[128,3072]{1,0:T(8,128)(2,1)S(1)}, u32[]{:S(2)}, u32[]{:S(2)}) collective-permute-start(bf16[128,3072]{1,0:T(8,128)(2,1)S(1)} %get-tuple-element.23), channel_id=1, source_target_pairs={{0,32},{32,0},{1,33},{33,1},{2,34},{34,2},{3,35},{35,3},{4,36},{36... | collective-permute-start | bytes 2359304 | tf_op jit(solution)/shard_map/ppermute | solution.py:41
  12.7 12.8 %collective-permute-start.2 = (bf16[128,3072]{1,0:T(8,128)(2,1)S(1)}, bf16[128,3072]{1,0:T(8,128)(2,1)S(1)}, u32[]{:S(2)}, u32[]{:S(2)}) collective-permute-start(bf16[128,3072]{1,0:T(8,128)(2,1)S(1)} %add_convert_fusion.3), channel_id=1, source_target_pairs={{0,16},{8,24},{16,0},{24,8},{32,160},{40,168},{48,176},{56,184},{6... | collective-permute-start | bytes 2359304 | tf_op jit(solution)/shard_map/ppermute | solution.py:55
  14.2 19.7 %collective-permute-start.4 = (bf16[128,3072]{1,0:T(8,128)(2,1)S(1)}, bf16[128,3072]{1,0:T(8,128)(2,1)S(1)}, u32[]{:S(2)}, u32[]{:S(2)}) collective-permute-start(bf16[128,3072]{1,0:T(8,128)(2,1)S(1)} %add_convert_fusion.2), channel_id=1, source_target_pairs={{0,8},{8,16},{16,24},{24,0},{32,96},{40,104},{48,112},{56,120},{64... | collective-permute-start | bytes 2359304 | tf_op jit(solution)/shard_map/ppermute | solution.py:55
  16.1 17.8 %collective-permute-start.6 = (bf16[128,3072]{1,0:T(8,128)(2,1)S(1)}, bf16[128,3072]{1,0:T(8,128)(2,1)S(1)}, u32[]{:S(2)}, u32[]{:S(2)}) collective-permute-start(bf16[128,3072]{1,0:T(8,128)(2,1)S(1)} %add_convert_fusion.1), channel_id=1, source_target_pairs={{0,24},{8,0},{16,8},{24,16},{32,224},{40,232},{48,240},{56,248},{6... | collective-permute-start | bytes 2359304 | tf_op jit(solution)/shard_map/ppermute | solution.py:55
  34.6 50.1 %copy-start = (f32[384,256]{1,0:T(8,128)S(1)}, f32[384,256]{1,0:T(8,128)}, u32[]{:S(2)}) copy-start(f32[384,256]{1,0:T(8,128)} %refs_0_.3) | copy-start | bytes 1179652
  34.6 50.1 %copy-start.1 = (f32[384,256]{1,0:T(8,128)S(1)}, f32[384,256]{1,0:T(8,128)}, u32[]{:S(2)}) copy-start(f32[384,256]{1,0:T(8,128)} %refs_1_.3) | copy-start | bytes 1179652
  34.6 50.1 %copy-start.2 = (f32[384,256]{1,0:T(8,128)S(1)}, f32[384,256]{1,0:T(8,128)}, u32[]{:S(2)}) copy-start(f32[384,256]{1,0:T(8,128)} %refs_2_.3) | copy-start | bytes 1179652
  34.6 6.4 %collective-permute-start.7 = (bf16[32,3072]{1,0:T(8,128)(2,1)S(1)}, bf16[32,3072]{1,0:T(8,128)(2,1)S(1)}, u32[]{:S(2)}, u32[]{:S(2)}) collective-permute-start(bf16[32,3072]{1,0:T(8,128)(2,1)S(1)} %get-tuple-element.28), channel_id=1, source_target_pairs={{0,128},{8,136},{16,144},{24,152},{32,48},{40,56},{48,32},{56,40},... | collective-permute-start | bytes 589832 | tf_op jit(solution)/shard_map/ppermute | solution.py:55
  36.1 5.8 %collective-permute-start.9 = (bf16[32,3072]{1,0:T(8,128)(2,1)S(1)}, bf16[32,3072]{1,0:T(8,128)(2,1)S(1)}, u32[]{:S(2)}, u32[]{:S(2)}) collective-permute-start(bf16[32,3072]{1,0:T(8,128)(2,1)S(1)} %get-tuple-element.29), channel_id=1, source_target_pairs={{0,192},{8,200},{16,208},{24,216},{32,56},{40,32},{48,40},{56,48},... | collective-permute-start | bytes 589832 | tf_op jit(solution)/shard_map/ppermute | solution.py:55
  36.9 6.2 %collective-permute-start.8 = (bf16[32,3072]{1,0:T(8,128)(2,1)S(1)}, bf16[32,3072]{1,0:T(8,128)(2,1)S(1)}, u32[]{:S(2)}, u32[]{:S(2)}) collective-permute-start(bf16[32,3072]{1,0:T(8,128)(2,1)S(1)} %get-tuple-element.30), channel_id=1, source_target_pairs={{0,64},{8,72},{16,80},{24,88},{32,40},{40,48},{48,56},{56,32},{64,... | collective-permute-start | bytes 589832 | tf_op jit(solution)/shard_map/ppermute | solution.py:55
  96.8 26.6 %collective-permute-start.17 = (bf16[32,3072]{1,0:T(8,128)(2,1)S(1)}, bf16[32,3072]{1,0:T(8,128)(2,1)S(1)}, u32[]{:S(2)}, u32[]{:S(2)}) collective-permute-start(bf16[32,3072]{1,0:T(8,128)(2,1)S(1)} %bitcast.29), channel_id=1, source_target_pairs={{0,24},{8,0},{16,8},{24,16},{32,224},{40,232},{48,240},{56,248},{6... | collective-permute-start | bytes 589832 | tf_op jit(solution)/shard_map/ppermute | solution.py:55
  97.7 21.8 %collective-permute-start.15 = (bf16[32,3072]{1,0:T(8,128)(2,1)S(1)}, bf16[32,3072]{1,0:T(8,128)(2,1)S(1)}, u32[]{:S(2)}, u32[]{:S(2)}) collective-permute-start(bf16[32,3072]{1,0:T(8,128)(2,1)S(1)} %bitcast.30), channel_id=1, source_target_pairs={{0,16},{8,24},{16,0},{24,8},{32,160},{40,168},{48,176},{56,184},{6... | collective-permute-start | bytes 589832 | tf_op jit(solution)/shard_map/ppermute | solution.py:55
  99.3 19.5 %collective-permute-start.13 = (bf16[32,3072]{1,0:T(8,128)(2,1)S(1)}, bf16[32,3072]{1,0:T(8,128)(2,1)S(1)}, u32[]{:S(2)}, u32[]{:S(2)}) collective-permute-start(bf16[32,3072]{1,0:T(8,128)(2,1)S(1)} %bitcast.31), channel_id=1, source_target_pairs={{0,8},{8,16},{16,24},{24,0},{32,96},{40,104},{48,112},{56,120},{64... | collective-permute-start | bytes 589832 | tf_op jit(solution)/shard_map/ppermute | solution.py:55
  99.3 15.5 %collective-permute-start.12 = (bf16[32,3072]{1,0:T(8,128)(2,1)S(1)}, bf16[32,3072]{1,0:T(8,128)(2,1)S(1)}, u32[]{:S(2)}, u32[]{:S(2)}) collective-permute-start(bf16[32,3072]{1,0:T(8,128)(2,1)S(1)} %bitcast.32), channel_id=1, source_target_pairs={{0,192},{8,200},{16,208},{24,216},{32,56},{40,32},{48,40},{56,48},... | collective-permute-start | bytes 589832 | tf_op jit(solution)/shard_map/ppermute | solution.py:55
  100.2 8.5 %collective-permute-start.10 = (bf16[32,3072]{1,0:T(8,128)(2,1)S(1)}, bf16[32,3072]{1,0:T(8,128)(2,1)S(1)}, u32[]{:S(2)}, u32[]{:S(2)}) collective-permute-start(bf16[32,3072]{1,0:T(8,128)(2,1)S(1)} %bitcast.33), channel_id=1, source_target_pairs={{0,64},{8,72},{16,80},{24,88},{32,40},{40,48},{48,56},{56,32},{64,... | collective-permute-start | bytes 589832 | tf_op jit(solution)/shard_map/ppermute | solution.py:55
  108.7 6.0 %collective-permute-start.11 = (bf16[32,3072]{1,0:T(8,128)(2,1)S(1)}, bf16[32,3072]{1,0:T(8,128)(2,1)S(1)}, u32[]{:S(2)}, u32[]{:S(2)}) collective-permute-start(bf16[32,3072]{1,0:T(8,128)(2,1)S(1)} %bitcast.35), channel_id=1, source_target_pairs={{0,128},{8,136},{16,144},{24,152},{32,48},{40,56},{48,32},{56,40},... | collective-permute-start | bytes 589832 | tf_op jit(solution)/shard_map/ppermute | solution.py:55
  114.8 24.8 %collective-permute-start.18 = (bf16[96,3072]{1,0:T(8,128)(2,1)S(1)}, bf16[96,3072]{1,0:T(8,128)(2,1)S(1)}, u32[]{:S(2)}, u32[]{:S(2)}) collective-permute-start(bf16[96,3072]{1,0:T(8,128)(2,1)S(1)} %get-tuple-element.31), channel_id=1, source_target_pairs={{0,24},{8,0},{16,8},{24,16},{32,224},{40,232},{48,240},{56,248},{6... | collective-permute-start | bytes 1769480 | tf_op jit(solution)/shard_map/ppermute | solution.py:55
  118.2 21.3 %collective-permute-start.16 = (bf16[96,3072]{1,0:T(8,128)(2,1)S(1)}, bf16[96,3072]{1,0:T(8,128)(2,1)S(1)}, u32[]{:S(2)}, u32[]{:S(2)}) collective-permute-start(bf16[96,3072]{1,0:T(8,128)(2,1)S(1)} %get-tuple-element.31), channel_id=1, source_target_pairs={{0,16},{8,24},{16,0},{24,8},{32,160},{40,168},{48,176},{56,184},{6... | collective-permute-start | bytes 1769480 | tf_op jit(solution)/shard_map/ppermute | solution.py:55
  118.8 16.3 %collective-permute-start.14 = (bf16[96,3072]{1,0:T(8,128)(2,1)S(1)}, bf16[96,3072]{1,0:T(8,128)(2,1)S(1)}, u32[]{:S(2)}, u32[]{:S(2)}) collective-permute-start(bf16[96,3072]{1,0:T(8,128)(2,1)S(1)} %get-tuple-element.31), channel_id=1, source_target_pairs={{0,8},{8,16},{16,24},{24,0},{32,96},{40,104},{48,112},{56,120},{64... | collective-permute-start | bytes 1769480 | tf_op jit(solution)/shard_map/ppermute | solution.py:55
  119.6 22.2 %collective-permute-start.19 = (bf16[128,3072]{1,0:T(8,128)(2,1)S(1)}, bf16[128,3072]{1,0:T(8,128)(2,1)S(1)}, u32[]{:S(2)}, u32[]{:S(2)}) collective-permute-start(bf16[128,3072]{1,0:T(8,128)(2,1)S(1)} %get-tuple-element.32.refs_0_), channel_id=1, source_target_pairs={{0,32},{32,0},{1,33},{33,1},{2,34},{34,2},{3,35},{35,3},{4,36},{36... | collective-permute-start | bytes 2359304 | tf_op jit(solution)/shard_map/ppermute | solution.py:41
  135.1 6.6 %collective-permute-start.20 = (bf16[128,3072]{1,0:T(8,128)(2,1)S(1)}, bf16[128,3072]{1,0:T(8,128)(2,1)S(1)}, u32[]{:S(2)}, u32[]{:S(2)}) collective-permute-start(bf16[128,3072]{1,0:T(8,128)(2,1)S(1)} %constant_dynamic-update-slice_fusion.7.refs_1_), channel_id=1, source_target_pairs={{0,32},{32,0},{1,33},{33,1},{2,34},{34,2},{3,35},{35,3},{4,36},{36... | collective-permute-start | bytes 2359304 | tf_op jit(solution)/shard_map/ppermute | solution.py:41
  139.5 3.0 %collective-permute-start.21 = (bf16[128,3072]{1,0:T(8,128)(2,1)S(1)}, bf16[128,3072]{1,0:T(8,128)(2,1)S(1)}, u32[]{:S(2)}, u32[]{:S(2)}) collective-permute-start(bf16[128,3072]{1,0:T(8,128)(2,1)S(1)} %constant_dynamic-update-slice_fusion.9.refs_2_), channel_id=1, source_target_pairs={{0,32},{32,0},{1,33},{33,1},{2,34},{34,2},{3,35},{35,3},{4,36},{36... | collective-permute-start | bytes 2359304 | tf_op jit(solution)/shard_map/ppermute | solution.py:41
  139.7 4.0 %collective-permute-start.22 = (bf16[128,3072]{1,0:T(8,128)(2,1)S(1)}, bf16[128,3072]{1,0:T(8,128)(2,1)S(1)}, u32[]{:S(2)}, u32[]{:S(2)}) collective-permute-start(bf16[128,3072]{1,0:T(8,128)(2,1)S(1)} %constant_dynamic-update-slice_fusion.11.refs_3_), channel_id=1, source_target_pairs={{0,32},{32,0},{1,33},{33,1},{2,34},{34,2},{3,35},{35,3},{4,36},{36... | collective-permute-start | bytes 2359304 | tf_op jit(solution)/shard_map/ppermute | solution.py:41
